TPU v7x, 32 devices: a whole 2x2x4 slice. The times are simulated.
32 devices in a mesh: dp: 8 (over y, x, core), tensor: 4 (over z).
Axes of the slice: x: 2, y: 2, z: 4, core: 2. Of those that a mesh axis runs over, the one named last changes fastest.
Arguments:
- tokens: bfloat16 [32, 576, 768], P('dp'), may hold values from -6 to 6
- cotangent: bfloat16 [32, 576, 768], P('dp'), may hold values from -6 to 6
- counts: int32 [32], P('dp'), may hold values from 196 to 576, as said below
- qkv_master: float32 [768, 3, 768], P('dp', None, 'tensor'), may hold values from -0.21875 to 0.21875
- qkv_first: float32 [768, 3, 768], P('dp', None, 'tensor'), may hold values from -384 to 384
- qkv_second: float32 [768, 3, 768], P('dp', None, 'tensor'), may hold values from 4608 to 18432
- out_master: float32 [768, 768], P('tensor', 'dp'), may hold values from -1.25 to 1.25
- out_first: float32 [768, 768], P('tensor', 'dp'), may hold values from -112 to 112
- out_second: float32 [768, 768], P('tensor', 'dp'), may hold values from 368 to 1474
- up_master: float32 [768, 4, 768], P('dp', None, 'tensor'), may hold values from -0.21875 to 0.21875
- up_first: float32 [768, 4, 768], P('dp', None, 'tensor'), may hold values from -192 to 192
- up_second: float32 [768, 4, 768], P('dp', None, 'tensor'), may hold values from 1152 to 4608
- down_master: float32 [4, 768, 768], P(None, 'tensor', 'dp'), may hold values from -0.109375 to 0.109375
- down_first: float32 [4, 768, 768], P(None, 'tensor', 'dp'), may hold values from -384 to 384
- down_second: float32 [4, 768, 768], P(None, 'tensor', 'dp'), may hold values from 4608 to 18432
- shared_master: float32 [6, 768], P(None, 'dp'), may hold values from -1.5 to 1.5
- shared_first: float32 [6, 768], P(None, 'dp'), may hold values from -512 to 512
- shared_second: float32 [6, 768], P(None, 'dp'), may hold values from 9216 to 36864
- split_master: float32 [6, 768], P(None, ('tensor', 'dp')), may hold values from -1.5 to 1.5
- split_first: float32 [6, 768], P(None, ('tensor', 'dp')), may hold values from -384 to 384
- split_second: float32 [6, 768], P(None, ('tensor', 'dp')), may hold values from 3686 to 14745
Outputs:
- mixed: bfloat16 [32, 576, 768], P('dp')
- input_grad: float32 [32, 576, 768], P('dp')
- qkv_master_new: float32 [768, 3, 768], P('dp', None, 'tensor')
- qkv_copy_new: bfloat16 [768, 3, 768], P('dp', None, 'tensor')
- qkv_first_new: float32 [768, 3, 768], P('dp', None, 'tensor')
- qkv_second_new: float32 [768, 3, 768], P('dp', None, 'tensor')
- out_master_new: float32 [768, 768], P('tensor', 'dp')
- out_copy_new: bfloat16 [768, 768], P('tensor', 'dp')
- out_first_new: float32 [768, 768], P('tensor', 'dp')
- out_second_new: float32 [768, 768], P('tensor', 'dp')
- up_master_new: float32 [768, 4, 768], P('dp', None, 'tensor')
- up_copy_new: bfloat16 [768, 4, 768], P('dp', None, 'tensor')
- up_first_new: float32 [768, 4, 768], P('dp', None, 'tensor')
- up_second_new: float32 [768, 4, 768], P('dp', None, 'tensor')
- down_master_new: float32 [4, 768, 768], P(None, 'tensor', 'dp')
- down_copy_new: bfloat16 [4, 768, 768], P(None, 'tensor', 'dp')
- down_first_new: float32 [4, 768, 768], P(None, 'tensor', 'dp')
- down_second_new: float32 [4, 768, 768], P(None, 'tensor', 'dp')
- shared_master_new: float32 [6, 768], P(None, 'dp')
- shared_copy_new: bfloat16 [6, 768], P(None, 'dp')
- shared_first_new: float32 [6, 768], P(None, 'dp')
- shared_second_new: float32 [6, 768], P(None, 'dp')
- split_master_new: float32 [6, 768], P(None, ('tensor', 'dp'))
- split_copy_new: bfloat16 [6, 768], P(None, ('tensor', 'dp'))
- split_first_new: float32 [6, 768], P(None, ('tensor', 'dp'))
- split_second_new: float32 [6, 768], P(None, ('tensor', 'dp'))
Inputs may be any that keep to these rules, and one draw needn't show every extreme that they name: `counts`: every count is 196 or 576, and both values occur in every draw.
All inputs are finite; a program needn't handle non-finite values.
Results may differ from a plain program's by a relative error of at most 0.012.
The roundings to bfloat16 on the way count: a program that leaves them out, or rounds other values in their place, can miss the bound.
Values may be sent and summed in bfloat16 or wider, within the bound.
A program may use at most 192 MiB of HBM per device.

v0:
```python
import jax
import jax.numpy as jnp
from jax import lax
from jax.sharding import PartitionSpec as P

D = 768
FF = 3072
HEAD_DIM = 64
LEN = 576
STEP = 10


LN_EPS = 1e-05
MASK_FILL = -1e30
BETA_ONE = 0.5
BETA_TWO = 0.5
ADAM_EPS = 1e-08
MATRIX_DECAY = 0.01
SQRT_HALF = 0.7071067811865476
INV_ROOT_TAU = 0.3989422804014327


def norm_forward(inputs, norm_gain, norm_shift):
    row_mean = jnp.mean(inputs, axis=-1, keepdims=True)
    centred = inputs - row_mean
    variance = jnp.mean(centred * centred, axis=-1, keepdims=True)
    inverse = lax.rsqrt(variance + LN_EPS)
    normal = centred * inverse
    return (normal * norm_gain + norm_shift, normal, inverse)


def norm_backward(grad_normed, normal, inverse, norm_gain):
    scaled = grad_normed * norm_gain
    first_mean = jnp.mean(scaled, axis=-1, keepdims=True)
    second_mean = jnp.mean(scaled * normal, axis=-1, keepdims=True)
    return inverse * (scaled - first_mean - normal * second_mean)


def gelu_exact(values):
    return 0.5 * values * (1.0 + lax.erf(values * SQRT_HALF))


def gelu_slope(values):
    return (
        0.5 * (1.0 + lax.erf(values * SQRT_HALF))
        + values * jnp.exp(-0.5 * values * values) * INV_ROOT_TAU
    )


def kind_rates():
    return (
        0.7 * D ** (-0.5),
        0.7 * (D * 16 // LEN) ** (-0.5),
        0.7 * D ** (-0.5),
        0.7 * FF ** (-0.5),
        0.6,
        0.4,
    )


def adamw(master, first, second, gradient, step_rate, decay_rate):
    first_new = BETA_ONE * first + (1.0 - BETA_ONE) * gradient
    second_new = BETA_TWO * second + (1.0 - BETA_TWO) * gradient * gradient
    first_hat = first_new / (1.0 - BETA_ONE**STEP)
    second_hat = second_new / (1.0 - BETA_TWO**STEP)
    master_new = master - step_rate * (
        first_hat / (jnp.sqrt(second_hat) + ADAM_EPS) + decay_rate * master
    )
    return (master_new, master_new.astype(jnp.bfloat16), first_new, second_new)


def local(
    tokens,
    cotangent,
    counts,
    qkv_master,
    qkv_first,
    qkv_second,
    out_master,
    out_first,
    out_second,
    up_master,
    up_first,
    up_second,
    down_master,
    down_first,
    down_second,
    shared_master,
    shared_first,
    shared_second,
    split_master,
    split_first,
    split_second,
):
    f32 = jnp.float32
    bf16 = jnp.bfloat16
    seq_count, length, model_width = tokens.shape
    row_count = seq_count * length
    qkv_weight, out_weight, up_weight, down_weight, shared_weight, split_weight = (
        lax.all_gather(qkv_master.astype(bf16), "dp", axis=0, tiled=True),
        lax.all_gather(out_master.astype(bf16), "dp", axis=1, tiled=True),
        lax.all_gather(up_master.astype(bf16), "dp", axis=0, tiled=True),
        lax.all_gather(down_master.astype(bf16), "dp", axis=2, tiled=True),
        lax.all_gather(shared_master.astype(bf16), "dp", axis=1, tiled=True),
        lax.all_gather(split_master.astype(bf16), "dp", axis=1, tiled=True),
    )
    shared_vecs = shared_weight.astype(f32)
    split_vecs = split_weight.astype(f32)
    local_width = qkv_weight.shape[2]
    local_heads = local_width // HEAD_DIM
    score_scale = HEAD_DIM ** (-0.5)
    places = lax.broadcasted_iota(jnp.int32, (seq_count, length), 1)
    valid_rows = (places < counts[:, None]).astype(f32)
    key_valid = valid_rows[:, None, None, :] > 0
    row_valid = valid_rows.reshape(row_count, 1)
    inputs = tokens.astype(f32).reshape(row_count, model_width)
    normed_one, normal_one, inverse_one = norm_forward(inputs, shared_vecs[0], shared_vecs[1])
    first_in = normed_one.astype(bf16)
    projected = jnp.einsum("rd,dkc->rkc", first_in, qkv_weight, preferred_element_type=f32)
    head_shape = (seq_count, length, local_heads, HEAD_DIM)
    queries = (projected[:, 0] + split_vecs[0]).astype(bf16).reshape(head_shape)
    keys_all = projected[:, 1].astype(bf16).reshape(head_shape)
    values_all = (projected[:, 2] + split_vecs[1]).astype(bf16).reshape(head_shape)
    raw_scores = (
        jnp.einsum("sqhe,skhe->shqk", queries, keys_all, preferred_element_type=f32) * score_scale
    )
    scores = jnp.where(key_valid, raw_scores, MASK_FILL)
    row_top = jnp.max(scores, axis=-1, keepdims=True)
    lifted = jnp.exp(scores - row_top)
    row_total = jnp.sum(lifted, axis=-1, keepdims=True)
    probs = lifted / row_total
    log_total = row_top + jnp.log(row_total)
    attended = jnp.einsum(
        "shqk,skhe->sqhe", probs.astype(bf16), values_all, preferred_element_type=f32
    )
    attended = attended.reshape(row_count, local_width).astype(bf16)
    attn_part = jnp.dot(attended, out_weight, preferred_element_type=f32)
    branch = lax.psum(attn_part, "tensor")
    middle = inputs + branch + shared_vecs[2]
    normed_two, normal_two, inverse_two = norm_forward(middle, shared_vecs[3], shared_vecs[4])
    second_in = normed_two.astype(bf16)
    hidden_pre = (
        jnp.einsum("rd,dfc->rfc", second_in, up_weight, preferred_element_type=f32) + split_vecs[2:]
    )
    hidden = gelu_exact(hidden_pre).astype(bf16)
    down_part = jnp.einsum("rfc,fcd->rd", hidden, down_weight, preferred_element_type=f32)
    down_sum = lax.psum(down_part, "tensor")
    result = middle + down_sum + shared_vecs[5]
    mixed_own = (result * row_valid).astype(bf16)
    grad_out = cotangent.astype(f32).reshape(row_count, model_width) * row_valid
    grad_out_low = grad_out.astype(bf16)
    grad_down = jnp.einsum("rfc,rd->fcd", hidden, grad_out_low, preferred_element_type=f32)
    grad_hidden = jnp.einsum("rd,fcd->rfc", grad_out_low, down_weight, preferred_element_type=f32)
    grad_pre = (grad_hidden * gelu_slope(hidden_pre)).astype(bf16)
    grad_up = jnp.einsum("rd,rfc->dfc", second_in, grad_pre, preferred_element_type=f32)
    grad_up_bias = jnp.sum(grad_pre, axis=0, dtype=f32)
    norm_two_part = jnp.einsum("rfc,dfc->rd", grad_pre, up_weight, preferred_element_type=f32)
    grad_norm_two = lax.psum(norm_two_part, "tensor")
    grad_middle = grad_out + norm_backward(grad_norm_two, normal_two, inverse_two, shared_vecs[3])
    grad_middle_low = grad_middle.astype(bf16)
    grad_out_weight = jnp.einsum("rc,rd->cd", attended, grad_middle_low, preferred_element_type=f32)
    grad_attended = jnp.einsum("rd,cd->rc", grad_middle_low, out_weight, preferred_element_type=f32)
    grad_attended = grad_attended.astype(bf16).reshape(head_shape)
    again_scores = (
        jnp.einsum("sqhe,skhe->shqk", queries, keys_all, preferred_element_type=f32) * score_scale
    )
    again_scores = jnp.where(key_valid, again_scores, MASK_FILL)
    again_probs = jnp.exp(again_scores - log_total)
    grad_values = jnp.einsum(
        "shqk,sqhe->skhe", again_probs.astype(bf16), grad_attended, preferred_element_type=f32
    )
    grad_probs = jnp.einsum(
        "sqhe,skhe->shqk", grad_attended, values_all, preferred_element_type=f32
    )
    row_inner = jnp.sum(again_probs * grad_probs, axis=-1, keepdims=True)
    grad_scores = (again_probs * (grad_probs - row_inner)).astype(bf16)
    grad_queries = (
        jnp.einsum("shqk,skhe->sqhe", grad_scores, keys_all, preferred_element_type=f32)
        * score_scale
    )
    grad_keys = (
        jnp.einsum("shqk,sqhe->skhe", grad_scores, queries, preferred_element_type=f32)
        * score_scale
    )
    grad_proj = jnp.stack(
        [
            grad_queries.reshape(row_count, local_width),
            grad_keys.reshape(row_count, local_width),
            grad_values.reshape(row_count, local_width),
        ],
        axis=1,
    ).astype(bf16)
    grad_qkv = jnp.einsum("rd,rkc->dkc", first_in, grad_proj, preferred_element_type=f32)
    norm_one_part = jnp.einsum("rkc,dkc->rd", grad_proj, qkv_weight, preferred_element_type=f32)
    grad_norm_one = lax.psum(norm_one_part, "tensor")
    grad_inputs = grad_middle + norm_backward(
        grad_norm_one, normal_one, inverse_one, shared_vecs[0]
    )
    shared_grad = jnp.stack(
        [
            jnp.sum(grad_norm_one * normal_one, axis=0),
            jnp.sum(grad_norm_one, axis=0),
            jnp.sum(grad_middle, axis=0),
            jnp.sum(grad_norm_two * normal_two, axis=0),
            jnp.sum(grad_norm_two, axis=0),
            jnp.sum(grad_out, axis=0),
        ]
    )
    bias_sums = jnp.sum(grad_proj, axis=0, dtype=f32)
    split_grad = jnp.concatenate([bias_sums[0:1], bias_sums[2:3], grad_up_bias], axis=0)
    summed_qkv, summed_out, summed_up, summed_down, summed_shared, summed_split = (
        lax.psum_scatter(grad_qkv, "dp", scatter_dimension=0, tiled=True),
        lax.psum_scatter(grad_out_weight, "dp", scatter_dimension=1, tiled=True),
        lax.psum_scatter(grad_up, "dp", scatter_dimension=0, tiled=True),
        lax.psum_scatter(grad_down, "dp", scatter_dimension=2, tiled=True),
        lax.psum_scatter(shared_grad, "dp", scatter_dimension=1, tiled=True),
        lax.psum_scatter(split_grad, "dp", scatter_dimension=1, tiled=True),
    )
    masters = (qkv_master, out_master, up_master, down_master, shared_master, split_master)
    firsts = (qkv_first, out_first, up_first, down_first, shared_first, split_first)
    seconds = (qkv_second, out_second, up_second, down_second, shared_second, split_second)
    summed = (summed_qkv, summed_out, summed_up, summed_down, summed_shared, summed_split)
    decays = (MATRIX_DECAY, MATRIX_DECAY, MATRIX_DECAY, MATRIX_DECAY, 0.0, 0.0)
    rates = kind_rates()
    outputs = [mixed_own.reshape(tokens.shape), grad_inputs.reshape(tokens.shape)]
    for kind in range(6):
        outputs.extend(
            adamw(
                masters[kind], firsts[kind], seconds[kind], summed[kind], rates[kind], decays[kind]
            )
        )
    return tuple(outputs)


def solution(mesh):
    in_specs = (
        P("dp", None, None),
        P("dp", None, None),
        P("dp"),
        P("dp", None, "tensor"),
        P("dp", None, "tensor"),
        P("dp", None, "tensor"),
        P("tensor", "dp"),
        P("tensor", "dp"),
        P("tensor", "dp"),
        P("dp", None, "tensor"),
        P("dp", None, "tensor"),
        P("dp", None, "tensor"),
        P(None, "tensor", "dp"),
        P(None, "tensor", "dp"),
        P(None, "tensor", "dp"),
        P(None, "dp"),
        P(None, "dp"),
        P(None, "dp"),
        P(None, ("tensor", "dp")),
        P(None, ("tensor", "dp")),
        P(None, ("tensor", "dp")),
    )
    out_specs = (
        P("dp", None, None),
        P("dp", None, None),
        P("dp", None, "tensor"),
        P("dp", None, "tensor"),
        P("dp", None, "tensor"),
        P("dp", None, "tensor"),
        P("tensor", "dp"),
        P("tensor", "dp"),
        P("tensor", "dp"),
        P("tensor", "dp"),
        P("dp", None, "tensor"),
        P("dp", None, "tensor"),
        P("dp", None, "tensor"),
        P("dp", None, "tensor"),
        P(None, "tensor", "dp"),
        P(None, "tensor", "dp"),
        P(None, "tensor", "dp"),
        P(None, "tensor", "dp"),
        P(None, "dp"),
        P(None, "dp"),
        P(None, "dp"),
        P(None, "dp"),
        P(None, ("tensor", "dp")),
        P(None, ("tensor", "dp")),
        P(None, ("tensor", "dp")),
        P(None, ("tensor", "dp")),
    )
    return jax.shard_map(local, mesh=mesh, in_specs=in_specs, out_specs=out_specs, check_vma=False)
```

profile of v0, /device:TPU:0, one launch (start us, length us, event | category | flops | bytes accessed | tf_op | source)
XLA Modules:
  0.0 1285.4 jit_solution(1328081314007520663)
XLA Ops:
  21.0 10.5 all-gather
  36.3 14.2 %all_gather.19 = bf16[768,3,192]{2,1,0:T(4,128)(2,1)} all-gather(bf16[96,3,192]{2,1,0:T(4,128)(2,1)S(1)} %copy.137), channel_id=1, replica_groups=mesh['dp'=8,'tensor'=4] {'dp'}, dimensions={0}, use_global_device_ids=true | all-gather | bytes 995328 | tf_op jit(solution)/shard_map/all_gather | solution.py:100
  62.1 8.9 all-gather.1
  90.3 5.5 fusion.45
  97.2 8.9 all_gather.21
  124.9 234.6 %all-reduce.6.cloned.1.call-done = f32[2304,768]{1,0:T(8,128)} async-done(((f32[2304,768]{1,0:T(8,128)}), f32[2304,768]{1,0:T(8,128)}) %all-reduce.6.cloned.1.call-update) | async-done | bytes 7077904 | tf_op jit(solution)/shard_map/psum | solution.py:138
  369.0 6.7 convert_reduce_fusion.1
  404.4 10.4 fusion.29
  414.9 214.7 %all-reduce.8.cloned.1.call-done = f32[2304,768]{1,0:T(8,128)} async-done(((f32[2304,768]{1,0:T(8,128)}), f32[2304,768]{1,0:T(8,128)}) %all-reduce.8.cloned.1.call-update) | async-done | bytes 7077904 | tf_op jit(solution)/shard_map/psum | solution.py:158
  629.6 8.0 multiply_reduce_fusion.2
  637.8 8.4 fusion.80
  654.9 10.7 fusion.48
  665.6 14.2 %multiply_reduce_fusion = (f32[4,3,576]{2,1,0:T(4,128)}, f32[4,3,576,576]{2,3,1,0:T(8,128)}) fusion(f32[4,3,576]{2,1,0:T(4,128)S(1)} %copy-done.28, f32[4,3,576,576]{2,3,1,0:T(8,128)} %copy-done, pred[4,576]{1,0:T(4,128)(4,1)S(1)} %get-tuple-element.181, f32[4,576,3,64]{1,0,3,2:T(4,128)S(1)} %copy-done.11, f32[3,64]{1,0:T(4,128)S(1)} %copy-done.43, ...), kind=kOutput, calls=%fused_computation.1 | convolution fusion | flops 530392320 | bytes 34563072 | tf_op jit(solution)/shard_map/sqhe,skhe->shqk/dot_general | solution.py:172
  684.3 16.1 %multiply_convert_fusion = bf16[4,3,576,576]{2,3,1,0:T(8,128)(2,1)} fusion(f32[4,3,576,576]{2,3,1,0:T(8,128)} %get-tuple-element.185, f32[4,3,576]{2,1,0:T(4,128)} %get-tuple-element.184, f32[4,3,576]{2,1,0:T(4,128)} %log_add_fusion, f32[4,3,576,576]{2,3,1,0:T(8,128)} %copy-done, pred[4,576]{1,0:T(4,128)(4,1)S(1)} %get-tuple-element.181), kind=kLoop, calls=%fused_computation | loop fusion | flops 23887872 | bytes 39870720 | tf_op jit(solution)/shard_map/convert_element_type | solution.py:176
  710.3 6.8 fusion.47
  723.8 5.7 fusion.51
  733.9 7.3 fusion.31
  741.3 8.3 convolution_bitcast_fusion.2
  775.4 15.3 %all-reduce = f32[6,192]{1,0:T(8,128)} all-reduce(f32[6,192]{1,0:T(8,128)} %pad_maximum_fusion), channel_id=7, replica_groups=mesh['dp'=8,'tensor'=4] {'dp'}, use_global_device_ids=true, to_apply=%region_28.29.clone | all-reduce | flops 1152 | bytes 9216
  795.5 13.8 %reduce-scatter.13.cloned.1.call-done = f32[96,3,192]{2,0,1:T(8,128)} async-done(((f32[768,3,192]{2,0,1:T(8,128)}), f32[96,3,192]{2,0,1:T(8,128)}) %reduce-scatter.13.cloned.1.call-update) | async-done | bytes 221200 | tf_op jit(solution)/shard_map/reduce_scatter | solution.py:212
  811.7 419.6 %all-reduce.10.cloned.1.call-done = (f32[2304,768]{1,0:T(8,128)}, f32[2304,768]{1,0:T(8,128)}) async-done(((f32[2304,768]{1,0:T(8,128)}, f32[2304,768]{1,0:T(8,128)}), (f32[2304,768]{1,0:T(8,128)}, f32[2304,768]{1,0:T(8,128)})) %all-reduce.10.cloned.1.call-update) | async-done | bytes 14155792 | tf_op jit(solution)/shard_map/psum | solution.py:147
  1231.2 5.8 fusion.26
  1242.5 14.1 %fusion.25 = (f32[2304,768]{1,0:T(8,128)}, bf16[2304,768]{1,0:T(8,128)(2,1)}) fusion(f32[2304,768]{1,0:T(8,128)} %get-tuple-element.157, bf16[4,576,768]{2,1,0:T(8,128)(2,1)S(1)} %copy-done.3, f32[2304,768]{1,0:T(8,128)} %get-tuple-element.147, f32[2304]{0:T(1024)} %broadcast_multiply_fusion, f32[2304]{0:T(1024)} %broadcast_multiply_fusion.1, ...), kind=kLoop, calls=%fused_computation.36 | loop fusion | flops 23003136 | bytes 42519552 | tf_op jit(solution)/shard_map/add | solution.py:196
  1256.6 18.7 %reduce-scatter.21.cloned.1.call-done = f32[96,6]{1,0:T(8,128)} async-done(((f32[768,6]{1,0:T(8,128)}), f32[96,6]{1,0:T(8,128)}) %reduce-scatter.21.cloned.1.call-update) | async-done | bytes 2320
  (234 shorter events, 181.1 us)
Async XLA Ops:
  8.1 109.3 %all-gather.5.cloned.1.call-start = ((), (), s32[]{:S(2)}) async-start(), calls=%async_computation.6 | async-start | bytes 1769472 | tf_op jit(solution)/shard_map/all_gather | solution.py:102
  10.0 111.2 %all-gather.7.cloned.1.call-start = ((), (), s32[]{:S(2)}) async-start(), calls=%async_computation.7 | async-start | bytes 1769472 | tf_op jit(solution)/shard_map/all_gather | solution.py:103
  12.0 347.4 %all-reduce.6.cloned.1.call-start = ((), (), s32[]{:S(2)}) async-start(), calls=%async_computation.5 | async-start | bytes 14155776 | tf_op jit(solution)/shard_map/psum | solution.py:138
  17.8 41.1 %copy-start.29 = (f32[2304]{0:T(1024)}, f32[2304]{0:T(1024)S(1)}, u32[]{:S(2)}) copy-start(f32[2304]{0:T(1024)S(1)} %div.89) | copy-start | bytes 27652
  35.2 23.8 %copy-start.40 = (f32[768]{0:T(1024)}, f32[768]{0:T(1024)S(1)}, u32[]{:S(2)}) copy-start(f32[768]{0:T(1024)S(1)} %get-tuple-element.143) | copy-start | bytes 9220
  59.0 12.3 copy-start.26
  71.2 16.5 %copy-start.42 = (f32[3,64]{1,0:T(4,128)}, f32[3,64]{1,0:T(4,128)S(1)}, u32[]{:S(2)}) copy-start(f32[3,64]{1,0:T(4,128)S(1)} %add.228) | copy-start | bytes 2308
  71.3 12.4 copy-start.36
  97.2 13.7 %copy-start.7 = (bf16[2304,192]{0,1:T(8,128)(2,1)}, bf16[2304,192]{0,1:T(8,128)(2,1)S(1)}, u32[]{:S(2)}) copy-start(bf16[2304,192]{0,1:T(8,128)(2,1)S(1)} %convert_element_type.141) | copy-start | bytes 2654212
  111.0 248.5 %copy-start.3 = (bf16[4,576,768]{2,1,0:T(8,128)(2,1)S(1)}, bf16[4,576,768]{2,1,0:T(8,128)(2,1)}, u32[]{:S(2)}) copy-start(bf16[4,576,768]{2,1,0:T(8,128)(2,1)} %param.21) | copy-start | bytes 10616836
  111.0 518.6 %all-reduce.8.cloned.1.call-start = ((), (), s32[]{:S(2)}) async-start(), calls=%async_computation.8 | async-start | bytes 14155776 | tf_op jit(solution)/shard_map/psum | solution.py:158
  112.7 250.7 %copy-start.31 = (f32[2304]{0:T(1024)}, f32[2304]{0:T(1024)S(1)}, u32[]{:S(2)}) copy-start(f32[2304]{0:T(1024)S(1)} %reshape.204) | copy-start | bytes 27652
  382.5 377.7 %reduce-scatter.19.cloned.1.call-start = ((), (), s32[]{:S(2)}) async-start(), calls=%async_computation.12 | async-start | bytes 2654208
  402.9 361.3 %reduce-scatter.15.cloned.1.call-start = ((), (), s32[]{:S(2)}) async-start(), calls=%async_computation.10 | async-start | bytes 3538944 | tf_op jit(solution)/shard_map/reduce_scatter | solution.py:214
  414.8 377.2 %reduce-scatter.17.cloned.1.call-start = ((), (), s32[]{:S(2)}) async-start(), calls=%async_computation.11 | async-start | bytes 884736
  654.9 10.7 copy-start.15
  654.9 10.7 copy-start.28
  654.9 10.7 copy-start.43
  684.3 16.1 %copy-start.9 = (bf16[4,576,3,64]{1,0,3,2:T(4,128)(2,1)S(1)}, bf16[4,576,3,64]{1,0,3,2:T(4,128)(2,1)}, u32[]{:S(2)}) copy-start(bf16[4,576,3,64]{1,0,3,2:T(4,128)(2,1)} %copy-done.8) | copy-start | bytes 2654212
  729.5 79.8 %reduce-scatter.13.cloned.1.call-start = ((), (), s32[]{:S(2)}) async-start(), calls=%async_computation.9 | async-start | bytes 2654208 | tf_op jit(solution)/shard_map/reduce_scatter | solution.py:212
  741.2 490.0 %all-reduce.10.cloned.1.call-start = ((), (), s32[]{:S(2)}) async-start(), calls=%async_computation.14 | async-start | bytes 28311552 | tf_op jit(solution)/shard_map/psum | solution.py:147
  754.9 520.5 %reduce-scatter.21.cloned.1.call-start = ((), (), s32[]{:S(2)}) async-start(), calls=%async_computation.13 | async-start | bytes 442368
  764.2 467.0 %copy-start.30 = (f32[2304]{0:T(1024)S(1)}, f32[2304]{0:T(1024)}, u32[]{:S(2)}) copy-start(f32[2304]{0:T(1024)} %copy-done.29) | copy-start | bytes 27652
  764.2 467.0 %copy-start.41 = (f32[768]{0:T(1024)S(1)}, f32[768]{0:T(1024)}, u32[]{:S(2)}) copy-start(f32[768]{0:T(1024)} %copy-done.40) | copy-start | bytes 9220
  (43 other events, 249.4 us)
Sparse Core Ops, SparseCore 0:
  11.4 28.3 all-gather.4
  42.2 25.6 all-gather.6
  403.0 41.9 reduce-scatter.18
  449.2 46.2 reduce-scatter.14
  729.6 33.8 reduce-scatter.16
  766.8 42.5 reduce-scatter.12
  1242.6 32.6 reduce-scatter.20
Sparse Core Ops, SparseCore 1:
  111.0 248.3 all-reduce.5
  382.6 247.0 all-reduce.7
  755.0 476.2 all-reduce.9
where the time goes:
time: 1290 us
  waiting for transfers between devices  902 us (70%)
  matrix products  115 us (9%)
  other arithmetic  102 us (8%)
  local copies, waits for them, and re-layouts  91.9 us (7%)
  blocking collectives  57.7 us (4%)
  between operations  17.4 us (1%)
    psum x1, waiting for transfers between devices, local(): down_sum = lax.psum(down_part, 'tensor')  420 us
    psum x1, waiting for transfers between devices, local(): branch = lax.psum(attn_part, 'tensor')  235 us
    psum x1, waiting for transfers between devices, local(): grad_norm_two = lax.psum(norm_two_part, 'tensor')  215 us
    unnamed x130, local copies, waits for them, and re-layouts  37.6 us
  transfers between devices with their start and end apart: 10, of which 5 were waited for; matrix products, arithmetic and copies ran while one was open for 21% of the time, Pallas kernels for 0%

commit v1 on v0

v1 whole, which is shorter than its diff:
```python
import jax
import jax.numpy as jnp
from jax import lax
from jax.sharding import PartitionSpec as P

D = 768
FF = 3072
HEAD_DIM = 64
LEN = 576
STEP = 10


LN_EPS = 1e-05
MASK_FILL = -1e30
BETA_ONE = 0.5
BETA_TWO = 0.5
ADAM_EPS = 1e-08
MATRIX_DECAY = 0.01
SQRT_HALF = 0.7071067811865476
INV_ROOT_TAU = 0.3989422804014327
AXES = ("tensor", "dp")


def norm_forward(inputs, norm_gain, norm_shift):
    row_mean = jnp.mean(inputs, axis=-1, keepdims=True)
    centred = inputs - row_mean
    variance = jnp.mean(centred * centred, axis=-1, keepdims=True)
    inverse = lax.rsqrt(variance + LN_EPS)
    normal = centred * inverse
    return (normal * norm_gain + norm_shift, normal, inverse)


def norm_backward(grad_normed, normal, inverse, norm_gain):
    scaled = grad_normed * norm_gain
    first_mean = jnp.mean(scaled, axis=-1, keepdims=True)
    second_mean = jnp.mean(scaled * normal, axis=-1, keepdims=True)
    return inverse * (scaled - first_mean - normal * second_mean)


def gelu_exact(values):
    return 0.5 * values * (1.0 + lax.erf(values * SQRT_HALF))


def gelu_slope(values):
    return (
        0.5 * (1.0 + lax.erf(values * SQRT_HALF))
        + values * jnp.exp(-0.5 * values * values) * INV_ROOT_TAU
    )


def kind_rates():
    return (
        0.7 * D ** (-0.5),
        0.7 * (D * 16 // LEN) ** (-0.5),
        0.7 * D ** (-0.5),
        0.7 * FF ** (-0.5),
        0.6,
        0.4,
    )


def adamw(master, first, second, gradient, step_rate, decay_rate):
    first_new = BETA_ONE * first + (1.0 - BETA_ONE) * gradient
    second_new = BETA_TWO * second + (1.0 - BETA_TWO) * gradient * gradient
    first_hat = first_new / (1.0 - BETA_ONE**STEP)
    second_hat = second_new / (1.0 - BETA_TWO**STEP)
    master_new = master - step_rate * (
        first_hat / (jnp.sqrt(second_hat) + ADAM_EPS) + decay_rate * master
    )
    return (master_new, master_new.astype(jnp.bfloat16), first_new, second_new)


def pack_attention(qkv, out):
    q, k, v = qkv[:, 0], qkv[:, 1], qkv[:, 2]
    return jnp.concatenate(
        [
            q[:, :128], k[:, :128], v[:, :128],
            q[:, 128:], out[:, :64], k[:, 128:], out[:, 64:128], v[:, 128:], out[:, 128:],
        ],
        axis=1,
    )


def unpack_attention(block):
    pair = [block[:, 128 * i : 128 * i + 128] for i in range(6)]
    q = jnp.concatenate([pair[0], pair[3][:, :64]], axis=1)
    k = jnp.concatenate([pair[1], pair[4][:, :64]], axis=1)
    v = jnp.concatenate([pair[2], pair[5][:, :64]], axis=1)
    o = jnp.concatenate([pair[3][:, 64:], pair[4][:, 64:], pair[5][:, 64:]], axis=1)
    return jnp.stack([q, k, v], axis=1), o


def local(tokens, cotangent, counts, *state):
    f32 = jnp.float32
    bf16 = jnp.bfloat16
    masters, firsts, seconds = state[0::3], state[1::3], state[2::3]
    qkv_master, out_master, up_master, down_master, shared_master, split_master = masters
    groups = lax.axis_size("tensor")
    copies = lax.axis_size("dp")
    seq_count, length, width = tokens.shape
    share = seq_count // groups
    mine = lax.axis_index("tensor") * share
    rows = share * length
    band = qkv_master.shape[0]

    attn_own = pack_attention(qkv_master.astype(bf16), out_master.astype(bf16).T)
    up_own = up_master.astype(bf16).reshape(band, -1)
    down_own = down_master.astype(bf16).reshape(-1, band).T
    mats = lax.all_gather(jnp.stack([attn_own, up_own, down_own]), AXES, axis=1, tiled=True)
    mats = mats.reshape(3, groups, width, width)
    shared_vecs = lax.all_gather(shared_master.astype(bf16), "dp", axis=1, tiled=True).astype(f32)
    split_vecs = lax.all_gather(split_master.astype(bf16), AXES, axis=1, tiled=True).astype(f32)

    x_low = lax.dynamic_slice_in_dim(tokens, mine, share, 0)
    cot = lax.dynamic_slice_in_dim(cotangent, mine, share, 0)
    cnt = lax.dynamic_slice_in_dim(counts, mine, share, 0)
    inputs = x_low.astype(f32).reshape(rows, width)
    places = lax.broadcasted_iota(jnp.int32, (share, length), 1)
    valid_rows = (places < cnt[:, None]).astype(f32)
    key_valid = valid_rows[None, :, None, None, :] > 0
    row_valid = valid_rows.reshape(rows, 1)

    normed_one, normal_one, inverse_one = norm_forward(inputs, shared_vecs[0], shared_vecs[1])
    first_in = normed_one.astype(bf16)
    proj = jnp.einsum("rd,gdc->grc", first_in, mats[0], preferred_element_type=f32)
    bias = split_vecs[:2].reshape(2, groups, 1, -1)
    part = [proj[:, :, 128 * i : 128 * i + 128] for i in range(6)]
    q = jnp.concatenate([part[0], part[3][:, :, :64]], axis=2) + bias[0]
    k = jnp.concatenate([part[1], part[4][:, :, :64]], axis=2)
    v = jnp.concatenate([part[2], part[5][:, :, :64]], axis=2) + bias[1]
    hs = (groups, share, length, -1, HEAD_DIM)
    q, k, v = (t.astype(bf16).reshape(hs) for t in (q, k, v))
    raw = jnp.einsum("gsqhe,gskhe->gshqk", q, k, preferred_element_type=f32) * HEAD_DIM ** (-0.5)
    scores = jnp.where(key_valid, raw, MASK_FILL)
    top = jnp.max(scores, axis=-1, keepdims=True)
    lifted = jnp.exp(scores - top)
    probs = lifted / jnp.sum(lifted, axis=-1, keepdims=True)
    probs_low = probs.astype(bf16)
    attended = jnp.einsum("gshqk,gskhe->gsqhe", probs_low, v, preferred_element_type=f32)
    attended = attended.reshape(groups, rows, -1).astype(bf16)
    out_t = jnp.concatenate(
        [mats[0][:, :, 128 * i + 64 : 128 * i + 128] for i in (3, 4, 5)], axis=2
    )
    branch = jnp.einsum("grc,gdc->rd", attended, out_t, preferred_element_type=f32)
    middle = inputs + branch + shared_vecs[2]
    normed_two, normal_two, inverse_two = norm_forward(middle, shared_vecs[3], shared_vecs[4])
    second_in = normed_two.astype(bf16)
    up_bias = split_vecs[2:].reshape(-1, groups, 1, width // groups)
    up_bias = jnp.swapaxes(up_bias, 0, 1).reshape(groups, 1, width)
    hidden_pre = jnp.einsum("rd,gdc->grc", second_in, mats[1], preferred_element_type=f32) + up_bias
    hidden = gelu_exact(hidden_pre).astype(bf16)
    down_sum = jnp.einsum("grc,gdc->rd", hidden, mats[2], preferred_element_type=f32)
    mixed = ((middle + down_sum + shared_vecs[5]) * row_valid).astype(bf16)
    mixed = lax.all_gather(mixed.reshape(share, length, width), "tensor", axis=0, tiled=True)

    grad_out = cot.astype(f32).reshape(rows, width) * row_valid
    grad_out_low = grad_out.astype(bf16)
    grad_down = jnp.einsum("rd,grc->gdc", grad_out_low, hidden, preferred_element_type=f32)
    grad_hidden = jnp.einsum("rd,gdc->grc", grad_out_low, mats[2], preferred_element_type=f32)
    grad_pre = (grad_hidden * gelu_slope(hidden_pre)).astype(bf16)
    grad_up = jnp.einsum("rd,grc->gdc", second_in, grad_pre, preferred_element_type=f32)
    grad_up_bias = jnp.sum(grad_pre, axis=1, dtype=f32)
    grad_norm_two = jnp.einsum("grc,gdc->rd", grad_pre, mats[1], preferred_element_type=f32)
    grad_middle = grad_out + norm_backward(grad_norm_two, normal_two, inverse_two, shared_vecs[3])
    grad_middle_low = grad_middle.astype(bf16)
    grad_out_t = jnp.einsum("rd,grc->gdc", grad_middle_low, attended, preferred_element_type=f32)
    grad_att = jnp.einsum("rd,gdc->grc", grad_middle_low, out_t, preferred_element_type=f32)
    grad_att = grad_att.astype(bf16).reshape(hs)
    grad_v = jnp.einsum("gshqk,gsqhe->gskhe", probs_low, grad_att, preferred_element_type=f32)
    grad_probs = jnp.einsum("gsqhe,gskhe->gshqk", grad_att, v, preferred_element_type=f32)
    inner = jnp.sum(probs * grad_probs, axis=-1, keepdims=True)
    grad_scores = (probs * (grad_probs - inner)).astype(bf16)
    scale = HEAD_DIM ** (-0.5)
    grad_q = jnp.einsum("gshqk,gskhe->gsqhe", grad_scores, k, preferred_element_type=f32) * scale
    grad_k = jnp.einsum("gshqk,gsqhe->gskhe", grad_scores, q, preferred_element_type=f32) * scale
    grad_q, grad_k, grad_v = (
        t.reshape(groups, rows, -1).astype(bf16) for t in (grad_q, grad_k, grad_v)
    )
    zero = jnp.zeros((groups, rows, 64), bf16)
    grad_proj = jnp.concatenate(
        [
            grad_q[:, :, :128], grad_k[:, :, :128], grad_v[:, :, :128],
            grad_q[:, :, 128:], zero, grad_k[:, :, 128:], zero, grad_v[:, :, 128:], zero,
        ],
        axis=2,
    )
    grad_attn = jnp.einsum("rd,grc->gdc", first_in, grad_proj, preferred_element_type=f32)
    wide = jnp.concatenate(
        [jnp.pad(grad_out_t[:, :, 64 * i : 64 * i + 64], ((0, 0), (0, 0), (64, 0))) for i in range(3)],
        axis=2,
    )
    grad_attn = grad_attn + jnp.pad(wide, ((0, 0), (0, 0), (384, 0)))
    grad_norm_one = jnp.einsum("grc,gdc->rd", grad_proj, mats[0], preferred_element_type=f32)
    grad_inputs = grad_middle + norm_backward(
        grad_norm_one, normal_one, inverse_one, shared_vecs[0]
    )
    grad_inputs = grad_inputs.astype(bf16).reshape(share, length, width)
    grad_inputs = lax.all_gather(grad_inputs, "tensor", axis=0, tiled=True).astype(f32)

    grads = jnp.stack([grad_attn, grad_up, grad_down]).astype(bf16)
    grads = grads.reshape(3, groups * copies, band, width)
    grads = lax.psum_scatter(grads, AXES, scatter_dimension=1, tiled=False).astype(f32)
    shared_grad = jnp.stack(
        [
            jnp.sum(grad_norm_one * normal_one, axis=0),
            jnp.sum(grad_norm_one, axis=0),
            jnp.sum(grad_middle, axis=0),
            jnp.sum(grad_norm_two * normal_two, axis=0),
            jnp.sum(grad_norm_two, axis=0),
            jnp.sum(grad_out, axis=0),
        ]
    )
    bias_q = jnp.sum(grad_q, axis=1, dtype=f32).reshape(1, width)
    bias_v = jnp.sum(grad_v, axis=1, dtype=f32).reshape(1, width)
    bias_u = jnp.swapaxes(grad_up_bias.reshape(groups, -1, width // groups), 0, 1)
    split_grad = jnp.concatenate([bias_q, bias_v, bias_u.reshape(-1, width)], axis=0)
    vec_sum = lax.psum(jnp.concatenate([shared_grad, split_grad]), AXES)
    at = lax.axis_index("dp")
    shared_sum = lax.dynamic_slice_in_dim(vec_sum[:6], at * band, band, 1)
    thin = split_master.shape[1]
    split_at = (lax.axis_index("tensor") * copies + at) * thin
    split_sum = lax.dynamic_slice_in_dim(vec_sum[6:], split_at, thin, 1)

    sum_qkv, sum_out = unpack_attention(grads[0])
    summed = (
        sum_qkv,
        sum_out.T,
        grads[1].reshape(up_master.shape),
        grads[2].T.reshape(down_master.shape),
        shared_sum,
        split_sum,
    )
    decays = (MATRIX_DECAY, MATRIX_DECAY, MATRIX_DECAY, MATRIX_DECAY, 0.0, 0.0)
    rates = kind_rates()
    outputs = [mixed, grad_inputs]
    for kind in range(6):
        outputs.extend(
            adamw(
                masters[kind], firsts[kind], seconds[kind], summed[kind], rates[kind], decays[kind]
            )
        )
    return tuple(outputs)


def solution(mesh):
    rows = P("dp", None, None)
    state = (
        P("dp", None, "tensor"),
        P("tensor", "dp"),
        P("dp", None, "tensor"),
        P(None, "tensor", "dp"),
        P(None, "dp"),
        P(None, ("tensor", "dp")),
    )
    in_specs = (rows, rows, P("dp")) + tuple(s for s in state for _ in range(3))
    out_specs = (rows, rows) + tuple(s for s in state for _ in range(4))
    return jax.shard_map(local, mesh=mesh, in_specs=in_specs, out_specs=out_specs, check_vma=False)
```

time: 1290 us -> 540 us (0.42)
  waiting for transfers between devices: 902 us -> 193 us
  other arithmetic: 102 us -> 53.1 us
  blocking collectives: 57.7 us -> 96 us
  local copies, waits for them, and re-layouts: 91.9 us -> 69.9 us
    psum x3 -> x0, waiting for transfers between devices: 869 us -> none  [the longest x1 420 us: local(): down_sum = lax.psum(down_part, 'tensor')]
    reduce_scatter x2 -> x1, waiting for transfers between devices: 13.8 us -> 159 us  [local(): lax.psum_scatter(grads, AXES, scatter_dimension=1, tiled=False).astype(f32)]
    psum x0 -> x1, blocking collectives: none -> 42.3 us  [local(): vec_sum = lax.psum(jnp.concatenate([shared_grad, split_grad]), AXES)]
    all_gather x2 -> x3, waiting for transfers between devices: 0.01 us -> 33.4 us  [the longest x1 33.4 us: local(): lax.all_gather(jnp.stack([attn_own, up_own, down_own]), AXES, axis=1, til...]
    unnamed x130 -> x134, local copies, waits for them, and re-layouts: 37.6 us -> 13.5 us
    slice x6 -> x30, local copies, waits for them, and re-layouts: 4.68 us -> 27.5 us  [the longest x1 9.5 us: local(): mats[2]]
    reduce_sum x5 -> x0, other arithmetic: 21 us -> none  [the longest x1 7.95 us: local(): jnp.sum(grad_norm_two * normal_two, axis=0)]
    unnamed x13 -> x4, waiting for transfers between devices: 18.9 us -> 0.07 us
  transfers between devices with their start and end apart: 10 -> 4, of which waited for: 5 -> 2; matrix products, arithmetic and copies ran while one was open for 21% -> 25% of each run, Pallas kernels for 0% -> 0%
where the time goes in v1:
time: 540 us; the launch traced here: 530 us
  waiting for transfers between devices  193 us (36%)
  matrix products  103 us (19%)
  blocking collectives  96 us (18%)
  local copies, waits for them, and re-layouts  69.9 us (13%)
  other arithmetic  53.1 us (10%)
  between operations  15.2 us (3%)
    reduce_scatter x1, waiting for transfers between devices, local(): lax.psum_scatter(grads, AXES, scatter_dimension=1, tiled=False).astype(f32)  159 us
    all_gather x1, blocking collectives, local(): lax.all_gather(split_master.astype(bf16), AXES, axis=1, tiled=True)  43.4 us
    psum x1, blocking collectives, local(): vec_sum = lax.psum(jnp.concatenate([shared_grad, split_grad]), AXES)  42.3 us
    all_gather x1, waiting for transfers between devices, local(): lax.all_gather(jnp.stack([attn_own, up_own, down_own]), AXES, axis=1, til...  33.4 us
    unnamed x134, local copies, waits for them, and re-layouts  13.5 us
    convert_element_type x1, other arithmetic, local(): grad_scores = (probs * (grad_probs - inner)).astype(bf16)  12.3 us
    dot_general x1, matrix products, local(): jnp.einsum('gsqhe,gskhe->gshqk', grad_att, v, preferred_element_type=f32)  11.2 us
  transfers between devices with their start and end apart: 4, of which 2 were waited for; matrix products, arithmetic and copies ran while one was open for 25% of the time, Pallas kernels for 0%

profile of v1, /device:TPU:0, one launch (start us, length us, event | category | flops | bytes accessed | tf_op | source)
XLA Modules:
  0.0 530.3 jit_solution(9219583557550730250)
XLA Ops:
  28.5 10.3 %all-gather.2 = bf16[8,96,6]{1,2,0:T(8,128)(2,1)S(1)} all-gather(bf16[1,96,6]{1,2,0:T(8,128)(2,1)S(1)} %convert_bitcast_fusion.4), channel_id=1, replica_groups=mesh['dp'=8,'tensor'=4] {'dp'}, dimensions={0}, use_global_device_ids=true | all-gather | bytes 10368 | tf_op jit(solution)/shard_map/all_gather | solution.py:111
  41.6 43.4 %all-gather.3 = bf16[32,24,6]{1,2,0:T(8,128)(2,1)} all-gather(bf16[1,24,6]{1,2,0:T(8,128)(2,1)S(1)} %convert_bitcast_fusion.3), channel_id=1, replica_groups=mesh['dp'=8,'tensor'=4] {'tensor','dp'}, dimensions={0}, use_global_device_ids=true | all-gather | bytes 9504 | tf_op jit(solution)/shard_map/all_gather | solution.py:112
  100.6 33.4 %all-gather.8.cloned.1.call-done = bf16[3,3072,768]{2,1,0:T(8,128)(2,1)} async-done(((bf16[3,96,768]{2,1,0:T(8,128)(2,1)}), bf16[3,3072,768]{2,1,0:T(8,128)(2,1)}) %all-gather.8.cloned.1.call-update) | async-done | bytes 14155792 | tf_op jit(solution)/shard_map/all_gather | solution.py:109
  134.1 9.5 %fusion.122 = (bf16[1,3072,768]{2,1,0:T(8,128)(2,1)}, bf16[1,3072,768]{2,1,0:T(8,128)(2,1)}, bf16[1,3072,768]{2,1,0:T(8,128)(2,1)S(1)}) fusion(bf16[3,3072,768]{2,1,0:T(8,128)(2,1)} %all-gather.8.cloned.1.call-done), kind=kLoop, calls=%fused_computation.202 | loop fusion | bytes 28311552 | tf_op jit(solution)/shard_map/slice | solution.py:152
  143.6 3.0 fusion.131
  156.1 10.3 %fusion.132 = (f32[4,3,576]{2,1,0:T(4,128)S(1)}, f32[4,3,576,576]{2,3,1,0:T(8,128)}) fusion(pred[576]{0:T(1024)(128)(4,1)S(1)} %copy-done.51, bf16[4,576,3,64]{1,3,2,0:T(8,128)(2,1)S(1)} %bitcast.284, f32[4,576,3,64]{1,3,2,0:T(8,128)S(1)} %bitcast.266, f32[4,3,64]{2,1,0:T(4,128)S(1)} %copy-done.30), kind=kOutput, calls=%fused_computation.212 | convolution fusion | flops 526418496 | bytes 18610752 | tf_op jit(solution)/shard_map/sub | solution.py:136
  166.5 8.5 %fusion.56 = bf16[4,3,64,576]{3,2,1,0:T(8,128)(2,1)S(1)} fusion(f32[4,576,3,64]{1,3,2,0:T(8,128)} %bitcast.288, f32[4,3,64]{2,1,0:T(4,128)S(1)} %copy-done.41, f32[4,3,576,576]{2,3,1,0:T(8,128)} %get-tuple-element.234, f32[4,3,576]{2,1,0:T(4,128)S(1)} %get-tuple-element.233), kind=kOutput, calls=%fused_computation.101 | convolution fusion | flops 518897664 | bytes 18610176 | tf_op jit(solution)/shard_map/gshqk,gskhe->gsqhe/dot_general | solution.py:139
  175.1 3.4 fusion.133
  179.0 7.5 %fusion.13 = (bf16[4,576,768]{2,1,0:T(8,128)(2,1)S(1)}, f32[4,768,576]{1,2,0:T(8,128)}) fusion(f32[4,768]{1,0:T(4,128)S(1)} %copy-done.40, bf16[4,768,768]{2,1,0:T(8,128)(2,1)} %bitcast.273, f32[576,768]{1,0:T(8,128)S(1)} %get-tuple-element.236, f32[768]{0:T(1024)S(1)} %copy-done.48, f32[768]{0:T(1024)S(1)} %copy-done.37, f32[576]{0:T(1024)S(1)} %add_rsqrt_fusion, ...), kind=kOutput, calls=%fused_computation.23 | convolution fusion | flops 2730737664 | bytes 17127936 | tf_op jit(solution)/shard_map/rd,gdc->grc/dot_general | solution.py:150
  188.4 3.9 fusion.53
  192.3 8.4 %convert_reduce_fusion = (f32[4,768]{1,0:T(4,128)S(1)}, bf16[4,576,768]{2,1,0:T(8,128)(2,1)S(1)}) fusion(f32[4,768,576]{1,2,0:T(8,128)} %get-tuple-element.238, f32[4,768]{1,0:T(4,128)S(1)} %copy-done.40, bf16[4,768,768]{2,1,0:T(8,128)(2,1)} %bitcast.275, f32[576]{0:T(1024)S(1)} %get-tuple-element.251, bf16[4,576,768]{2,1,0:T(8,128)(2,1)} %param.22, ...), kind=kOutput, calls=%fused_computation.26 | convolution fusion | flops 2742236160 | bytes 16247044 | tf_op jit(solution)/shard_map/rd,gdc->grc/dot_general | solution.py:159
  200.8 6.9 %fusion.50 = (f32[768]{0:T(1024)S(1)}, f32[576]{0:T(1024)S(1)}, f32[576]{0:T(1024)S(1)}, f32[768]{0:T(1024)S(1)}, f32[576,768,1]{1,0,2:T(8,128)S(1)}) fusion(f32[576,768]{1,0:T(8,128)S(1)} %copy-done.2, f32[576]{0:T(1024)S(1)} %add_rsqrt_fusion, f32[576]{0:T(1024)S(1)} %broadcast_multiply_fusion.4, f32[768]{0:T(1024)S(1)} %copy-done.37, ...), kind=kOutput, calls=%fused_computation.88 | convolution fusion | flops 2721887744 | bytes 11814912 | tf_op jit(solution)/shard_map/grc,gdc->rd/dot_general | solution.py:163
  212.2 11.2 %multiply_reduce_fusion = (f32[4,3,576]{2,1,0:T(4,128)S(1)}, f32[4,3,576,576]{2,3,1,0:T(8,128)}) fusion(f32[4,3,576,576]{2,3,1,0:T(8,128)} %get-tuple-element.234, f32[4,3,576]{2,1,0:T(4,128)S(1)} %get-tuple-element.233, bf16[4,576,3,64]{1,3,2,0:T(8,128)(2,1)S(1)} %bitcast.303, f32[4,576,3,64]{1,3,2,0:T(8,128)S(1)} %bitcast.289, f32[4,3,64]{2,1,0:T(4,128)S(1)} %copy-done.41), kind=kOutput, calls=%fused_computation.2 | convolution fusion | flops 522429696 | bytes 34563072 | tf_op jit(solution)/shard_map/gsqhe,gskhe->gshqk/dot_general | solution.py:170
  223.3 12.3 %multiply_convert_fusion = bf16[4,3,576,576]{2,3,1,0:T(8,128)(2,1)S(1)} fusion(f32[4,3,576,576]{2,3,1,0:T(8,128)} %get-tuple-element.241, f32[4,3,576]{2,1,0:T(4,128)S(1)} %get-tuple-element.240, f32[4,3,576,576]{2,3,1,0:T(8,128)} %get-tuple-element.234, f32[4,3,576]{2,1,0:T(4,128)S(1)} %get-tuple-element.233), kind=kLoop, calls=%fused_computation.1 | loop fusion | flops 15925248 | bytes 39868416 | tf_op jit(solution)/shard_map/convert_element_type | solution.py:172
  241.1 8.8 %convert_reduce_fusion.2 = (f32[4,3,64]{2,1,0:T(4,128)S(1)}, bf16[4,3,64,576]{3,2,1,0:T(8,128)(2,1)S(1)}) fusion(bf16[4,576,3,64]{1,3,2,0:T(8,128)(2,1)S(1)} %bitcast.304, f32[4,3,576,576]{2,3,1,0:T(8,128)} %get-tuple-element.234, f32[4,3,576]{2,1,0:T(4,128)S(1)} %get-tuple-element.233), kind=kOutput, calls=%fused_computation.56 | convolution fusion | flops 518896896 | bytes 17725440 | tf_op jit(solution)/shard_map/gshqk,gsqhe->gskhe/dot_general | solution.py:169
  255.3 6.6 %concatenate.50 = bf16[4,576,768]{2,1,0:T(8,128)(2,1)} concatenate(bf16[4,576,128]{2,1,0:T(8,128)(2,1)S(1)} %copy.233, bf16[4,576,128]{2,1,0:T(8,128)(2,1)S(1)} %copy.234, bf16[4,576,128]{2,1,0:T(8,128)(2,1)S(1)} %copy.235, bf16[4,576,64]{2,1,0:T(8,128)(2,1)S(1)} %copy.236, bf16[4,576,64]{2,1,0:T(8,128)(2,1)S(1)} %broadcast_in_dim.16, bf16[4,576,64]{2,1,0:T(8,128)(2,1)} %copy.237, ...), dimensions={2} | concatenate | bytes 7077888 | tf_op jit(solution)/shard_map/concatenate | solution.py:180
  261.9 7.0 %fusion.38 = (f32[768]{0:T(1024)S(1)}, f32[576]{0:T(1024)S(1)}, f32[576]{0:T(1024)S(1)}, f32[768]{0:T(1024)S(1)}, f32[576,768,1]{1,0,2:T(8,128)S(1)}) fusion(f32[576]{0:T(1024)S(1)} %copy-done.34, f32[576]{0:T(1024)S(1)} %copy-done.32, bf16[4,576,768]{2,1,0:T(8,128)(2,1)} %param.21, s32[]{:T(128)S(6)} %select_n.16, f32[768]{0:T(1024)S(1)} %copy-done.36, ...), kind=kOutput, calls=%fused_computation.71 | convolution fusion | flops 2722330112 | bytes 10930180 | tf_op jit(solution)/shard_map/grc,gdc->rd/dot_general | solution.py:193
  276.2 5.7 %convolution_convert_fusion = bf16[4,768,768]{1,2,0:T(8,128)(2,1)S(1)} fusion(bf16[4,576,768]{2,1,0:T(8,128)(2,1)S(1)} %copy-done.55, f32[576]{0:T(1024)S(1)} %get-tuple-element.251, bf16[4,576,768]{2,1,0:T(8,128)(2,1)} %param.22, s32[]{:T(128)S(6)} %select_n.16), kind=kOutput, calls=%fused_computation.39 | convolution fusion | flops 2721595392 | bytes 9144580 | tf_op jit(solution)/shard_map/rd,grc->gdc/dot_general | solution.py:158
  282.0 4.4 convolution_convert_fusion.1
  286.4 6.1 %fusion.2 = bf16[4,768,768]{2,1,0:T(8,128)(2,1)S(1)} fusion(f32[4,768,384]{2,1,0:T(8,128)S(1)} %select_maximum_fusion, bf16[4,576,768]{2,1,0:T(8,128)(2,1)S(1)} %copy-done.7, f32[768]{0:T(1024)S(1)} %copy-done.47, f32[768]{0:T(1024)S(1)} %copy-done.36, f32[576]{0:T(1024)S(1)} %copy-done.34, f32[576]{0:T(1024)S(1)} %copy-done.32, ...), kind=kOutput, calls=%fused_computation.9 | convolution fusion | flops 2725281792 | bytes 13871620 | tf_op jit(solution)/shard_map/rd,grc->gdc/dot_general | solution.py:187
  292.6 5.9 %pad_maximum_fusion = bf16[3,32,96,768]{3,2,0,1:T(8,128)(2,1)} fusion(bf16[1,32,96,768]{3,2,0,1:T(8,128)(2,1)S(1)} %bitcast.279, bf16[1,32,96,768]{3,2,0,1:T(8,128)(2,1)S(1)} %bitcast.280, bf16[1,32,96,768]{3,2,0,1:T(8,128)(2,1)S(1)} %bitcast.281), kind=kLoop, calls=%fused_computation.5 | loop fusion | flops 14155776 | bytes 28311552 | tf_op jit(solution)/shard_map/stack | solution.py:200
  300.2 42.3 %psum.7 = f32[12,768]{1,0:T(8,128)S(1)} all-reduce(f32[12,768]{1,0:T(8,128)S(1)} %concatenate.56), channel_id=1, replica_groups=mesh['dp'=8,'tensor'=4] {'tensor','dp'}, use_global_device_ids=true, to_apply=%region_21.22 | all-reduce | flops 9216 | bytes 73728 | tf_op jit(solution)/shard_map/psum | solution.py:217
  343.9 5.6 %convert.24 = f32[4,576,768]{2,1,0:T(8,128)} convert(bf16[4,576,768]{2,1,0:T(8,128)(2,1)} %bitcast.287) | non-fusion elementwise | flops 1769472 | bytes 10616832 | tf_op jit(solution)/shard_map/convert_element_type | solution.py:198
  349.5 159.1 %reduce-scatter.2.cloned.1.call-done = bf16[3,1,96,768]{3,2,0,1:T(8,128)(2,1)} async-done(((bf16[3,32,96,768]{3,2,0,1:T(8,128)(2,1)}), bf16[3,1,96,768]{3,2,0,1:T(8,128)(2,1)}) %reduce-scatter.2.cloned.1.call-update) | async-done | bytes 442384 | tf_op jit(solution)/shard_map/reduce_scatter | solution.py:202
  (246 shorter events, 91.5 us)
Async XLA Ops:
  7.2 126.9 %all-gather.8.cloned.1.call-start = ((), (), s32[]{:S(2)}) async-start(), calls=%async_computation.1 | async-start | bytes 14598144 | tf_op jit(solution)/shard_map/all_gather | solution.py:109
  11.3 85.9 %copy-start.8 = (bf16[4,576,768]{2,1,0:T(8,128)(2,1)S(1)}, bf16[4,576,768]{2,1,0:T(8,128)(2,1)}, u32[]{:S(2)}) copy-start(bf16[4,576,768]{2,1,0:T(8,128)(2,1)} %param.21) | copy-start | bytes 10616836
  27.8 316.2 %all-gather.10.cloned.1.call-start = ((), (), s32[]{:S(2)}) async-start(), calls=%async_computation.3 | async-start | bytes 4423680 | tf_op jit(solution)/shard_map/all_gather | solution.py:154
  100.2 43.4 %copy-start.35 = (f32[768]{0:T(1024)}, f32[768]{0:T(1024)S(1)}, u32[]{:S(2)}) copy-start(f32[768]{0:T(1024)S(1)} %get-tuple-element.169) | copy-start | bytes 9220
  100.2 43.4 %copy-start.31 = (f32[576]{0:T(1024)}, f32[576]{0:T(1024)S(1)}, u32[]{:S(2)}) copy-start(f32[576]{0:T(1024)S(1)} %broadcast_multiply_fusion.5) | copy-start | bytes 6916
  100.6 43.0 %copy-start.33 = (f32[576]{0:T(1024)}, f32[576]{0:T(1024)S(1)}, u32[]{:S(2)}) copy-start(f32[576]{0:T(1024)S(1)} %add_rsqrt_fusion.1) | copy-start | bytes 6916
  134.1 9.5 %copy-start.46 = (f32[768]{0:T(1024)S(1)}, f32[768]{0:T(1024)}, u32[]{:S(2)}) copy-start(f32[768]{0:T(1024)} %get-tuple-element.168) | copy-start | bytes 9220
  156.1 10.3 %copy-start.41 = (f32[4,3,64]{2,1,0:T(4,128)S(1)}, f32[4,3,64]{2,1,0:T(4,128)}, u32[]{:S(2)}) copy-start(f32[4,3,64]{2,1,0:T(4,128)} %add.243) | copy-start | bytes 9220
  166.5 8.6 %copy-start.15 = (bf16[4,768,64]{2,1,0:T(8,128)(2,1)S(1)}, bf16[4,768,64]{2,1,0:T(8,128)(2,1)}, u32[]{:S(2)}) copy-start(bf16[4,768,64]{2,1,0:T(8,128)(2,1)} %get-tuple-element.205) | copy-start | bytes 1179652
  166.5 8.6 %copy-start.17 = (bf16[4,768,64]{2,1,0:T(8,128)(2,1)S(1)}, bf16[4,768,64]{2,1,0:T(8,128)(2,1)}, u32[]{:S(2)}) copy-start(bf16[4,768,64]{2,1,0:T(8,128)(2,1)} %get-tuple-element.206) | copy-start | bytes 1179652
  166.5 8.6 %copy-start.19 = (bf16[4,768,64]{2,1,0:T(8,128)(2,1)S(1)}, bf16[4,768,64]{2,1,0:T(8,128)(2,1)}, u32[]{:S(2)}) copy-start(bf16[4,768,64]{2,1,0:T(8,128)(2,1)} %get-tuple-element.207) | copy-start | bytes 1179652
  166.5 8.6 %copy-start.50 = (f32[768]{0:T(1024)S(1)}, f32[768]{0:T(1024)}, u32[]{:S(2)}) copy-start(f32[768]{0:T(1024)} %get-tuple-element.167) | copy-start | bytes 9220
  175.1 13.2 %slice-start = ((s8[4718592]{0:T(1024)(128)(4,1)}), s8[4194304]{0:T(1024)(128)(4,1)S(1)}, s32[]{:S(2)}) async-start(s8[4718592]{0:T(1024)(128)(4,1)} %bitcast.276), calls=%async_computation.5 | async-start | bytes 8388608
  179.0 9.4 %slice-start.1 = ((s8[4718592]{0:T(1024)(128)(4,1)}), s8[524288]{0:T(1024)(128)(4,1)S(1)}, s32[]{:S(2)}) async-start(s8[4718592]{0:T(1024)(128)(4,1)} %bitcast.276), calls=%async_computation.6 | async-start | bytes 1048576
  179.0 9.4 %copy-start.49 = (f32[768]{0:T(1024)S(1)}, f32[768]{0:T(1024)}, u32[]{:S(2)}) copy-start(f32[768]{0:T(1024)} %get-tuple-element.164) | copy-start | bytes 9220
  192.3 151.6 %all-gather.12.cloned.1.call-start = ((), (), s32[]{:S(2)}) async-start(), calls=%async_computation.4 | async-start | bytes 4423680 | tf_op jit(solution)/shard_map/all_gather | solution.py:198
  192.3 8.5 %copy-start.2 = (f32[576,768]{1,0:T(8,128)S(1)}, f32[576,768]{1,0:T(8,128)}, u32[]{:S(2)}) copy-start(f32[576,768]{1,0:T(8,128)} %copy-done.1) | copy-start | bytes 5308420
  271.9 236.6 %reduce-scatter.2.cloned.1.call-start = ((), (), s32[]{:S(2)}) async-start(), calls=%async_computation.2 | async-start | bytes 14598144 | tf_op jit(solution)/shard_map/reduce_scatter | solution.py:202
  298.5 44.0 %copy-start.38 = (f32[6,96]{1,0:T(8,128)S(1)}, f32[6,96]{1,0:T(8,128)}, u32[]{:S(2)}) copy-start(f32[6,96]{1,0:T(8,128)} %param.36) | copy-start | bytes 6916
  298.5 44.0 %copy-start.42 = (f32[6,96]{1,0:T(8,128)S(1)}, f32[6,96]{1,0:T(8,128)}, u32[]{:S(2)}) copy-start(f32[6,96]{1,0:T(8,128)} %param.37) | copy-start | bytes 6916
  298.5 44.0 %copy-start.43 = (f32[6,96]{1,0:T(8,128)S(1)}, f32[6,96]{1,0:T(8,128)}, u32[]{:S(2)}) copy-start(f32[6,96]{1,0:T(8,128)} %param.38) | copy-start | bytes 6916
  298.5 44.7 %copy-start.39 = (f32[6,24]{1,0:T(8,128)S(1)}, f32[6,24]{1,0:T(8,128)}, u32[]{:S(2)}) copy-start(f32[6,24]{1,0:T(8,128)} %param.39) | copy-start | bytes 1732
  298.5 44.7 %copy-start.44 = (f32[6,24]{1,0:T(8,128)S(1)}, f32[6,24]{1,0:T(8,128)}, u32[]{:S(2)}) copy-start(f32[6,24]{1,0:T(8,128)} %param.40) | copy-start | bytes 1732
  298.5 44.7 %copy-start.45 = (f32[6,24]{1,0:T(8,128)S(1)}, f32[6,24]{1,0:T(8,128)}, u32[]{:S(2)}) copy-start(f32[6,24]{1,0:T(8,128)} %param.41) | copy-start | bytes 1732
  (40 other events, 162.4 us)
Sparse Core Ops, SparseCore 0:
  27.9 106.1 all-gather.7
  192.4 68.1 all-gather.9
  272.0 69.2 all-gather.11
  347.1 161.3 reduce-scatter.1

commit v2 on v1

v2 whole, which is shorter than its diff:
```python
import functools

import jax
import jax.numpy as jnp
from jax import lax
from jax.experimental import pallas as pl
from jax.experimental.pallas import tpu as pltpu
from jax.sharding import PartitionSpec as P

D = 768
FF = 3072
HEAD_DIM = 64
LEN = 576
STEP = 10


LN_EPS = 1e-05
MASK_FILL = -1e30
BETA_ONE = 0.5
BETA_TWO = 0.5
ADAM_EPS = 1e-08
MATRIX_DECAY = 0.01
SQRT_HALF = 0.7071067811865476
INV_ROOT_TAU = 0.3989422804014327
AXES = ("tensor", "dp")
MESH = pl.DeviceIdType.MESH
bf16, f32 = jnp.bfloat16, jnp.float32
NN = (((1,), (0,)), ((), ()))
NT = (((1,), (1,)), ((), ()))
RT = 192
RL = 96


def kind_rates():
    return (
        0.7 * D ** (-0.5),
        0.7 * (D * 16 // LEN) ** (-0.5),
        0.7 * D ** (-0.5),
        0.7 * FF ** (-0.5),
        0.6,
        0.4,
    )


def adamw(master, first, second, gradient, step_rate, decay_rate):
    first_new = BETA_ONE * first + (1.0 - BETA_ONE) * gradient
    second_new = BETA_TWO * second + (1.0 - BETA_TWO) * gradient * gradient
    first_hat = first_new / (1.0 - BETA_ONE**STEP)
    second_hat = second_new / (1.0 - BETA_TWO**STEP)
    master_new = master - step_rate * (
        first_hat / (jnp.sqrt(second_hat) + ADAM_EPS) + decay_rate * master
    )
    return (master_new, master_new.astype(jnp.bfloat16), first_new, second_new)


def flip(index, bit):
    return index + bit - 2 * bit * lax.rem(lax.div(index, bit), 2)

def send(src, dst, ssem, rsem, to):
    return pltpu.make_async_remote_copy(
        src_ref=src, dst_ref=dst, send_sem=ssem, recv_sem=rsem, device_id=to, device_id_type=MESH
    )

def arrived(dst, sem):
    pltpu.make_async_copy(dst, dst, sem).wait()

def gather_kernel(rows_of, own, *refs):
    nb = len(rows_of)
    outs = refs[:nb]
    lsem, zs, zr, ps, pr, ds, dr, cs, cr = refs[nb:]
    z, me = lax.axis_index("tensor"), lax.axis_index("dp")
    nz = lax.axis_size("tensor")
    cp, xp, yp = flip(me, 1), flip(me, 2), flip(me, 4)
    dg = flip(xp, 4)
    pair = (xp, yp)
    bar = pltpu.get_barrier_semaphore()
    for d in (cp, xp, yp):
        pl.semaphore_signal(bar, inc=1, device_id=(d, z), device_id_type=MESH)
    @pl.when(z > 0)
    def _():
        pl.semaphore_signal(bar, inc=1, device_id=(me, z - 1), device_id_type=MESH)
    @pl.when(z < nz - 1)
    def _():
        pl.semaphore_signal(bar, inc=1, device_id=(me, z + 1), device_id_type=MESH)
    edges = jnp.where(z > 0, 1, 0) + jnp.where(z < nz - 1, 1, 0)
    pl.semaphore_wait(bar, 3 + edges)

    starts = [sum(rows_of[:b]) for b in range(nb)]
    def own_ref(b):
        return own.at[pl.ds(starts[b], rows_of[b])]
    def right(b, s, src):
        return send(src, outs[b].at[s, me], zs.at[b, 0, z - s], zr.at[b, s], (me, z + 1))
    def left(b, s, src):
        return send(src, outs[b].at[s, me], zs.at[b, 1, s - z], zr.at[b, s], (me, z - 1))
    def side(b, s, src, k):
        return send(src, outs[b].at[s, me], ps.at[b, k, s], pr.at[b, k, s], (pair[k], z))
    def spread(b, s, src):
        for k in range(2):
            side(b, s, src, k).start()
    half = [[(0, r//32*16), (r//32*16, r - r//32*16)] for r in rows_of]
    def diag(b, k):
        lo, n = half[b][k]
        part = outs[b].at[:, pair[k], pl.ds(lo, n)]
        return send(part, part, ds.at[b, k], dr.at[b, k], (pair[1 - k], z))
    def twin(b, j):
        part = outs[b].at[:, (me, xp, yp, dg)[j]]
        return send(part, part, cs.at[b, j], cr.at[b, j], (cp, z))
    keep = [pltpu.make_async_copy(own_ref(b), outs[b].at[z, me], lsem.at[b]) for b in range(nb)]

    def open_block(b):
        @pl.when(z < nz - 1)
        def _():
            right(b, z, own_ref(b)).start()
        @pl.when(z > 0)
        def _():
            left(b, z, own_ref(b)).start()
        spread(b, z, own_ref(b))
        keep[b].start()

    def hop(b, t):
        @pl.when(z >= t)
        def _():
            s = z - t
            arrived(outs[b].at[s, me], zr.at[b, s])
            @pl.when(z < nz - 1)
            def _():
                right(b, s, outs[b].at[s, me]).start()
            spread(b, s, outs[b].at[s, me])
        @pl.when(z + t < nz)
        def _():
            s = z + t
            arrived(outs[b].at[s, me], zr.at[b, s])
            @pl.when(z > 0)
            def _():
                left(b, s, outs[b].at[s, me]).start()
            spread(b, s, outs[b].at[s, me])
    def twin_own(b):
        keep[b].wait()
        twin(b, 0).start()
    def square(b):
        for k in range(2):
            for s in range(4):
                arrived(outs[b].at[s, pair[k]], pr.at[b, k, s])
            diag(b, k).start()
            twin(b, 1 + k).start()
    def corner(b):
        for k in range(2):
            lo, n = half[b][k]
            arrived(outs[b].at[:, dg, pl.ds(lo, n)], dr.at[b, k])
        twin(b, 3).start()
    def finish(b):
        for j, d in enumerate((cp, flip(xp, 1), flip(yp, 1), flip(dg, 1))):
            arrived(outs[b].at[:, d], cr.at[b, j])
    for b in range(nb):
        open_block(b)
    for t in (1, 2, 3):
        for b in range(nb):
            hop(b, t)
    for step in (twin_own, square, corner):
        for b in range(nb):
            step(b)
    for b in range(nb):
        finish(b)
    for b in range(nb):
        for t in range(4):
            @pl.when((z < nz - 1) & (z >= t))
            def _():
                right(b, z - t, outs[b].at[z - t, me]).wait_send()
            @pl.when((z > 0) & (z + t < nz))
            def _():
                left(b, z + t, outs[b].at[z + t, me]).wait_send()
            for k in range(2):
                side(b, t, outs[b].at[t, me], k).wait_send()
            twin(b, t).wait_send()
        for k in range(2):
            diag(b, k).wait_send()

def gather(own, rows_of, cid=1):
    nb = len(rows_of)
    S = pltpu.SemaphoreType.DMA
    return pl.pallas_call(
        functools.partial(gather_kernel, rows_of),
        out_shape=[jax.ShapeDtypeStruct((4, 8, r, D), jnp.bfloat16) for r in rows_of],
        in_specs=[pl.BlockSpec(memory_space=pltpu.VMEM)],
        out_specs=[pl.BlockSpec(memory_space=pl.ANY)] * nb,
        scratch_shapes=[S((nb,)), S((nb, 2, 4)), S((nb, 4)), S((nb, 2, 4)), S((nb, 2, 4)), S((nb, 2)), S((nb, 2)), S((nb, 4)), S((nb, 4))],
        compiler_params=pltpu.CompilerParams(collective_id=cid, has_side_effects=True),
    )(own)


def mm(a, b, dims=NN):
    return lax.dot_general(a, b, dims, preferred_element_type=f32)

def normal_of(rows):
    mean = jnp.mean(rows, axis=-1, keepdims=True)
    centred = rows - mean
    inverse = lax.rsqrt(jnp.mean(centred * centred, axis=-1, keepdims=True) + LN_EPS)
    return centred * inverse, inverse

def normal_back(grad, normal, inverse, gain):
    scaled = grad * gain
    return inverse * (
        scaled
        - jnp.mean(scaled, axis=-1, keepdims=True)
        - normal * jnp.mean(scaled * normal, axis=-1, keepdims=True)
    )

def row_tiles(size):
    return range(0, LEN, size)

def colsum(v):
    return jnp.sum(v, axis=0, keepdims=True)

def compute_kernel(x, cot, valid_col, keybias, vecs, bias, A, B, C,
                   mixed, ig, gA, gB, gC, vsum, bsum,
                   first_in, second_in, gout_low, gm_low, fT, sT, goT, gmT,
                   qkv, probs, att, middle, acc, acc2, gm, stage, sems):
    for r in row_tiles(RL):
        rs = pl.ds(r, RL)
        n, _ = normal_of(x[rs].astype(f32))
        first_in[rs] = (n * vecs[0:1] + vecs[1:2]).astype(bf16)
        go = cot[rs].astype(f32) * valid_col[rs]
        gout_low[rs] = go.astype(bf16)
    fT[...] = first_in[...].T
    goT[...] = gout_low[...].T
    lane = lax.broadcasted_iota(jnp.int32, (1, 128), 1)
    low = lane < 64
    acc[...] = jnp.zeros_like(acc)

    def forward(g, carry):
        w = A.at[g]
        for r in row_tiles(RT):
            rs = pl.ds(r, RT)
            p = mm(first_in[rs], w[...]) + bias[0, g]
            qkv[g, rs] = p.astype(bf16)
        def tile(i):
            return qkv[g, :, 128 * i : 128 * i + 128]
        outs = []
        for h in range(3):
            q, k, v = (tile(0), tile(1), tile(2)) if h < 2 else (tile(3), tile(4), tile(3))
            q = jnp.where(low if h != 1 else ~low, q, 0) * bf16(0.125)
            vt = v.T
            vt = vt[64:] if h else vt[:64]
            cols = []
            for r in row_tiles(RT):
                s = mm(k, q[r : r + RT], NT) + keybias[...]
                top = jnp.max(s, axis=0, keepdims=True)
                e = jnp.exp(s - top)
                p = (e * (1.0 / jnp.sum(e, axis=0, keepdims=True))).astype(bf16)
                probs[g, h, r // RT] = p
                cols.append(mm(vt, p))
            outs.append(jnp.concatenate(cols, axis=1))
        att[g, :, 128:256] = jnp.concatenate(outs[:2], axis=0).T.astype(bf16)
        att[g, :, 0:128] = jnp.concatenate([jnp.zeros_like(outs[2]), outs[2]], axis=0).T.astype(bf16)
        for r in row_tiles(RT):
            rs = pl.ds(r, RT)
            acc[rs] += mm(att[g, rs], w[:, 512:768], NT)
        return carry
    lax.fori_loop(0, 4, forward, 0)

    for r in row_tiles(RL):
        rs = pl.ds(r, RL)
        m = x[rs].astype(f32) + acc[rs] + vecs[2:3]
        middle[rs] = m
        n, _ = normal_of(m)
        second_in[rs] = (n * vecs[3:4] + vecs[4:5]).astype(bf16)
    sT[...] = second_in[...].T
    acc[...] = jnp.zeros_like(acc)
    acc2[...] = jnp.zeros_like(acc2)

    def put(dst, g, slot, compute):
        @pl.when(g > 0)
        def _():
            pltpu.make_async_copy(stage.at[slot], dst.at[g - 1], sems.at[slot]).wait()
        for c in range(0, D, 256):
            stage[slot, pl.ds(c, 256)] = compute(c).astype(bf16)
        pltpu.make_async_copy(stage.at[slot], dst.at[g], sems.at[slot]).start()
    def drain(dst, slot):
        pltpu.make_async_copy(stage.at[slot], dst.at[3], sems.at[slot]).wait()

    def mlp(g, carry):
        hid, gps = [], []
        for r in row_tiles(RT):
            rs = pl.ds(r, RT)
            u = mm(second_in[rs], B[g]) + bias[1, g]
            phi = 0.5 * (1.0 + lax.erf(u * SQRT_HALF))
            hidden = (u * phi).astype(bf16)
            slope = phi + u * jnp.exp(-0.5 * u * u) * INV_ROOT_TAU
            gp = (mm(gout_low[rs], C[g]) * slope).astype(bf16)
            acc[rs] += mm(hidden, C[g], NT)
            acc2[rs] += mm(gp, B[g], NT)
            hid.append(hidden)
            gps.append(gp)
        hid = jnp.concatenate(hid, axis=0)
        gps = jnp.concatenate(gps, axis=0)
        bsum[1, g] = colsum(gps.astype(f32))
        put(gC, g, 0, lambda c: mm(goT[pl.ds(c, 256)], hid))
        put(gB, g, 1, lambda c: mm(sT[pl.ds(c, 256)], gps))
        return carry
    lax.fori_loop(0, 4, mlp, 0)
    drain(gC, 0)
    drain(gB, 1)

    sums = [jnp.zeros((1, D), f32) for _ in range(6)]
    for r in row_tiles(RL):
        rs = pl.ds(r, RL)
        m = middle[rs]
        mixed[rs] = ((m + acc[rs] + vecs[5:6]) * valid_col[rs]).astype(bf16)
        n, inv = normal_of(m)
        gn = acc2[rs]
        go = gout_low[rs].astype(f32)
        t = go + normal_back(gn, n, inv, vecs[3:4])
        gm[rs] = t
        gm_low[rs] = t.astype(bf16)
        sums[2] += colsum(t)
        sums[3] += colsum(gn * n)
        sums[4] += colsum(gn)
        sums[5] += colsum(go)
    gmT[...] = gm_low[...].T
    acc[...] = jnp.zeros_like(acc)

    def backward(g, carry):
        w = A.at[g]
        ga = mm(gm_low[...], w[:, 512:768]).astype(bf16)
        def tile(i):
            return qkv[g, :, 128 * i : 128 * i + 128]
        dq, dk, dv = [], [], []
        for h in range(3):
            q, k, v = (tile(0), tile(1), tile(2)) if h < 2 else (tile(3), tile(4), tile(3))
            gt = ga[:, 128:256] if h < 2 else ga[:, 0:128]
            gmask = jnp.where(low if h == 0 else ~low, gt, 0)
            kt = k.T
            kt = kt[64:] if h == 1 else kt[:64]
            dqs, dks, dvs = [], 0.0, 0.0
            for r in row_tiles(RT):
                p = probs[g, h, r // RT]
                dp = mm(v, gmask[r : r + RT], NT)
                pf = p.astype(f32)
                inner = jnp.sum(pf * dp, axis=0, keepdims=True)
                ds = (pf * (dp - inner)).astype(bf16)
                dqs.append(mm(kt, ds))
                dks = dks + mm(ds, q[r : r + RT])
                dvs = dvs + mm(p, gt[r : r + RT])
            dq.append(jnp.concatenate(dqs, axis=1))
            dk.append(dks * 0.125)
            dv.append(dvs)
        dq01 = jnp.concatenate(dq[:2], axis=0).T * 0.125
        dq2 = jnp.concatenate([dq[2], jnp.zeros_like(dq[2])], axis=0).T * 0.125
        parts = [
            dq01,
            jnp.where(low, dk[0], dk[1]),
            jnp.where(low, dv[0], dv[1]),
            jnp.where(low, dq2, dv[2]),
            jnp.where(low, dk[2], 0.0),
        ]
        for i, part in enumerate(parts):
            part = part.astype(bf16)
            qkv[g, :, 128 * i : 128 * i + 128] = part
            bsum[0, g, :, 128 * i : 128 * i + 128] = colsum(part.astype(f32))
        qkv[g, :, 640:768] = jnp.zeros((LEN, 128), bf16)
        bsum[0, g, :, 640:768] = jnp.zeros((1, 128), f32)
        for r in row_tiles(RT):
            rs = pl.ds(r, RT)
            acc[rs] += mm(qkv[g, rs], w[...], NT)
        def grad(c):
            left = mm(fT[pl.ds(c, 256)], qkv[g])
            right = mm(gmT[pl.ds(c, 256)], att[g])
            return jnp.concatenate([left[:, :512], left[:, 512:] + right], axis=1)
        put(gA, g, 0, grad)
        return carry
    lax.fori_loop(0, 4, backward, 0)
    drain(gA, 0)

    for r in row_tiles(RL):
        rs = pl.ds(r, RL)
        n, inv = normal_of(x[rs].astype(f32))
        gn = acc[rs]
        ig[rs] = (gm[rs] + normal_back(gn, n, inv, vecs[0:1])).astype(bf16)
        sums[0] += colsum(gn * n)
        sums[1] += colsum(gn)
    for i in range(6):
        vsum[i : i + 1] = sums[i]

def compute(x, cot, valid_col, keybias, vecs, bias, A, B, C):
    V = pltpu.VMEM
    vm = pl.BlockSpec(memory_space=V)
    hb = pl.BlockSpec(memory_space=pl.ANY)
    S = jax.ShapeDtypeStruct
    return pl.pallas_call(
        compute_kernel,
        out_shape=[S((LEN, D), bf16), S((LEN, D), bf16)] + [S((4, D, D), bf16)] * 3 + [S((6, D), f32), S((2, 4, 1, D), f32)],
        in_specs=[vm] * 9,
        out_specs=[vm, vm, hb, hb, hb, vm, vm],
        scratch_shapes=[V((LEN, D), bf16)] * 4 + [V((D, LEN), bf16)] * 4 + [
            V((4, LEN, D), bf16), V((4, 3, 3, LEN, RT), bf16), V((4, LEN, 256), bf16),
            V((LEN, D), f32), V((LEN, D), f32), V((LEN, D), f32), V((LEN, D), f32),
            V((2, D, D), bf16), pltpu.SemaphoreType.DMA((2,)),
        ],
        compiler_params=pltpu.CompilerParams(vmem_limit_bytes=63 * 1024 * 1024),
        cost_estimate=pl.CostEstimate(flops=57_000_000_000, bytes_accessed=32_000_000, transcendentals=6_000_000),
    )(x, cot, valid_col, keybias, vecs, bias, A, B, C)


def pack_attention(qkv, out):
    q, k, v = qkv[:, 0], qkv[:, 1], qkv[:, 2]
    return jnp.concatenate(
        [
            q[:, :128], k[:, :128], v[:, :128],
            q[:, 128:], v[:, 128:], k[:, 128:], out[:, 128:], out[:, :128],
        ],
        axis=1,
    )


def unpack_attention(block):
    pair = [block[:, 128 * i : 128 * i + 128] for i in range(6)]
    q = jnp.concatenate([pair[0], pair[3][:, :64]], axis=1)
    k = jnp.concatenate([pair[1], pair[4][:, :64]], axis=1)
    v = jnp.concatenate([pair[2], pair[3][:, 64:]], axis=1)
    o = jnp.concatenate([pair[5], pair[4][:, 64:]], axis=1)
    return jnp.stack([q, k, v], axis=1), o


def local(tokens, cotangent, counts, *state):
    masters, firsts, seconds = state[0::3], state[1::3], state[2::3]
    qkv_master, out_master, up_master, down_master, shared_master, split_master = masters
    groups = lax.axis_size("tensor")
    copies = lax.axis_size("dp")
    seq_count, length, width = tokens.shape
    share = seq_count // groups
    mine = lax.axis_index("tensor") * share
    band = qkv_master.shape[0]
    thin = split_master.shape[1]

    attn_own = pack_attention(qkv_master.astype(bf16), out_master.astype(bf16).T)
    up_own = up_master.astype(bf16).reshape(band, -1)
    down_own = down_master.astype(bf16).reshape(-1, band).T
    vec_own = jnp.zeros((16, width), bf16)
    vec_own = vec_own.at[:6, :band].set(shared_master.astype(bf16))
    vec_own = vec_own.at[:6, 128 : 128 + thin].set(split_master.astype(bf16))
    own = jnp.concatenate([attn_own, vec_own, up_own, down_own])
    sizes = (band + 16, band, band)
    if (groups, copies) == (4, 8):
        mats = gather(own, sizes)
    else:
        whole = lax.all_gather(own, AXES).reshape(groups, copies, -1, width)
        ends = [0, sizes[0], sizes[0] + sizes[1], sum(sizes)]
        mats = [whole[:, :, ends[i] : ends[i + 1]] for i in range(3)]
    attn_all, up_all, down_all = mats
    vec_all = attn_all[:, :, band:].astype(f32)
    attn_all, up_all, down_all = (
        t[:, :, :band].reshape(groups, width, width) for t in (attn_all, up_all, down_all)
    )
    shared_vecs = jnp.swapaxes(vec_all[0, :, :6, :band], 0, 1).reshape(6, width)
    split_vecs = vec_all[:, :, :6, 128 : 128 + thin].reshape(groups, copies, 6, thin)
    split_vecs = jnp.swapaxes(split_vecs, 1, 2).reshape(groups, 6, copies * thin)
    bq, bv = split_vecs[:, 0], split_vecs[:, 1]
    zero = jnp.zeros((groups, 128), f32)
    attn_bias = jnp.concatenate(
        [bq[:, :128], zero, bv[:, :128], bq[:, 128:], bv[:, 128:], zero, zero], axis=1
    )
    up_bias = split_vecs[:, 2:].reshape(groups, width)
    bias = jnp.stack([attn_bias, up_bias]).reshape(2, groups, 1, width)

    x = lax.dynamic_slice_in_dim(tokens, mine, share, 0).reshape(length, width)
    cot = lax.dynamic_slice_in_dim(cotangent, mine, share, 0).reshape(length, width)
    count = lax.dynamic_slice_in_dim(counts, mine, share, 0)
    valid = lax.broadcasted_iota(jnp.int32, (length, 1), 0) < count
    mixed, grad_inputs, grad_attn, grad_up, grad_down, shared_grad, split_grad = compute(
        x, cot, valid.astype(f32), jnp.where(valid, 0.0, MASK_FILL), shared_vecs, bias,
        attn_all, up_all, down_all,
    )
    mixed = lax.all_gather(mixed[None], "tensor", axis=0, tiled=True)
    grad_inputs = lax.all_gather(grad_inputs[None], "tensor", axis=0, tiled=True).astype(f32)

    grads = jnp.stack([grad_attn, grad_up, grad_down])
    grads = grads.reshape(3, groups * copies, band, width)
    grads = lax.psum_scatter(grads, AXES, scatter_dimension=1, tiled=False).astype(f32)
    cols = split_grad.reshape(2, groups, width)
    grad_bq = jnp.concatenate([cols[0, :, :128], cols[0, :, 384:448]], axis=1).reshape(1, width)
    grad_bv = jnp.concatenate([cols[0, :, 256:384], cols[0, :, 448:512]], axis=1).reshape(1, width)
    grad_bu = jnp.swapaxes(cols[1].reshape(groups, -1, width // groups), 0, 1).reshape(-1, width)
    vec_sum = lax.psum(jnp.concatenate([shared_grad, grad_bq, grad_bv, grad_bu]), AXES)
    at = lax.axis_index("dp")
    shared_sum = lax.dynamic_slice_in_dim(vec_sum[:6], at * band, band, 1)
    split_at = (lax.axis_index("tensor") * copies + at) * thin
    split_sum = lax.dynamic_slice_in_dim(vec_sum[6:], split_at, thin, 1)

    sum_qkv, sum_out = unpack_attention(grads[0])
    summed = (
        sum_qkv,
        sum_out.T,
        grads[1].reshape(up_master.shape),
        grads[2].T.reshape(down_master.shape),
        shared_sum,
        split_sum,
    )
    decays = (MATRIX_DECAY, MATRIX_DECAY, MATRIX_DECAY, MATRIX_DECAY, 0.0, 0.0)
    rates = kind_rates()
    outputs = [mixed, grad_inputs]
    for kind in range(6):
        outputs.extend(
            adamw(
                masters[kind], firsts[kind], seconds[kind], summed[kind], rates[kind], decays[kind]
            )
        )
    return tuple(outputs)


def solution(mesh):
    rows = P("dp", None, None)
    state = (
        P("dp", None, "tensor"),
        P("tensor", "dp"),
        P("dp", None, "tensor"),
        P(None, "tensor", "dp"),
        P(None, "dp"),
        P(None, ("tensor", "dp")),
    )
    in_specs = (rows, rows, P("dp")) + tuple(s for s in state for _ in range(3))
    out_specs = (rows, rows) + tuple(s for s in state for _ in range(4))
    return jax.shard_map(local, mesh=mesh, in_specs=in_specs, out_specs=out_specs, check_vma=False)
```

time: 540 us -> 445 us (0.82); the launches traced: 530 us -> 444 us
  Pallas kernels: 0 us -> 167 us
  matrix products: 103 us -> 0 us
  blocking collectives: 96 us -> 44.7 us
  local copies, waits for them, and re-layouts: 69.9 us -> 24.8 us
  waiting for transfers between devices: 193 us -> 150 us
  other arithmetic: 53.1 us -> 41 us
    pallas_call x0 -> x2, Pallas kernels: none -> 167 us  [the longest x1 97 us: compute(): pl.pallas_call(compute_kernel, out_shape=[S((LEN, D), bf16), S((LEN, D),...]
    reduce_scatter x1, waiting for transfers between devices: 159 us -> 47.6 us  [local(): lax.psum_scatter(grads, AXES, scatter_dimension=1, tiled=False).astype(f32)]
    dot_general x17 -> x0, matrix products: 92.9 us -> none  [the longest x1 11.2 us: local(): jnp.einsum('gsqhe,gskhe->gshqk', grad_att, v, preferred_element_type=f32)]
    all_gather x3 -> x2, waiting for transfers between devices: 33.4 us -> 102 us  [the longest x1 89.6 us: local(): mixed = lax.all_gather(mixed[None], 'tensor', axis=0, tiled=True)]
    all_gather x2 -> x0, blocking collectives: 53.7 us -> none  [the longest x1 43.4 us: local(): lax.all_gather(split_master.astype(bf16), AXES, axis=1, tiled=True)]
    slice x19 -> x10, local copies, waits for them, and re-layouts: 21.8 us -> 5.6 us  [the longest x1 4.84 us: local(): t[:, :, :band].reshape(groups, width, width)]
    convert_element_type x5 -> x4, other arithmetic: 22.6 us -> 8.97 us  [the longest x1 5.57 us: local(): lax.all_gather(grad_inputs[None], 'tensor', axis=0, tiled=True).astype(f32)]
    concatenate x6 -> x3, local copies, waits for them, and re-layouts: 13 us -> 0.2 us  [the longest x1 0.11 us: pack_attention(): jnp.concatenate([q[:, :128], k[:, :128], v[:, :128], q[:, 128:], v[:, 128...]
  transfers between devices with their start and end apart: 4 -> 3, of which waited for: 2 -> 3; matrix products, arithmetic and copies ran while one was open for 25% -> 4% of each run, Pallas kernels for 0% -> 0%
where the time goes in v2:
time: 445 us; the launch traced here: 444 us
  Pallas kernels  167 us (38%)
  waiting for transfers between devices  150 us (34%)
  blocking collectives  44.7 us (10%)
  other arithmetic  41 us (9%)
  local copies, waits for them, and re-layouts  24.8 us (6%)
  between operations  16 us (4%)
    pallas_call x1, Pallas kernels, compute(): pl.pallas_call(compute_kernel, out_shape=[S((LEN, D), bf16), S((LEN, D),...  97 us
    all_gather x1, waiting for transfers between devices, local(): mixed = lax.all_gather(mixed[None], 'tensor', axis=0, tiled=True)  89.6 us
    pallas_call x1, Pallas kernels, gather(): pl.pallas_call(functools.partial(gather_kernel, rows_of), out_shape=[jax....  70.2 us
    reduce_scatter x1, waiting for transfers between devices, local(): lax.psum_scatter(grads, AXES, scatter_dimension=1, tiled=False).astype(f32)  47.6 us
    psum x1, blocking collectives, local(): lax.psum(jnp.concatenate([shared_grad, grad_bq, grad_bv, grad_bu]), AXES)  44.7 us
    all_gather x1, waiting for transfers between devices, local(): lax.all_gather(grad_inputs[None], 'tensor', axis=0, tiled=True).astype(f32)  12.3 us
    another operation x1, other arithmetic, local(): grads = jnp.stack([grad_attn, grad_up, grad_down])  10.8 us
  transfers between devices with their start and end apart: 3, of which 3 were waited for; matrix products, arithmetic and copies ran while one was open for 4% of the time, Pallas kernels for 0%

profile of v2, /device:TPU:0, one launch (start us, length us, event | category | flops | bytes accessed | tf_op | source)
XLA Modules:
  0.0 443.9 jit_solution(13452484268755704647)
XLA Ops:
  11.5 1.3 and_reduce_fusion
  12.8 1.0 convert_element_type.55
  13.9 1.1 convert_element_type.54
  15.2 2.7 fusion.8
  17.9 1.6 scatter.9
  20.5 70.2 %shard_map.404 = (bf16[4,8,112,768]{3,2,1,0:T(8,128)(2,1)}, bf16[4,8,96,768]{3,2,1,0:T(8,128)(2,1)}, bf16[4,8,96,768]{3,2,1,0:T(8,128)(2,1)}) custom-call(bf16[304,768]{1,0:T(8,128)(2,1)} %pad_maximum_fusion.1.own), custom_call_target="tpu_custom_call" | custom-call | tf_op jit(solution)/shard_map/pallas_call | solution.py:181
  90.7 1.3 slice_convert_fusion
  92.2 4.8 %slice.199 = bf16[4,8,96,768]{3,2,1,0:T(8,128)(2,1)} slice(bf16[4,8,112,768]{3,2,1,0:T(8,128)(2,1)} %get-tuple-element.60), slice={[0:4], [0:8], [0:96], [0:768]} | slice | bytes 9437184 | tf_op jit(solution)/shard_map/slice | solution.py:452
  97.7 1.4 fusion.3.keybias
  99.1 1.4 fusion.4.valid_col
  102.0 2.8 dynamic-slice_bitcast_fusion
  104.7 97.0 %shard_map.405 = (bf16[576,768]{1,0:T(8,128)(2,1)}, bf16[576,768]{1,0:T(8,128)(2,1)}, bf16[4,768,768]{2,1,0:T(8,128)(2,1)}, bf16[4,768,768]{2,1,0:T(8,128)(2,1)}...) custom-call(bf16[576,768]{1,0:T(8,128)(2,1)} %get-tuple-element.170.x, ...), custom_call_target="tpu_custom_call" | custom-call | flops 57000001536 | bytes 32000000 | tf_op jit(solution)/shard_map/pallas_call | solution.py:389
  202.6 10.8 %pad_maximum_fusion = bf16[3,32,96,768]{3,2,0,1:T(8,128)(2,1)} fusion(bf16[1,32,96,768]{3,2,0,1:T(8,128)(2,1)} %bitcast.86, bf16[1,32,96,768]{3,2,0,1:T(8,128)(2,1)} %bitcast.85, bf16[1,32,96,768]{3,2,0,1:T(8,128)(2,1)} %bitcast.84), kind=kLoop, calls=%fused_computation | loop fusion | flops 14155776 | bytes 28311552 | tf_op jit(solution)/shard_map/stack | solution.py:476
  214.8 44.7 %psum.7 = f32[12,768]{1,0:T(8,128)S(1)} all-reduce(f32[12,768]{1,0:T(8,128)S(1)} %pad_maximum_fusion.3), channel_id=1, replica_groups=mesh['dp'=8,'tensor'=4] {'tensor','dp'}, use_global_device_ids=true, to_apply=%region_2.3 | all-reduce | flops 9216 | bytes 73728 | tf_op jit(solution)/shard_map/psum | solution.py:483
  261.0 12.3 %all-gather.7.cloned.1.call-done = bf16[2304,768]{1,0:T(8,128)(2,1)} async-done(((bf16[576,768]{1,0:T(8,128)(2,1)}), bf16[2304,768]{1,0:T(8,128)(2,1)}) %all-gather.7.cloned.1.call-update) | async-done | bytes 3538960 | tf_op jit(solution)/shard_map/all_gather | solution.py:474
  273.3 5.6 %convert = f32[4,576,768]{2,1,0:T(8,128)} convert(bf16[4,576,768]{2,1,0:T(8,128)(2,1)} %bitcast.89) | non-fusion elementwise | flops 1769472 | bytes 10616832 | tf_op jit(solution)/shard_map/convert_element_type | solution.py:474
  278.8 89.6 %all-gather.5.cloned.1.call-done = bf16[2304,768]{1,0:T(8,128)(2,1)} async-done(((bf16[576,768]{1,0:T(8,128)(2,1)}), bf16[2304,768]{1,0:T(8,128)(2,1)}) %all-gather.5.cloned.1.call-update) | async-done | bytes 3538960 | tf_op jit(solution)/shard_map/all_gather | solution.py:473
  368.4 47.6 %reduce-scatter.2.cloned.1.call-done = bf16[3,1,96,768]{3,2,0,1:T(8,128)(2,1)} async-done(((bf16[3,32,96,768]{3,2,0,1:T(8,128)(2,1)}), bf16[3,1,96,768]{3,2,0,1:T(8,128)(2,1)}) %reduce-scatter.2.cloned.1.call-update) | async-done | bytes 442384 | tf_op jit(solution)/shard_map/reduce_scatter | solution.py:478
  415.9 1.1 convert_element_type.58
  423.2 2.1 reshape_squeeze.6
  427.9 2.6 fusion.13
  430.6 3.0 fusion.15
  433.6 1.1 fusion.19
  434.7 1.8 copy.91
  (108 shorter events, 19.1 us)
Async XLA Ops:
  8.0 265.2 %all-gather.7.cloned.1.call-start = ((), (), s32[]{:S(2)}) async-start(), calls=%async_computation.3 | async-start | bytes 4423680 | tf_op jit(solution)/shard_map/all_gather | solution.py:474
  92.2 4.8 %copy-start.15 = (s32[4]{0:T(128)S(1)}, s32[4]{0:T(128)}, u32[]{:S(2)}) copy-start(s32[4]{0:T(128)} %param.27) | copy-start | bytes 52
  201.8 166.6 %all-gather.5.cloned.1.call-start = ((), (), s32[]{:S(2)}) async-start(), calls=%async_computation.2 | async-start | bytes 4423680 | tf_op jit(solution)/shard_map/all_gather | solution.py:473
  202.5 213.4 %reduce-scatter.2.cloned.1.call-start = ((), (), s32[]{:S(2)}) async-start(), calls=%async_computation.1 | async-start | bytes 14598144 | tf_op jit(solution)/shard_map/reduce_scatter | solution.py:478
  213.4 0.7 copy-start.7
  213.4 1.2 copy-start.5
  213.4 1.3 copy-start.6
  213.4 1.4 copy-start.8
  213.4 46.1 %copy-start.9 = (f32[6,24]{1,0:T(8,128)S(1)}, f32[6,24]{1,0:T(8,128)}, u32[]{:S(2)}) copy-start(f32[6,24]{1,0:T(8,128)} %param.43) | copy-start | bytes 1732
  213.4 46.1 %copy-start.11 = (f32[6,24]{1,0:T(8,128)S(1)}, f32[6,24]{1,0:T(8,128)}, u32[]{:S(2)}) copy-start(f32[6,24]{1,0:T(8,128)} %param.44) | copy-start | bytes 1732
  213.4 46.1 %copy-start.12 = (f32[6,24]{1,0:T(8,128)S(1)}, f32[6,24]{1,0:T(8,128)}, u32[]{:S(2)}) copy-start(f32[6,24]{1,0:T(8,128)} %param.45) | copy-start | bytes 1732
  213.4 46.8 %copy-start.10 = (f32[6,96]{1,0:T(8,128)S(1)}, f32[6,96]{1,0:T(8,128)}, u32[]{:S(2)}) copy-start(f32[6,96]{1,0:T(8,128)} %param.40) | copy-start | bytes 6916
  213.4 46.8 %copy-start.13 = (f32[6,96]{1,0:T(8,128)S(1)}, f32[6,96]{1,0:T(8,128)}, u32[]{:S(2)}) copy-start(f32[6,96]{1,0:T(8,128)} %param.41) | copy-start | bytes 6916
  213.4 46.8 %copy-start.14 = (f32[6,96]{1,0:T(8,128)S(1)}, f32[6,96]{1,0:T(8,128)}, u32[]{:S(2)}) copy-start(f32[6,96]{1,0:T(8,128)} %param.42) | copy-start | bytes 6916
  415.9 6.5 %copy-start.1 = (bf16[3,1,96,768]{3,2,0,1:T(8,128)(2,1)S(1)}, bf16[3,1,96,768]{3,2,0,1:T(8,128)(2,1)}, u32[]{:S(2)}) copy-start(bf16[3,1,96,768]{3,2,0,1:T(8,128)(2,1)} %reduce-scatter.2.cloned.1.call-done) | copy-start | bytes 1327108
  423.2 11.5 %copy-start = (bf16[2304,768]{1,0:T(8,128)(2,1)S(1)}, bf16[2304,768]{1,0:T(8,128)(2,1)}, u32[]{:S(2)}) copy-start(bf16[2304,768]{1,0:T(8,128)(2,1)} %all-gather.5.cloned.1.call-done) | copy-start | bytes 10616836
  425.3 8.2 %copy-start.2 = (f32[96,3,192]{2,0,1:T(8,128)S(1)}, f32[96,3,192]{2,0,1:T(8,128)}, u32[]{:S(2)}) copy-start(f32[96,3,192]{2,0,1:T(8,128)} %param.28) | copy-start | bytes 663556
  425.3 8.2 %copy-start.3 = (f32[96,3,192]{2,0,1:T(8,128)S(1)}, f32[96,3,192]{2,0,1:T(8,128)}, u32[]{:S(2)}) copy-start(f32[96,3,192]{2,0,1:T(8,128)} %param.29) | copy-start | bytes 663556
  425.4 8.2 %copy-start.4 = (f32[96,3,192]{2,0,1:T(8,128)S(1)}, f32[96,3,192]{2,0,1:T(8,128)}, u32[]{:S(2)}) copy-start(f32[96,3,192]{2,0,1:T(8,128)} %param.30) | copy-start | bytes 663556
Sparse Core Ops, SparseCore 0:
  201.9 71.3 all-gather.6
  274.8 93.5 all-gather.4
Sparse Core Ops, SparseCore 1:
  213.6 202.3 reduce-scatter.1

commit v3 on v2

--- a/solution.py
+++ b/solution.py
@@ -29,6 +29,7 @@
 NT = (((1,), (1,)), ((), ()))
 RT = 192
 RL = 96
+BAND = 96
 
 
 def kind_rates():
@@ -64,17 +65,9 @@
 def arrived(dst, sem):
     pltpu.make_async_copy(dst, dst, sem).wait()
 
-def gather_kernel(rows_of, own, *refs):
-    nb = len(rows_of)
-    outs = refs[:nb]
-    lsem, zs, zr, ps, pr, ds, dr, cs, cr = refs[nb:]
-    z, me = lax.axis_index("tensor"), lax.axis_index("dp")
-    nz = lax.axis_size("tensor")
-    cp, xp, yp = flip(me, 1), flip(me, 2), flip(me, 4)
-    dg = flip(xp, 4)
-    pair = (xp, yp)
+def greet(z, nz, me, others, meanwhile):
     bar = pltpu.get_barrier_semaphore()
-    for d in (cp, xp, yp):
+    for d in others:
         pl.semaphore_signal(bar, inc=1, device_id=(d, z), device_id_type=MESH)
     @pl.when(z > 0)
     def _():
@@ -82,8 +75,42 @@
     @pl.when(z < nz - 1)
     def _():
         pl.semaphore_signal(bar, inc=1, device_id=(me, z + 1), device_id_type=MESH)
+    meanwhile()
     edges = jnp.where(z > 0, 1, 0) + jnp.where(z < nz - 1, 1, 0)
-    pl.semaphore_wait(bar, 3 + edges)
+    pl.semaphore_wait(bar, len(others) + edges)
+
+
+def pack(own, qkv, out, up, down, shared, split):
+    band, thin = shared.shape[1], split.shape[1]
+    low = [qkv[:, i].astype(bf16) for i in range(3)]
+    ot = out[...].T.astype(bf16)
+    pieces = [
+        low[0][:, :128], low[1][:, :128], low[2][:, :128],
+        jnp.concatenate([low[0][:, 128:], low[2][:, 128:]], axis=1),
+        jnp.concatenate([low[1][:, 128:], ot[:, 128:]], axis=1),
+        ot[:, :128],
+    ]
+    for i, piece in enumerate(pieces):
+        own[0:band, 128 * i : 128 * i + 128] = piece
+    own[band : band + 16] = jnp.zeros((16, D), bf16)
+    own[band : band + 6, 0:band] = shared[...].astype(bf16)
+    own[band : band + 6, 128 : 128 + thin] = split[...].astype(bf16)
+    width = D // 4
+    for f in range(4):
+        own[band + 16 : 2 * band + 16, f * width : (f + 1) * width] = up[:, f].astype(bf16)
+        own[2 * band + 16 :, f * width : (f + 1) * width] = down[f].T.astype(bf16)
+
+
+def gather_kernel(rows_of, *refs):
+    nb = len(rows_of)
+    masters, outs, own = refs[:6], refs[6 : 6 + nb], refs[6 + nb]
+    lsem, zs, zr, ps, pr, ds, dr, cs, cr = refs[7 + nb :]
+    z, me = lax.axis_index("tensor"), lax.axis_index("dp")
+    nz = lax.axis_size("tensor")
+    cp, xp, yp = flip(me, 1), flip(me, 2), flip(me, 4)
+    dg = flip(xp, 4)
+    pair = (xp, yp)
+    greet(z, nz, me, (cp, xp, yp), lambda: pack(own, *masters))
 
     starts = [sum(rows_of[:b]) for b in range(nb)]
     def own_ref(b):
@@ -175,17 +202,18 @@
         for k in range(2):
             diag(b, k).wait_send()
 
-def gather(own, rows_of, cid=1):
+def gather(masters, rows_of, cid=1):
     nb = len(rows_of)
     S = pltpu.SemaphoreType.DMA
     return pl.pallas_call(
         functools.partial(gather_kernel, rows_of),
-        out_shape=[jax.ShapeDtypeStruct((4, 8, r, D), jnp.bfloat16) for r in rows_of],
-        in_specs=[pl.BlockSpec(memory_space=pltpu.VMEM)],
+        out_shape=[jax.ShapeDtypeStruct((4, 8, r, D), bf16) for r in rows_of],
+        in_specs=[pl.BlockSpec(memory_space=pltpu.VMEM)] * 6,
         out_specs=[pl.BlockSpec(memory_space=pl.ANY)] * nb,
-        scratch_shapes=[S((nb,)), S((nb, 2, 4)), S((nb, 4)), S((nb, 2, 4)), S((nb, 2, 4)), S((nb, 2)), S((nb, 2)), S((nb, 4)), S((nb, 4))],
+        scratch_shapes=[pltpu.VMEM((sum(rows_of), D), bf16), S((nb,)), S((nb, 2, 4)), S((nb, 4))]
+        + [S((nb, 2, 4))] * 2 + [S((nb, 2))] * 2 + [S((nb, 4))] * 2,
         compiler_params=pltpu.CompilerParams(collective_id=cid, has_side_effects=True),
-    )(own)
+    )(*masters)
 
 
 def mm(a, b, dims=NN):
@@ -212,9 +240,10 @@
     return jnp.sum(v, axis=0, keepdims=True)
 
 def compute_kernel(x, cot, valid_col, keybias, vecs, bias, A, B, C,
-                   mixed, ig, gA, gB, gC, vsum, bsum,
+                   mixed, ig, gA, gB, gC,
                    first_in, second_in, gout_low, gm_low, fT, sT, goT, gmT,
-                   qkv, probs, att, middle, acc, acc2, gm, stage, sems):
+                   qkv, probs, att, middle, acc, acc2, gm, stage, bsum, vrow, sems):
+    band = stage.shape[2]
     for r in row_tiles(RL):
         rs = pl.ds(r, RL)
         n, _ = normal_of(x[rs].astype(f32))
@@ -271,12 +300,14 @@
     def put(dst, g, slot, compute):
         @pl.when(g > 0)
         def _():
-            pltpu.make_async_copy(stage.at[slot], dst.at[g - 1], sems.at[slot]).wait()
-        for c in range(0, D, 256):
-            stage[slot, pl.ds(c, 256)] = compute(c).astype(bf16)
-        pltpu.make_async_copy(stage.at[slot], dst.at[g], sems.at[slot]).start()
+            off(dst, g - 1, slot).wait()
+        for c in range(0, D, 2 * band):
+            stage[slot, pl.ds(c // band, 2)] = compute(c).astype(bf16).reshape(2, band, D)
+        off(dst, g, slot).start()
+    def off(dst, g, slot):
+        return pltpu.make_async_copy(stage.at[slot], dst.at[g, :, pl.ds(0, band)], sems.at[slot])
     def drain(dst, slot):
-        pltpu.make_async_copy(stage.at[slot], dst.at[3], sems.at[slot]).wait()
+        off(dst, 3, slot).wait()
 
     def mlp(g, carry):
         hid, gps = [], []
@@ -294,8 +325,8 @@
         hid = jnp.concatenate(hid, axis=0)
         gps = jnp.concatenate(gps, axis=0)
         bsum[1, g] = colsum(gps.astype(f32))
-        put(gC, g, 0, lambda c: mm(goT[pl.ds(c, 256)], hid))
-        put(gB, g, 1, lambda c: mm(sT[pl.ds(c, 256)], gps))
+        put(gC, g, 0, lambda c: mm(goT[pl.ds(c, 2 * band)], hid))
+        put(gB, g, 1, lambda c: mm(sT[pl.ds(c, 2 * band)], gps))
         return carry
     lax.fori_loop(0, 4, mlp, 0)
     drain(gC, 0)
@@ -363,8 +394,8 @@
             rs = pl.ds(r, RT)
             acc[rs] += mm(qkv[g, rs], w[...], NT)
         def grad(c):
-            left = mm(fT[pl.ds(c, 256)], qkv[g])
-            right = mm(gmT[pl.ds(c, 256)], att[g])
+            left = mm(fT[pl.ds(c, 2 * band)], qkv[g])
+            right = mm(gmT[pl.ds(c, 2 * band)], att[g])
             return jnp.concatenate([left[:, :512], left[:, 512:] + right], axis=1)
         put(gA, g, 0, grad)
         return carry
@@ -378,27 +409,283 @@
         ig[rs] = (gm[rs] + normal_back(gn, n, inv, vecs[0:1])).astype(bf16)
         sums[0] += colsum(gn * n)
         sums[1] += colsum(gn)
-    for i in range(6):
-        vsum[i : i + 1] = sums[i]
+    lines = sums + [bsum[i, j] for i in range(2) for j in range(4)] + [jnp.zeros((2, D), f32)]
+    lines = jnp.concatenate(lines, axis=0).astype(bf16)
+    for i in range(8):
+        vrow[i] = lines
+    def vecs_out(g):
+        return pltpu.make_async_copy(vrow, gA.at[g, :, pl.ds(band, 16)], sems.at[2 + g])
+    for g in range(4):
+        vecs_out(g).start()
+    for g in range(4):
+        vecs_out(g).wait()
+
 
 def compute(x, cot, valid_col, keybias, vecs, bias, A, B, C):
+    band = BAND
     V = pltpu.VMEM
     vm = pl.BlockSpec(memory_space=V)
     hb = pl.BlockSpec(memory_space=pl.ANY)
     S = jax.ShapeDtypeStruct
     return pl.pallas_call(
         compute_kernel,
-        out_shape=[S((LEN, D), bf16), S((LEN, D), bf16)] + [S((4, D, D), bf16)] * 3 + [S((6, D), f32), S((2, 4, 1, D), f32)],
+        out_shape=[S((LEN, D), bf16)] * 2 + [S((4, D // band, r, D), bf16) for r in (band + 16, band, band)],
         in_specs=[vm] * 9,
-        out_specs=[vm, vm, hb, hb, hb, vm, vm],
+        out_specs=[vm, vm, hb, hb, hb],
         scratch_shapes=[V((LEN, D), bf16)] * 4 + [V((D, LEN), bf16)] * 4 + [
             V((4, LEN, D), bf16), V((4, 3, 3, LEN, RT), bf16), V((4, LEN, 256), bf16),
             V((LEN, D), f32), V((LEN, D), f32), V((LEN, D), f32), V((LEN, D), f32),
-            V((2, D, D), bf16), pltpu.SemaphoreType.DMA((2,)),
+            V((2, D // band, band, D), bf16), V((2, 4, 1, D), f32), V((8, 16, D), bf16),
+            pltpu.SemaphoreType.DMA((6,)),
         ],
         compiler_params=pltpu.CompilerParams(vmem_limit_bytes=63 * 1024 * 1024),
-        cost_estimate=pl.CostEstimate(flops=57_000_000_000, bytes_accessed=32_000_000, transcendentals=6_000_000),
+        cost_estimate=pl.CostEstimate(
+            flops=57_000_000_000, bytes_accessed=32_000_000, transcendentals=6_000_000
+        ),
     )(x, cot, valid_col, keybias, vecs, bias, A, B, C)
+
+
+def scatter_kernel(rows_of, *refs):
+    nb = len(rows_of)
+    grads, (mixed, ig), (mixed_all, ig_all, total) = refs[:nb], refs[nb : nb + 2], refs[nb + 2 : nb + 5]
+    refs = refs[nb + 5 :]
+    own, got1, got2, got3, gotz = (refs[i * nb : (i + 1) * nb] for i in range(5))
+    ls, cs, cr, hs, hr, ss, sr, zs, zr, ms, mr, ml = refs[5 * nb :]
+    z, me = lax.axis_index("tensor"), lax.axis_index("dp")
+    nz = 4
+    cp, xp, yp = flip(me, 1), flip(me, 2), flip(me, 4)
+    groups = (me, xp, yp, flip(xp, 4))
+    pair = (xp, yp)
+    greet(z, nz, me, (cp, xp, yp), lambda: None)
+    starts = [sum(rows_of[:b]) for b in range(nb)]
+    half = [((0, 48), (48, r - 48)) for r in rows_of]
+
+    full = ((mixed, mixed_all), (ig, ig_all))
+    def along(i, s, src, step):
+        return send(src, full[i][1].at[s], ms.at[i, (step + 1) // 2, jnp.abs(s - z)], mr.at[i, s], (me, z + step))
+    def keep(i):
+        return pltpu.make_async_copy(full[i][0], full[i][1].at[z], ml.at[i])
+    def open_line(i):
+        @pl.when(z < nz - 1)
+        def _():
+            along(i, z, full[i][0], 1).start()
+        @pl.when(z > 0)
+        def _():
+            along(i, z, full[i][0], -1).start()
+        keep(i).start()
+    def hop(i, t):
+        for side, ok in ((-1, z >= t), (1, z + t < nz)):
+            @pl.when(ok)
+            def _():
+                s = z + side * t
+                arrived(full[i][1].at[s], mr.at[i, s])
+                @pl.when((z < nz - 1) if side < 0 else (z > 0))
+                def _():
+                    along(i, s, full[i][1].at[s], -side).start()
+    def close_line(i):
+        keep(i).wait()
+        for t in range(4):
+            @pl.when((z < nz - 1) & (z >= t))
+            def _():
+                along(i, z - t, full[i][1].at[z - t], 1).wait_send()
+            @pl.when((z > 0) & (z + t < nz))
+            def _():
+                along(i, z + t, full[i][1].at[z + t], -1).wait_send()
+
+    def twin(b, j):
+        return send(grads[b].at[:, flip(groups[j], 1)], got1[b].at[j], cs.at[b, j], cr.at[b, j], (cp, z))
+    def load(b, j):
+        return pltpu.make_async_copy(grads[b].at[:, groups[j]], own[b].at[j], ls.at[b, j])
+    def corner(b, k):
+        lo, n = half[b][k]
+        return send(own[b].at[3, :, pl.ds(lo, n)], got2[b].at[:, pl.ds(lo, n)], hs.at[b, k], hr.at[b, k], (pair[k], z))
+    def square(b, k):
+        return send(own[b].at[1 + k], got3[b].at[k], ss.at[b, k], sr.at[b, k], (pair[k], z))
+    def line(b, t, step):
+        return send(own[b].at[0, t], gotz[b].at[(1 - step) // 2, t], zs.at[b, t], zr.at[b, (1 - step) // 2, t], (me, z + step))
+
+    def add(dst, *srcs):
+        dst[...] = sum((s[...].astype(f32) for s in srcs), dst[...].astype(f32)).astype(bf16)
+    def over_z(body):
+        lax.fori_loop(0, 4, lambda s, c: (body(s), c)[1], 0)
+
+    def first(b):
+        for j in (3, 1, 2, 0):
+            twin(b, j).start()
+            load(b, j).start()
+    def merge(b, j):
+        load(b, j).wait()
+        arrived(got1[b].at[j], cr.at[b, j])
+        over_z(lambda s: add(own[b].at[j, s], got1[b].at[j, s]))
+    def second(b):
+        merge(b, 3)
+        for k in range(2):
+            corner(b, k).start()
+    def third(b):
+        for k in range(2):
+            lo, n = half[b][k]
+            part = pl.ds(lo, n)
+            arrived(got2[b].at[:, part], hr.at[b, k])
+            over_z(lambda s: add(own[b].at[2 - k, s, part], got2[b].at[s, part]))
+        for k in range(2):
+            square(b, k).start()
+    def fourth(b):
+        for k in range(2):
+            arrived(got3[b].at[k], sr.at[b, k])
+        over_z(lambda s: add(own[b].at[0, s], got3[b].at[0, s], got3[b].at[1, s]))
+        for t in (3, 2, 1):
+            @pl.when(z + t < nz)
+            def _():
+                @pl.when(z > 0)
+                def _():
+                    arrived(gotz[b].at[0, z + t], zr.at[b, 0, z + t])
+                    add(own[b].at[0, z + t], gotz[b].at[0, z + t])
+                line(b, z + t, 1).start()
+            @pl.when(z >= t)
+            def _():
+                @pl.when(z < nz - 1)
+                def _():
+                    arrived(gotz[b].at[1, z - t], zr.at[b, 1, z - t])
+                    add(own[b].at[0, z - t], gotz[b].at[1, z - t])
+                line(b, z - t, -1).start()
+    def last(b):
+        span = pl.ds(starts[b], rows_of[b])
+        total[span] = own[b][0, z].astype(f32)
+        for i, ok in ((0, z > 0), (1, z < nz - 1)):
+            @pl.when(ok)
+            def _():
+                arrived(gotz[b].at[i, z], zr.at[b, i, z])
+                total[span] += gotz[b][i, z].astype(f32)
+    def close(b):
+        for j in range(4):
+            twin(b, j).wait_send()
+        for k in range(2):
+            corner(b, k).wait_send()
+            square(b, k).wait_send()
+        for t in (3, 2, 1):
+            @pl.when(z + t < nz)
+            def _():
+                line(b, z + t, 1).wait_send()
+            @pl.when(z >= t)
+            def _():
+                line(b, z - t, -1).wait_send()
+    def rest(b):
+        for j in (1, 2, 0):
+            merge(b, j)
+
+    for b in (2, 1, 0):
+        first(b)
+    open_line(0)
+    open_line(1)
+    second(2)
+    rest(2)
+    second(1)
+    rest(1)
+    third(2)
+    second(0)
+    rest(0)
+    hop(0, 1)
+    third(1)
+    fourth(2)
+    hop(1, 1)
+    third(0)
+    fourth(1)
+    hop(0, 2)
+    last(2)
+    fourth(0)
+    hop(1, 2)
+    last(1)
+    hop(0, 3)
+    last(0)
+    hop(1, 3)
+    for i in range(2):
+        close_line(i)
+    for b in range(3):
+        close(b)
+
+
+def scatter(grads, mixed, ig, cid=2):
+    rows_of = [g.shape[2] for g in grads]
+    nb = len(rows_of)
+    S, V = pltpu.SemaphoreType.DMA, pltpu.VMEM
+    hb = pl.BlockSpec(memory_space=pl.ANY)
+    scratch = [V((4, 4, r, D), bf16) for r in rows_of] + [V((4, 4, r, D), bf16) for r in rows_of]
+    scratch += [V((4, r, D), bf16) for r in rows_of] + [V((2, 4, r, D), bf16) for r in rows_of] * 2
+    scratch += [S((nb, 4))] * 3 + [S((nb, 2))] * 4 + [S((nb, 4)), S((nb, 2, 4)), S((2, 2, 4)), S((2, 4)), S((2,))]
+    return pl.pallas_call(
+        functools.partial(scatter_kernel, rows_of),
+        out_shape=[jax.ShapeDtypeStruct((4, LEN, D), bf16)] * 2 + [jax.ShapeDtypeStruct((sum(rows_of), D), f32)],
+        in_specs=[hb] * (nb + 2),
+        out_specs=[hb, hb, pl.BlockSpec(memory_space=V)],
+        scratch_shapes=scratch,
+        compiler_params=pltpu.CompilerParams(collective_id=cid, has_side_effects=True, vmem_limit_bytes=60 * 1024 * 1024),
+    )(*grads, mixed, ig)
+
+
+def step_kernel(total, *refs):
+    ins, outs = refs[:18], refs[18:]
+    z, me = lax.axis_index("tensor"), lax.axis_index("dp")
+    band, thin = ins[12].shape[1], ins[15].shape[1]
+    vec = total[band : band + 16]
+    row = lax.broadcasted_iota(jnp.int32, (D, 128), 0)
+    col = lax.broadcasted_iota(jnp.int32, (D, 128), 1)
+
+    def pick(source):
+        chosen = jnp.where(row == source, 1.0, 0.0)
+        return lax.dot_general(
+            vec, chosen, NN, precision=lax.Precision.HIGHEST, preferred_element_type=f32
+        )
+
+    place = me * thin + col
+    shared = pick(me * band + col)[:6, :band]
+    head = jnp.where(place < 128, place, place + 256)
+    late = jnp.where(place < 128, place + 256, place + 320)
+    spots = [head, late] + [f * (D // 4) + place for f in range(4)]
+    at = lax.broadcasted_iota(jnp.int32, (16, 128), 0)
+    lines = []
+    for i, spot in enumerate(spots):
+        mine = jnp.where(at == z + (6 if i < 2 else 10), pick(spot), 0.0)
+        lines.append(jnp.sum(mine, axis=0, keepdims=True)[:, :thin])
+    split = jnp.concatenate(lines, axis=0)
+
+    def apply(kind, where, gradient):
+        rates, decays = kind_rates(), (MATRIX_DECAY,) * 4 + (0.0, 0.0)
+        m, f, s = (ins[3 * kind + i][where] for i in range(3))
+        results = adamw(m, f, s, gradient, rates[kind], decays[kind])
+        for i in range(4):
+            outs[4 * kind + i][where] = results[i]
+
+    attn = total[:band]
+    def pair(a, b):
+        return jnp.concatenate([attn[:, a : a + 128], attn[:, b : b + 64]], axis=1)
+    apply(0, (slice(None), 0), pair(0, 384))
+    apply(0, (slice(None), 1), pair(128, 512))
+    apply(0, (slice(None), 2), pair(256, 448))
+    apply(1, (slice(None),), pair(640, 576).T)
+    up = total[band + 16 : 2 * band + 16]
+    down = total[2 * band + 16 :]
+    down = down.T
+    width = D // 4
+    for f in range(4):
+        apply(2, (slice(None), f), up[:, f * width : (f + 1) * width])
+        apply(3, (f,), down[f * width : (f + 1) * width])
+    apply(4, (slice(None),), shared)
+    apply(5, (slice(None),), split)
+
+
+def step(total, state):
+    vm = pl.BlockSpec(memory_space=pltpu.VMEM)
+    shapes = []
+    for kind in range(6):
+        shape = state[3 * kind].shape
+        shapes += [jax.ShapeDtypeStruct(shape, t) for t in (f32, bf16, f32, f32)]
+    return pl.pallas_call(
+        step_kernel,
+        out_shape=shapes,
+        in_specs=[vm] * 19,
+        out_specs=[vm] * 24,
+        compiler_params=pltpu.CompilerParams(vmem_limit_bytes=56 * 1024 * 1024),
+    )(total, *state)
 
 
 def pack_attention(qkv, out):
@@ -421,36 +708,79 @@
     return jnp.stack([q, k, v], axis=1), o
 
 
+def gather_plain(masters):
+    qkv, out, up, down, shared, split = (t.astype(bf16) for t in masters)
+    band, thin, width = shared.shape[1], split.shape[1], down.shape[1] * lax.axis_size("tensor")
+    groups, copies = lax.axis_size("tensor"), lax.axis_size("dp")
+    vecs = jnp.zeros((16, width), bf16).at[:6, :band].set(shared).at[:6, 128 : 128 + thin].set(split)
+    own = jnp.concatenate(
+        [pack_attention(qkv, out.T), vecs, up.reshape(band, -1), down.reshape(-1, band).T]
+    )
+    whole = lax.all_gather(own, AXES).reshape(groups, copies, -1, width)
+    return jnp.split(whole, [band + 16, 2 * band + 16], axis=2)
+
+
+def step_plain(grads, mixed, grad_inputs, state):
+    masters, firsts, seconds = state[0::3], state[1::3], state[2::3]
+    band, thin = masters[4].shape[1], masters[5].shape[1]
+    groups, copies = lax.axis_size("tensor"), lax.axis_size("dp")
+    z, at = lax.axis_index("tensor"), lax.axis_index("dp")
+    width = grads[0].shape[-1]
+    summed = [
+        lax.psum_scatter(
+            g[:, :, :BAND].reshape(groups * copies, band, width), AXES, scatter_dimension=0
+        ).astype(f32)
+        for g in grads
+    ]
+    vec = lax.psum(grads[0][0, 0, BAND:].astype(f32), AXES)
+    shared = lax.dynamic_slice_in_dim(vec[:6], at * band, band, 1)
+    cols = lax.dynamic_slice_in_dim(vec[6:10], z, 1, 0)[0]
+    ups = lax.dynamic_slice_in_dim(vec[10:14], z, 1, 0).reshape(-1, width // groups)
+    split = jnp.stack(
+        [
+            jnp.concatenate([cols[:128], cols[384:448]]),
+            jnp.concatenate([cols[256:384], cols[448:512]]),
+        ]
+    )
+    split = lax.dynamic_slice_in_dim(jnp.concatenate([split, ups]), at * thin, thin, 1)
+    sum_qkv, sum_out = unpack_attention(summed[0])
+    gradients = (
+        sum_qkv,
+        sum_out.T,
+        summed[1].reshape(masters[2].shape),
+        summed[2].T.reshape(masters[3].shape),
+        shared,
+        split,
+    )
+    decays = (MATRIX_DECAY, MATRIX_DECAY, MATRIX_DECAY, MATRIX_DECAY, 0.0, 0.0)
+    rates = kind_rates()
+    outputs = []
+    for kind in range(6):
+        outputs.extend(
+            adamw(masters[kind], firsts[kind], seconds[kind], gradients[kind], rates[kind], decays[kind])
+        )
+    mixed, grad_inputs = (lax.all_gather(t, "tensor") for t in (mixed, grad_inputs))
+    return mixed, grad_inputs, outputs
+
+
 def local(tokens, cotangent, counts, *state):
-    masters, firsts, seconds = state[0::3], state[1::3], state[2::3]
-    qkv_master, out_master, up_master, down_master, shared_master, split_master = masters
+    masters = state[0::3]
+    shared_master, split_master = masters[4:]
     groups = lax.axis_size("tensor")
     copies = lax.axis_size("dp")
     seq_count, length, width = tokens.shape
     share = seq_count // groups
     mine = lax.axis_index("tensor") * share
-    band = qkv_master.shape[0]
+    band = shared_master.shape[1]
     thin = split_master.shape[1]
-
-    attn_own = pack_attention(qkv_master.astype(bf16), out_master.astype(bf16).T)
-    up_own = up_master.astype(bf16).reshape(band, -1)
-    down_own = down_master.astype(bf16).reshape(-1, band).T
-    vec_own = jnp.zeros((16, width), bf16)
-    vec_own = vec_own.at[:6, :band].set(shared_master.astype(bf16))
-    vec_own = vec_own.at[:6, 128 : 128 + thin].set(split_master.astype(bf16))
-    own = jnp.concatenate([attn_own, vec_own, up_own, down_own])
-    sizes = (band + 16, band, band)
-    if (groups, copies) == (4, 8):
-        mats = gather(own, sizes)
+    linked = (groups, copies) == (4, 8)
+
+    if linked:
+        mats = gather(masters, (band + 16, band, band))
     else:
-        whole = lax.all_gather(own, AXES).reshape(groups, copies, -1, width)
-        ends = [0, sizes[0], sizes[0] + sizes[1], sum(sizes)]
-        mats = [whole[:, :, ends[i] : ends[i + 1]] for i in range(3)]
-    attn_all, up_all, down_all = mats
-    vec_all = attn_all[:, :, band:].astype(f32)
-    attn_all, up_all, down_all = (
-        t[:, :, :band].reshape(groups, width, width) for t in (attn_all, up_all, down_all)
-    )
+        mats = gather_plain(masters)
+    vec_all = mats[0][:, :, band:].astype(f32)
+    attn_all, up_all, down_all = (t[:, :, :band].reshape(groups, width, width) for t in mats)
     shared_vecs = jnp.swapaxes(vec_all[0, :, :6, :band], 0, 1).reshape(6, width)
     split_vecs = vec_all[:, :, :6, 128 : 128 + thin].reshape(groups, copies, 6, thin)
     split_vecs = jnp.swapaxes(split_vecs, 1, 2).reshape(groups, 6, copies * thin)
@@ -466,45 +796,16 @@
     cot = lax.dynamic_slice_in_dim(cotangent, mine, share, 0).reshape(length, width)
     count = lax.dynamic_slice_in_dim(counts, mine, share, 0)
     valid = lax.broadcasted_iota(jnp.int32, (length, 1), 0) < count
-    mixed, grad_inputs, grad_attn, grad_up, grad_down, shared_grad, split_grad = compute(
+    mixed, grad_inputs, *grads = compute(
         x, cot, valid.astype(f32), jnp.where(valid, 0.0, MASK_FILL), shared_vecs, bias,
         attn_all, up_all, down_all,
     )
-    mixed = lax.all_gather(mixed[None], "tensor", axis=0, tiled=True)
-    grad_inputs = lax.all_gather(grad_inputs[None], "tensor", axis=0, tiled=True).astype(f32)
-
-    grads = jnp.stack([grad_attn, grad_up, grad_down])
-    grads = grads.reshape(3, groups * copies, band, width)
-    grads = lax.psum_scatter(grads, AXES, scatter_dimension=1, tiled=False).astype(f32)
-    cols = split_grad.reshape(2, groups, width)
-    grad_bq = jnp.concatenate([cols[0, :, :128], cols[0, :, 384:448]], axis=1).reshape(1, width)
-    grad_bv = jnp.concatenate([cols[0, :, 256:384], cols[0, :, 448:512]], axis=1).reshape(1, width)
-    grad_bu = jnp.swapaxes(cols[1].reshape(groups, -1, width // groups), 0, 1).reshape(-1, width)
-    vec_sum = lax.psum(jnp.concatenate([shared_grad, grad_bq, grad_bv, grad_bu]), AXES)
-    at = lax.axis_index("dp")
-    shared_sum = lax.dynamic_slice_in_dim(vec_sum[:6], at * band, band, 1)
-    split_at = (lax.axis_index("tensor") * copies + at) * thin
-    split_sum = lax.dynamic_slice_in_dim(vec_sum[6:], split_at, thin, 1)
-
-    sum_qkv, sum_out = unpack_attention(grads[0])
-    summed = (
-        sum_qkv,
-        sum_out.T,
-        grads[1].reshape(up_master.shape),
-        grads[2].T.reshape(down_master.shape),
-        shared_sum,
-        split_sum,
-    )
-    decays = (MATRIX_DECAY, MATRIX_DECAY, MATRIX_DECAY, MATRIX_DECAY, 0.0, 0.0)
-    rates = kind_rates()
-    outputs = [mixed, grad_inputs]
-    for kind in range(6):
-        outputs.extend(
-            adamw(
-                masters[kind], firsts[kind], seconds[kind], summed[kind], rates[kind], decays[kind]
-            )
-        )
-    return tuple(outputs)
+    if linked:
+        mixed, grad_inputs, total = scatter(grads, mixed, grad_inputs)
+        outputs = step(total, state)
+    else:
+        mixed, grad_inputs, outputs = step_plain(grads, mixed, grad_inputs, state)
+    return (mixed, grad_inputs.astype(f32), *outputs)
 
 
 def solution(mesh):

time: 445 us -> 349 us (0.78)
  waiting for transfers between devices: 150 us -> 0 us
  Pallas kernels: 167 us -> 316 us
  blocking collectives: 44.7 us -> 0 us
  other arithmetic: 41 us -> 9.74 us
  between operations: 16 us -> 0.82 us
    pallas_call x1 -> x3, Pallas kernels: 97 us -> 246 us  [the longest x1 139 us: scatter(): pl.pallas_call(functools.partial(scatter_kernel, rows_of), out_shape=[jax...]
    all_gather x2 -> x0, waiting for transfers between devices: 102 us -> none  [the longest x1 89.6 us: local(): mixed = lax.all_gather(mixed[None], 'tensor', axis=0, tiled=True)]
    reduce_scatter x1 -> x0, waiting for transfers between devices: 47.6 us -> none  [local(): lax.psum_scatter(grads, AXES, scatter_dimension=1, tiled=False).astype(f32)]
    psum x1 -> x0, blocking collectives: 44.7 us -> none  [local(): lax.psum(jnp.concatenate([shared_grad, grad_bq, grad_bv, grad_bu]), AXES)]
    another operation x7 -> x0, other arithmetic: 17.4 us -> none  [the longest x1 10.8 us: local(): grads = jnp.stack([grad_attn, grad_up, grad_down])]
    convert_element_type x13 -> x2, other arithmetic: 20 us -> 6.95 us  [the longest x1 5.63 us: local(): return (mixed, grad_inputs.astype(f32), *outputs)]
    unnamed x41 -> x16, local copies, waits for them, and re-layouts: 6.57 us -> 12.6 us
  transfers between devices with their start and end apart: 3 -> 0, of which waited for: 3 -> 0; matrix products, arithmetic and copies ran while one was open for 4% -> 0% of each run, Pallas kernels for 0% -> 0%
where the time goes in v3:
time: 349 us
  Pallas kernels  316 us (91%)
  local copies, waits for them, and re-layouts  22.5 us (6%)
  other arithmetic  9.74 us (3%)
    pallas_call x1, Pallas kernels, scatter(): pl.pallas_call(functools.partial(scatter_kernel, rows_of), out_shape=[jax...  139 us
    pallas_call x1, Pallas kernels, compute(): pl.pallas_call(compute_kernel, out_shape=[S((LEN, D), bf16)] * 2 + [S((4,...  98.3 us
    pallas_call x1, Pallas kernels, gather(): pl.pallas_call(functools.partial(gather_kernel, rows_of), out_shape=[jax....  70.5 us
    unnamed x16, local copies, waits for them, and re-layouts  12.6 us
    pallas_call x1, Pallas kernels, step(): pl.pallas_call(step_kernel, out_shape=shapes, in_specs=[vm] * 19, out_spe...  8.36 us

profile of v3, /device:TPU:0, one launch (start us, length us, event | category | flops | bytes accessed | tf_op | source)
XLA Modules:
  0.0 349.1 jit_solution(2143328589237338999)
XLA Ops:
  0.7 1.9 copy.47.refs_0_
  2.6 70.5 %shard_map.404 = (bf16[4,8,112,768]{3,2,1,0:T(8,128)(2,1)}, bf16[4,8,96,768]{3,2,1,0:T(8,128)(2,1)}, bf16[4,8,96,768]{3,2,1,0:T(8,128)(2,1)}) custom-call(f32[96,3,192]{2,1,0:T(4,128)} %copy.47.refs_0_, f32[192,96]{1,0:T(8,128)} %refs_3_.3, f32[96,4,192]{2,1,0:T(4,128)} %refs_6_.1, f32[4,192,96]{2,1,0:T(8,128)} %refs_9_.1, f32[6,96]{1,0:T(8,128)} %refs_12_.1, ...), custom_call_target="tpu_custom_call" | custom-call | tf_op jit(solution)/shard_map/pallas_call | solution.py:208
  73.1 1.3 slice_convert_fusion
  74.5 0.1 reshape.98
  74.6 0.1 concatenate.7
  74.7 0.1 stack_reshape.3
  74.8 0.6 reshape.99.bias
  75.5 2.8 dynamic-slice_bitcast_fusion
  78.3 0.6 dynamic_slice.11
  78.9 1.4 fusion.keybias
  80.3 1.4 fusion.1.valid_col
  81.7 0.7 reshape.97.vecs
  82.4 4.8 %slice.43 = bf16[4,8,96,768]{3,2,1,0:T(8,128)(2,1)} slice(bf16[4,8,112,768]{3,2,1,0:T(8,128)(2,1)} %get-tuple-element.61), slice={[0:4], [0:8], [0:96], [0:768]} | slice | bytes 9437184 | tf_op jit(solution)/shard_map/slice | solution.py:783
  87.2 98.3 %shard_map.405 = (bf16[576,768]{1,0:T(8,128)(2,1)}, bf16[576,768]{1,0:T(8,128)(2,1)}, bf16[4,8,112,768]{3,2,1,0:T(8,128)(2,1)}, bf16[4,8,96,768]{3,2,1,0:T(8,128)(2,1)}, bf16[4,8,96,768]{3,2,1,0:T(8,128)(2,1)}) custom-call(bf16[576,768]{1,0:T(8,128)(2,1)} %get-tuple-element.125.x, bf16[576,768]{1,0:T(8,128)(2,1)} %get-tuple-element.124.cot, ...), custom_call_target="tpu_custom_call" | custom-call | flops 57000001536 | bytes 32000000 | tf_op jit(solution)/shard_map/pallas_call | solution.py:430
  185.5 138.9 %shard_map.406 = (bf16[4,576,768]{2,1,0:T(8,128)(2,1)}, bf16[4,576,768]{2,1,0:T(8,128)(2,1)}, f32[304,768]{1,0:T(8,128)}) custom-call(bf16[4,8,112,768]{3,2,1,0:T(8,128)(2,1)} %get-tuple-element.64.refs_0_, bf16[4,8,96,768]{3,2,1,0:T(8,128)(2,1)} %get-tuple-element.65.refs_1_, bf16[4,8,96,768]{3,2,1,0:T(8,128)(2,1)} %get-tuple-element.66.refs_2_, ...), custom_call_target="tpu_custom_call" | custom-call | tf_op jit(solution)/shard_map/pallas_call | solution.py:615
  324.4 5.6 %convert_element_type.11 = f32[4,576,768]{2,1,0:T(8,128)} convert(bf16[4,576,768]{2,1,0:T(8,128)(2,1)} %get-tuple-element.70) | non-fusion elementwise | flops 1769472 | bytes 10616832 | tf_op jit(solution)/shard_map/convert_element_type | solution.py:808
  330.1 0.9 copy.52.refs_1_
  331.0 1.0 copy.53.refs_2_
  332.0 8.4 %shard_map.407 = (f32[96,3,192]{2,1,0:T(4,128)}, bf16[96,3,192]{2,1,0:T(4,128)(2,1)}, f32[96,3,192]{2,1,0:T(4,128)}, f32[96,3,192]{2,1,0:T(4,128)}, f32[192,96]{...) custom-call(f32[304,768]{1,0:T(8,128)} %get-tuple-element.71.total, ...), custom_call_target="tpu_custom_call" | custom-call | tf_op jit(solution)/shard_map/pallas_call | solution.py:682
  340.4 1.8 copy.54
  342.1 1.8 copy.56
  343.9 1.8 copy.57
  345.7 1.6 copy.55
  347.3 1.8 copy.59
  (22 shorter events, 0.1 us)
Async XLA Ops:
  73.1 5.3 %copy-start.3 = (s32[4]{0:T(128)S(1)}, s32[4]{0:T(128)}, u32[]{:S(2)}) copy-start(s32[4]{0:T(128)} %param.23) | copy-start | bytes 52
  324.4 5.7 %copy-start.1 = (f32[96,3,192]{2,0,1:T(8,128)S(1)}, f32[96,3,192]{2,0,1:T(8,128)}, u32[]{:S(2)}) copy-start(f32[96,3,192]{2,0,1:T(8,128)} %param.25) | copy-start | bytes 663556
  324.4 6.6 %copy-start.2 = (f32[96,3,192]{2,0,1:T(8,128)S(1)}, f32[96,3,192]{2,0,1:T(8,128)}, u32[]{:S(2)}) copy-start(f32[96,3,192]{2,0,1:T(8,128)} %param.26) | copy-start | bytes 663556
  332.0 15.3 %copy-start = (bf16[4,576,768]{2,1,0:T(8,128)(2,1)S(1)}, bf16[4,576,768]{2,1,0:T(8,128)(2,1)}, u32[]{:S(2)}) copy-start(bf16[4,576,768]{2,1,0:T(8,128)(2,1)} %get-tuple-element.152) | copy-start | bytes 10616836

commit v4 on v3

--- a/solution.py
+++ b/solution.py
@@ -80,8 +80,32 @@
     pl.semaphore_wait(bar, len(others) + edges)
 
 
-def pack(own, qkv, out, up, down, shared, split):
+def mm(a, b, dims=NN):
+    return lax.dot_general(a, b, dims, preferred_element_type=f32)
+
+def normal_of(rows):
+    mean = jnp.mean(rows, axis=-1, keepdims=True)
+    centred = rows - mean
+    inverse = lax.rsqrt(jnp.mean(centred * centred, axis=-1, keepdims=True) + LN_EPS)
+    return centred * inverse, inverse
+
+def normal_back(grad, normal, inverse, gain):
+    scaled = grad * gain
+    return inverse * (
+        scaled
+        - jnp.mean(scaled, axis=-1, keepdims=True)
+        - normal * jnp.mean(scaled * normal, axis=-1, keepdims=True)
+    )
+
+def row_tiles(size):
+    return range(0, LEN, size)
+
+def colsum(v):
+    return jnp.sum(v, axis=0, keepdims=True)
+
+def pack(own, pad, qkv, out, up, down, shared, split):
     band, thin = shared.shape[1], split.shape[1]
+    me = lax.axis_index("dp")
     low = [qkv[:, i].astype(bf16) for i in range(3)]
     ot = out[...].T.astype(bf16)
     pieces = [
@@ -92,27 +116,38 @@
     ]
     for i, piece in enumerate(pieces):
         own[0:band, 128 * i : 128 * i + 128] = piece
-    own[band : band + 16] = jnp.zeros((16, D), bf16)
-    own[band : band + 6, 0:band] = shared[...].astype(bf16)
-    own[band : band + 6, 128 : 128 + thin] = split[...].astype(bf16)
     width = D // 4
     for f in range(4):
         own[band + 16 : 2 * band + 16, f * width : (f + 1) * width] = up[:, f].astype(bf16)
         own[2 * band + 16 :, f * width : (f + 1) * width] = down[f].T.astype(bf16)
-
-
-def gather_kernel(rows_of, *refs):
-    nb = len(rows_of)
-    masters, outs, own = refs[:6], refs[6 : 6 + nb], refs[6 + nb]
-    lsem, zs, zr, ps, pr, ds, dr, cs, cr = refs[7 + nb :]
-    z, me = lax.axis_index("tensor"), lax.axis_index("dp")
-    nz = lax.axis_size("tensor")
+    pad[...] = jnp.zeros_like(pad)
+    pad[0:6, 0:band] = shared[...]
+    pad[8:14, 0:thin] = split[...]
+    vals = pad[...].astype(bf16)
+    src = lax.broadcasted_iota(jnp.int32, (128, D), 0)
+    col = lax.broadcasted_iota(jnp.int32, (128, D), 1)
+
+    def placed(spot):
+        return mm(vals, jnp.where(col == spot, 1.0, 0.0).astype(bf16))
+
+    at = me * thin + src
+    attn = placed(jnp.where(at < 128, at, at + 256))[8:9]
+    attn += placed(jnp.where(at < 128, at + 256, at + 320))[9:10]
+    ups = sum(placed(f * width + at)[10 + f : 11 + f] for f in range(4))
+    rows = [placed(me * band + src)[0:6], attn, ups, jnp.zeros((8, D), f32)]
+    own[band : band + 16] = jnp.concatenate(rows, axis=0).astype(bf16)
+
+
+def gather_steps(own, outs, masters_rows, z, me, sems):
+    rows_of = masters_rows
+    nb, nz = len(rows_of), 4
+    lsem, zs, zr, ps, pr, ds, dr, cs, cr = sems
     cp, xp, yp = flip(me, 1), flip(me, 2), flip(me, 4)
     dg = flip(xp, 4)
     pair = (xp, yp)
-    greet(z, nz, me, (cp, xp, yp), lambda: pack(own, *masters))
-
     starts = [sum(rows_of[:b]) for b in range(nb)]
+    half = [[(0, 48), (48, r - 48)] for r in rows_of]
+
     def own_ref(b):
         return own.at[pl.ds(starts[b], rows_of[b])]
     def right(b, s, src):
@@ -124,7 +159,6 @@
     def spread(b, s, src):
         for k in range(2):
             side(b, s, src, k).start()
-    half = [[(0, r//32*16), (r//32*16, r - r//32*16)] for r in rows_of]
     def diag(b, k):
         lo, n = half[b][k]
         part = outs[b].at[:, pair[k], pl.ds(lo, n)]
@@ -132,9 +166,10 @@
     def twin(b, j):
         part = outs[b].at[:, (me, xp, yp, dg)[j]]
         return send(part, part, cs.at[b, j], cr.at[b, j], (cp, z))
-    keep = [pltpu.make_async_copy(own_ref(b), outs[b].at[z, me], lsem.at[b]) for b in range(nb)]
-
-    def open_block(b):
+    def keep(b):
+        return pltpu.make_async_copy(own_ref(b), outs[b].at[z, me], lsem.at[b])
+
+    def opens(b):
         @pl.when(z < nz - 1)
         def _():
             right(b, z, own_ref(b)).start()
@@ -142,8 +177,7 @@
         def _():
             left(b, z, own_ref(b)).start()
         spread(b, z, own_ref(b))
-        keep[b].start()
-
+        keep(b).start()
     def hop(b, t):
         @pl.when(z >= t)
         def _():
@@ -161,8 +195,8 @@
             def _():
                 left(b, s, outs[b].at[s, me]).start()
             spread(b, s, outs[b].at[s, me])
-    def twin_own(b):
-        keep[b].wait()
+    def lined(b):
+        keep(b).wait()
         twin(b, 0).start()
     def square(b):
         for k in range(2):
@@ -175,20 +209,10 @@
             lo, n = half[b][k]
             arrived(outs[b].at[:, dg, pl.ds(lo, n)], dr.at[b, k])
         twin(b, 3).start()
-    def finish(b):
+    def ready(b):
         for j, d in enumerate((cp, flip(xp, 1), flip(yp, 1), flip(dg, 1))):
             arrived(outs[b].at[:, d], cr.at[b, j])
-    for b in range(nb):
-        open_block(b)
-    for t in (1, 2, 3):
-        for b in range(nb):
-            hop(b, t)
-    for step in (twin_own, square, corner):
-        for b in range(nb):
-            step(b)
-    for b in range(nb):
-        finish(b)
-    for b in range(nb):
+    def sent(b):
         for t in range(4):
             @pl.when((z < nz - 1) & (z >= t))
             def _():
@@ -201,67 +225,143 @@
             twin(b, t).wait_send()
         for k in range(2):
             diag(b, k).wait_send()
-
-def gather(masters, rows_of, cid=1):
-    nb = len(rows_of)
-    S = pltpu.SemaphoreType.DMA
-    return pl.pallas_call(
-        functools.partial(gather_kernel, rows_of),
-        out_shape=[jax.ShapeDtypeStruct((4, 8, r, D), bf16) for r in rows_of],
-        in_specs=[pl.BlockSpec(memory_space=pltpu.VMEM)] * 6,
-        out_specs=[pl.BlockSpec(memory_space=pl.ANY)] * nb,
-        scratch_shapes=[pltpu.VMEM((sum(rows_of), D), bf16), S((nb,)), S((nb, 2, 4)), S((nb, 4))]
-        + [S((nb, 2, 4))] * 2 + [S((nb, 2))] * 2 + [S((nb, 4))] * 2,
-        compiler_params=pltpu.CompilerParams(collective_id=cid, has_side_effects=True),
-    )(*masters)
-
-
-def mm(a, b, dims=NN):
-    return lax.dot_general(a, b, dims, preferred_element_type=f32)
-
-def normal_of(rows):
-    mean = jnp.mean(rows, axis=-1, keepdims=True)
-    centred = rows - mean
-    inverse = lax.rsqrt(jnp.mean(centred * centred, axis=-1, keepdims=True) + LN_EPS)
-    return centred * inverse, inverse
-
-def normal_back(grad, normal, inverse, gain):
-    scaled = grad * gain
-    return inverse * (
-        scaled
-        - jnp.mean(scaled, axis=-1, keepdims=True)
-        - normal * jnp.mean(scaled * normal, axis=-1, keepdims=True)
-    )
-
-def row_tiles(size):
-    return range(0, LEN, size)
-
-def colsum(v):
-    return jnp.sum(v, axis=0, keepdims=True)
-
-def compute_kernel(x, cot, valid_col, keybias, vecs, bias, A, B, C,
-                   mixed, ig, gA, gB, gC,
-                   first_in, second_in, gout_low, gm_low, fT, sT, goT, gmT,
-                   qkv, probs, att, middle, acc, acc2, gm, stage, bsum, vrow, sems):
-    band = stage.shape[2]
+    return opens, hop, lined, square, corner, ready, sent
+
+
+def line_steps(block, whole, z, me, sems):
+    nz = 4
+    ms, mr, ml = sems
+
+    def along(s, src, way):
+        return send(src, whole.at[s], ms.at[(way + 1) // 2, jnp.abs(s - z)], mr.at[s], (me, z + way))
+    def keep():
+        return pltpu.make_async_copy(block, whole.at[z], ml.at[0])
+    def opens():
+        @pl.when(z < nz - 1)
+        def _():
+            along(z, block, 1).start()
+        @pl.when(z > 0)
+        def _():
+            along(z, block, -1).start()
+        keep().start()
+    def hop(t):
+        for way, ok in ((-1, z >= t), (1, z + t < nz)):
+            @pl.when(ok)
+            def _():
+                s = z + way * t
+                arrived(whole.at[s], mr.at[s])
+                @pl.when((z < nz - 1) if way < 0 else (z > 0))
+                def _():
+                    along(s, whole.at[s], -way).start()
+    def close():
+        keep().wait()
+        for t in range(4):
+            @pl.when((z < nz - 1) & (z >= t))
+            def _():
+                along(z - t, whole.at[z - t], 1).wait_send()
+            @pl.when((z > 0) & (z + t < nz))
+            def _():
+                along(z + t, whole.at[z + t], -1).wait_send()
+    return opens, hop, close
+
+
+QT = ((0, 256), (256, 256), (512, 64))
+
+
+def layer_kernel(linked, *refs):
+    tokens, cotangent, counts = refs[:3]
+    weights_in = refs[3 : 9 if linked else 6]
+    refs = refs[9 if linked else 6 :]
+    mixed_all, ig_out, gA, gB, gC = refs[:5]
+    (WA, WB, WC, x, gout_low, first_in, second_in, gm_low, left_t, right_t, qkv, probs, att,
+     middle, acc, acc2, hidden, slope, stage, bsum, vrow, vecs, bias, mixed, sems) = refs[5:30]
+    z, me = lax.axis_index("tensor"), lax.axis_index("dp")
+    band = BAND
+    if linked:
+        own, pad = refs[30:32]
+        opens, hop, lined, square, corner, ready, sent = gather_steps(
+            own, (WA, WB, WC), (band + 16, band, band), z, me, refs[32:41]
+        )
+        mopen, mhop, mclose = line_steps(mixed, mixed_all, z, me, refs[41:44])
+    else:
+        def nothing(*args):
+            return None
+        opens = hop = lined = square = corner = sent = mhop = nothing
+        def ready(b):
+            pltpu.make_async_copy(weights_in[b], (WA, WB, WC)[b], sems.at[8 + b]).wait()
+        def mopen():
+            pltpu.make_async_copy(mixed, mixed_all, sems.at[11]).start()
+        def mclose():
+            pltpu.make_async_copy(mixed, mixed_all, sems.at[11]).wait()
+
+    loads = [
+        pltpu.make_async_copy(tokens.at[z], x, sems.at[6]),
+        pltpu.make_async_copy(cotangent.at[z], gout_low, sems.at[7]),
+    ]
+    for load in loads:
+        load.start()
+    if linked:
+        greet(z, 4, me, (flip(me, 1), flip(me, 2), flip(me, 4)), lambda: pack(own, pad, *weights_in))
+    else:
+        for b in range(3):
+            pltpu.make_async_copy(weights_in[b], (WA, WB, WC)[b], sems.at[8 + b]).start()
+    count = counts[z]
+    column = lax.broadcasted_iota(jnp.int32, (LEN, 1), 0)
+    keybias = jnp.where(column < count, 0.0, MASK_FILL)
+    def valid(r):
+        return jnp.where(lax.broadcasted_iota(jnp.int32, (RL, 1), 0) + r < count, 1.0, 0.0)
+
+    opens(0)
+    for load in loads:
+        load.wait()
     for r in row_tiles(RL):
         rs = pl.ds(r, RL)
-        n, _ = normal_of(x[rs].astype(f32))
-        first_in[rs] = (n * vecs[0:1] + vecs[1:2]).astype(bf16)
-        go = cot[rs].astype(f32) * valid_col[rs]
-        gout_low[rs] = go.astype(bf16)
-    fT[...] = first_in[...].T
-    goT[...] = gout_low[...].T
+        gout_low[rs] = (gout_low[rs].astype(f32) * valid(r)).astype(bf16)
+        middle[rs] = normal_of(x[rs].astype(f32))[0]
+    hop(0, 1)
+    hop(0, 2)
+    opens(1)
+    right_t[...] = gout_low[...].T
+    hop(0, 3)
+    lined(0)
+    square(0)
+    hop(1, 1)
+    hop(1, 2)
+    opens(2)
+    hop(1, 3)
+    lined(1)
+    corner(0)
+    ready(0)
+    lines = [sum(WA[g, i, band : band + 16].astype(f32) for i in range(8)) for g in range(4)]
+    vecs[...] = lines[0]
+    for g in range(4):
+        bias[0, g] = lines[g][6:7]
+        bias[1, g] = lines[g][7:8]
+    for r in row_tiles(RL):
+        rs = pl.ds(r, RL)
+        first_in[rs] = (middle[rs] * vecs[0:1] + vecs[1:2]).astype(bf16)
     lane = lax.broadcasted_iota(jnp.int32, (1, 128), 1)
     low = lane < 64
     acc[...] = jnp.zeros_like(acc)
 
+    def at(g, table):
+        for i, steps in enumerate(table):
+            if steps:
+                @pl.when(g == i)
+                def _():
+                    for step, *args in steps:
+                        step(*args)
+    def wa(g, lo=0, hi=D):
+        return WA[g, :, 0:band, lo:hi].reshape(D, hi - lo)
+    def wb(g):
+        return WB[g].reshape(D, D)
+    def wc(g):
+        return WC[g].reshape(D, D)
+
     def forward(g, carry):
-        w = A.at[g]
         for r in row_tiles(RT):
             rs = pl.ds(r, RT)
-            p = mm(first_in[rs], w[...]) + bias[0, g]
-            qkv[g, rs] = p.astype(bf16)
+            qkv[g, rs] = (mm(first_in[rs], wa(g)) + bias[0, g]).astype(bf16)
         def tile(i):
             return qkv[g, :, 128 * i : 128 * i + 128]
         outs = []
@@ -271,19 +371,19 @@
             vt = v.T
             vt = vt[64:] if h else vt[:64]
             cols = []
-            for r in row_tiles(RT):
-                s = mm(k, q[r : r + RT], NT) + keybias[...]
-                top = jnp.max(s, axis=0, keepdims=True)
-                e = jnp.exp(s - top)
+            for r, n in QT:
+                s = mm(k, q[r : r + n], NT) + keybias
+                e = jnp.exp(s - jnp.max(s, axis=0, keepdims=True))
                 p = (e * (1.0 / jnp.sum(e, axis=0, keepdims=True))).astype(bf16)
-                probs[g, h, r // RT] = p
+                probs[g, h, :, pl.ds(r, n)] = p
                 cols.append(mm(vt, p))
             outs.append(jnp.concatenate(cols, axis=1))
         att[g, :, 128:256] = jnp.concatenate(outs[:2], axis=0).T.astype(bf16)
         att[g, :, 0:128] = jnp.concatenate([jnp.zeros_like(outs[2]), outs[2]], axis=0).T.astype(bf16)
         for r in row_tiles(RT):
             rs = pl.ds(r, RT)
-            acc[rs] += mm(att[g, rs], w[:, 512:768], NT)
+            acc[rs] += mm(att[g, rs], wa(g, 512, D), NT)
+        at(g, [[(hop, 2, 1), (hop, 2, 2)], [(hop, 2, 3), (lined, 2), (square, 1)], [(corner, 1)], []])
         return carry
     lax.fori_loop(0, 4, forward, 0)
 
@@ -291,68 +391,79 @@
         rs = pl.ds(r, RL)
         m = x[rs].astype(f32) + acc[rs] + vecs[2:3]
         middle[rs] = m
-        n, _ = normal_of(m)
-        second_in[rs] = (n * vecs[3:4] + vecs[4:5]).astype(bf16)
-    sT[...] = second_in[...].T
+        second_in[rs] = (normal_of(m)[0] * vecs[3:4] + vecs[4:5]).astype(bf16)
+    left_t[...] = second_in[...].T
     acc[...] = jnp.zeros_like(acc)
     acc2[...] = jnp.zeros_like(acc2)
-
-    def put(dst, g, slot, compute):
+    ready(1)
+
+    def mlp_up(g, carry):
+        for r in row_tiles(RT):
+            rs = pl.ds(r, RT)
+            u = mm(second_in[rs], wb(g)) + bias[1, g]
+            phi = 0.5 * (1.0 + lax.erf(u * SQRT_HALF))
+            hidden[g, rs] = (u * phi).astype(bf16)
+            slope[g, rs] = (phi + u * jnp.exp(-0.5 * u * u) * INV_ROOT_TAU).astype(bf16)
+        at(g, [[], [(square, 2)], [], []])
+        return carry
+    lax.fori_loop(0, 4, mlp_up, 0)
+    corner(2)
+    ready(2)
+
+    def mlp_down(g, carry):
+        for r in row_tiles(RT):
+            rs = pl.ds(r, RT)
+            acc[rs] += mm(hidden[g, rs], wc(g), NT)
+        return carry
+    lax.fori_loop(0, 4, mlp_down, 0)
+    for r in row_tiles(RL):
+        rs = pl.ds(r, RL)
+        mixed[rs] = ((middle[rs] + acc[rs] + vecs[5:6]) * valid(r)).astype(bf16)
+    mopen()
+
+    def off(dst, g, slot):
+        return pltpu.make_async_copy(stage.at[slot], dst.at[g, :, pl.ds(0, band)], sems.at[slot])
+    def put(dst, g, slot, part):
         @pl.when(g > 0)
         def _():
             off(dst, g - 1, slot).wait()
         for c in range(0, D, 2 * band):
-            stage[slot, pl.ds(c // band, 2)] = compute(c).astype(bf16).reshape(2, band, D)
+            stage[slot, pl.ds(c // band, 2)] = part(c).astype(bf16).reshape(2, band, D)
         off(dst, g, slot).start()
-    def off(dst, g, slot):
-        return pltpu.make_async_copy(stage.at[slot], dst.at[g, :, pl.ds(0, band)], sems.at[slot])
-    def drain(dst, slot):
-        off(dst, 3, slot).wait()
-
-    def mlp(g, carry):
-        hid, gps = [], []
+
+    def mlp_back(g, carry):
         for r in row_tiles(RT):
             rs = pl.ds(r, RT)
-            u = mm(second_in[rs], B[g]) + bias[1, g]
-            phi = 0.5 * (1.0 + lax.erf(u * SQRT_HALF))
-            hidden = (u * phi).astype(bf16)
-            slope = phi + u * jnp.exp(-0.5 * u * u) * INV_ROOT_TAU
-            gp = (mm(gout_low[rs], C[g]) * slope).astype(bf16)
-            acc[rs] += mm(hidden, C[g], NT)
-            acc2[rs] += mm(gp, B[g], NT)
-            hid.append(hidden)
-            gps.append(gp)
-        hid = jnp.concatenate(hid, axis=0)
-        gps = jnp.concatenate(gps, axis=0)
-        bsum[1, g] = colsum(gps.astype(f32))
-        put(gC, g, 0, lambda c: mm(goT[pl.ds(c, 2 * band)], hid))
-        put(gB, g, 1, lambda c: mm(sT[pl.ds(c, 2 * band)], gps))
+            gp = (mm(gout_low[rs], wc(g)) * slope[g, rs].astype(f32)).astype(bf16)
+            slope[g, rs] = gp
+            acc2[rs] += mm(gp, wb(g), NT)
+        bsum[1, g] = colsum(slope[g].astype(f32))
+        put(gC, g, 0, lambda c: mm(right_t[pl.ds(c, 2 * band)], hidden[g]))
+        put(gB, g, 1, lambda c: mm(left_t[pl.ds(c, 2 * band)], slope[g]))
         return carry
-    lax.fori_loop(0, 4, mlp, 0)
-    drain(gC, 0)
-    drain(gB, 1)
+    lax.fori_loop(0, 4, mlp_back, 0)
+    off(gC, 3, 0).wait()
+    off(gB, 3, 1).wait()
 
     sums = [jnp.zeros((1, D), f32) for _ in range(6)]
     for r in row_tiles(RL):
         rs = pl.ds(r, RL)
-        m = middle[rs]
-        mixed[rs] = ((m + acc[rs] + vecs[5:6]) * valid_col[rs]).astype(bf16)
-        n, inv = normal_of(m)
+        n, inv = normal_of(middle[rs])
         gn = acc2[rs]
         go = gout_low[rs].astype(f32)
         t = go + normal_back(gn, n, inv, vecs[3:4])
-        gm[rs] = t
+        middle[rs] = t
         gm_low[rs] = t.astype(bf16)
         sums[2] += colsum(t)
         sums[3] += colsum(gn * n)
         sums[4] += colsum(gn)
         sums[5] += colsum(go)
-    gmT[...] = gm_low[...].T
+    left_t[...] = first_in[...].T
+    right_t[...] = gm_low[...].T
     acc[...] = jnp.zeros_like(acc)
 
     def backward(g, carry):
-        w = A.at[g]
-        ga = mm(gm_low[...], w[:, 512:768]).astype(bf16)
+        ga = mm(gm_low[...], wa(g, 512, D)).astype(bf16)
         def tile(i):
             return qkv[g, :, 128 * i : 128 * i + 128]
         dq, dk, dv = [], [], []
@@ -363,15 +474,15 @@
             kt = k.T
             kt = kt[64:] if h == 1 else kt[:64]
             dqs, dks, dvs = [], 0.0, 0.0
-            for r in row_tiles(RT):
-                p = probs[g, h, r // RT]
-                dp = mm(v, gmask[r : r + RT], NT)
+            for r, n in QT:
+                p = probs[g, h, :, pl.ds(r, n)]
+                dp = mm(v, gmask[r : r + n], NT)
                 pf = p.astype(f32)
                 inner = jnp.sum(pf * dp, axis=0, keepdims=True)
                 ds = (pf * (dp - inner)).astype(bf16)
                 dqs.append(mm(kt, ds))
-                dks = dks + mm(ds, q[r : r + RT])
-                dvs = dvs + mm(p, gt[r : r + RT])
+                dks = dks + mm(ds, q[r : r + n])
+                dvs = dvs + mm(p, gt[r : r + n])
             dq.append(jnp.concatenate(dqs, axis=1))
             dk.append(dks * 0.125)
             dv.append(dvs)
@@ -392,23 +503,25 @@
         bsum[0, g, :, 640:768] = jnp.zeros((1, 128), f32)
         for r in row_tiles(RT):
             rs = pl.ds(r, RT)
-            acc[rs] += mm(qkv[g, rs], w[...], NT)
-        def grad(c):
-            left = mm(fT[pl.ds(c, 2 * band)], qkv[g])
-            right = mm(gmT[pl.ds(c, 2 * band)], att[g])
-            return jnp.concatenate([left[:, :512], left[:, 512:] + right], axis=1)
-        put(gA, g, 0, grad)
+            acc[rs] += mm(qkv[g, rs], wa(g), NT)
+        def part(c):
+            first = mm(left_t[pl.ds(c, 2 * band)], qkv[g])
+            second = mm(right_t[pl.ds(c, 2 * band)], att[g])
+            return jnp.concatenate([first[:, :512], first[:, 512:] + second], axis=1)
+        put(gA, g, 0, part)
+        at(g, [[(mhop, 1)], [], [(mhop, 2)], []])
         return carry
     lax.fori_loop(0, 4, backward, 0)
-    drain(gA, 0)
 
     for r in row_tiles(RL):
         rs = pl.ds(r, RL)
         n, inv = normal_of(x[rs].astype(f32))
         gn = acc[rs]
-        ig[rs] = (gm[rs] + normal_back(gn, n, inv, vecs[0:1])).astype(bf16)
+        first_in[rs] = (middle[rs] + normal_back(gn, n, inv, vecs[0:1])).astype(bf16)
         sums[0] += colsum(gn * n)
         sums[1] += colsum(gn)
+    ig_copy = pltpu.make_async_copy(first_in, ig_out, sems.at[1])
+    ig_copy.start()
     lines = sums + [bsum[i, j] for i in range(2) for j in range(4)] + [jnp.zeros((2, D), f32)]
     lines = jnp.concatenate(lines, axis=0).astype(bf16)
     for i in range(8):
@@ -417,40 +530,55 @@
         return pltpu.make_async_copy(vrow, gA.at[g, :, pl.ds(band, 16)], sems.at[2 + g])
     for g in range(4):
         vecs_out(g).start()
+    mhop(3)
+    off(gA, 3, 0).wait()
+    ig_copy.wait()
     for g in range(4):
         vecs_out(g).wait()
-
-
-def compute(x, cot, valid_col, keybias, vecs, bias, A, B, C):
-    band = BAND
-    V = pltpu.VMEM
-    vm = pl.BlockSpec(memory_space=V)
-    hb = pl.BlockSpec(memory_space=pl.ANY)
-    S = jax.ShapeDtypeStruct
+    mclose()
+    for b in range(3):
+        sent(b)
+
+
+def layer(linked, tokens, cotangent, counts, weights, cid=1):
+    V, S = pltpu.VMEM, pltpu.SemaphoreType.DMA
+    shape = jax.ShapeDtypeStruct
+    hb, vm = pl.BlockSpec(memory_space=pl.ANY), pl.BlockSpec(memory_space=V)
+    band, nb = BAND, 3
+    rows_of = (band + 16, band, band)
+    mixed_shape = (4, LEN, D) if linked else (LEN, D)
+    scratch = [V((4, 8, r, D), bf16) for r in rows_of]
+    scratch += [V((LEN, D), bf16)] * 5 + [V((D, LEN), bf16)] * 2
+    scratch += [V((4, LEN, D), bf16), V((4, 3, LEN, LEN), bf16), V((4, LEN, 256), bf16)]
+    scratch += [V((LEN, D), f32)] * 3 + [V((4, LEN, D), bf16)] * 2
+    scratch += [V((2, 8, band, D), bf16), V((2, 4, 1, D), f32), V((8, 16, D), bf16), V((16, D), f32)]
+    scratch += [V((2, 4, 1, D), f32), V((LEN, D), bf16), S((12,))]
+    if linked:
+        scratch += [V((sum(rows_of), D), bf16), V((16, 128), f32)]
+        scratch += [S((nb,)), S((nb, 2, 4)), S((nb, 4))]
+        scratch += [S((nb, 2, 4))] * 2 + [S((nb, 2))] * 2 + [S((nb, 4))] * 2
+        scratch += [S((2, 4)), S((4,)), S((1,))]
+    params = dict(collective_id=cid, has_side_effects=True) if linked else {}
     return pl.pallas_call(
-        compute_kernel,
-        out_shape=[S((LEN, D), bf16)] * 2 + [S((4, D // band, r, D), bf16) for r in (band + 16, band, band)],
-        in_specs=[vm] * 9,
-        out_specs=[vm, vm, hb, hb, hb],
-        scratch_shapes=[V((LEN, D), bf16)] * 4 + [V((D, LEN), bf16)] * 4 + [
-            V((4, LEN, D), bf16), V((4, 3, 3, LEN, RT), bf16), V((4, LEN, 256), bf16),
-            V((LEN, D), f32), V((LEN, D), f32), V((LEN, D), f32), V((LEN, D), f32),
-            V((2, D // band, band, D), bf16), V((2, 4, 1, D), f32), V((8, 16, D), bf16),
-            pltpu.SemaphoreType.DMA((6,)),
-        ],
-        compiler_params=pltpu.CompilerParams(vmem_limit_bytes=63 * 1024 * 1024),
+        functools.partial(layer_kernel, linked),
+        out_shape=[shape(mixed_shape, bf16), shape((LEN, D), bf16)]
+        + [shape((4, 8, r, D), bf16) for r in rows_of],
+        in_specs=[hb, hb, pl.BlockSpec(memory_space=pltpu.SMEM)] + ([vm] * 6 if linked else [hb] * 3),
+        out_specs=[hb] * 5,
+        scratch_shapes=scratch,
+        compiler_params=pltpu.CompilerParams(vmem_limit_bytes=63 * 1024 * 1024, **params),
         cost_estimate=pl.CostEstimate(
             flops=57_000_000_000, bytes_accessed=32_000_000, transcendentals=6_000_000
         ),
-    )(x, cot, valid_col, keybias, vecs, bias, A, B, C)
+    )(tokens, cotangent, counts, *weights)
 
 
 def scatter_kernel(rows_of, *refs):
     nb = len(rows_of)
-    grads, (mixed, ig), (mixed_all, ig_all, total) = refs[:nb], refs[nb : nb + 2], refs[nb + 2 : nb + 5]
-    refs = refs[nb + 5 :]
+    grads, (ig, ig_all, total) = refs[:nb], refs[nb : nb + 3]
+    refs = refs[nb + 3 :]
     own, got1, got2, got3, gotz = (refs[i * nb : (i + 1) * nb] for i in range(5))
-    ls, cs, cr, hs, hr, ss, sr, zs, zr, ms, mr, ml = refs[5 * nb :]
+    ls, cs, cr, hs, hr, ss, sr, zs, zr = refs[5 * nb : 5 * nb + 9]
     z, me = lax.axis_index("tensor"), lax.axis_index("dp")
     nz = 4
     cp, xp, yp = flip(me, 1), flip(me, 2), flip(me, 4)
@@ -460,37 +588,7 @@
     starts = [sum(rows_of[:b]) for b in range(nb)]
     half = [((0, 48), (48, r - 48)) for r in rows_of]
 
-    full = ((mixed, mixed_all), (ig, ig_all))
-    def along(i, s, src, step):
-        return send(src, full[i][1].at[s], ms.at[i, (step + 1) // 2, jnp.abs(s - z)], mr.at[i, s], (me, z + step))
-    def keep(i):
-        return pltpu.make_async_copy(full[i][0], full[i][1].at[z], ml.at[i])
-    def open_line(i):
-        @pl.when(z < nz - 1)
-        def _():
-            along(i, z, full[i][0], 1).start()
-        @pl.when(z > 0)
-        def _():
-            along(i, z, full[i][0], -1).start()
-        keep(i).start()
-    def hop(i, t):
-        for side, ok in ((-1, z >= t), (1, z + t < nz)):
-            @pl.when(ok)
-            def _():
-                s = z + side * t
-                arrived(full[i][1].at[s], mr.at[i, s])
-                @pl.when((z < nz - 1) if side < 0 else (z > 0))
-                def _():
-                    along(i, s, full[i][1].at[s], -side).start()
-    def close_line(i):
-        keep(i).wait()
-        for t in range(4):
-            @pl.when((z < nz - 1) & (z >= t))
-            def _():
-                along(i, z - t, full[i][1].at[z - t], 1).wait_send()
-            @pl.when((z > 0) & (z + t < nz))
-            def _():
-                along(i, z + t, full[i][1].at[z + t], -1).wait_send()
+    open_line, hop, close_line = line_steps(ig, ig_all, z, me, refs[5 * nb + 9 :])
 
     def twin(b, j):
         return send(grads[b].at[:, flip(groups[j], 1)], got1[b].at[j], cs.at[b, j], cr.at[b, j], (cp, z))
@@ -575,8 +673,7 @@
 
     for b in (2, 1, 0):
         first(b)
-    open_line(0)
-    open_line(1)
+    open_line()
     second(2)
     rest(2)
     second(1)
@@ -584,42 +681,38 @@
     third(2)
     second(0)
     rest(0)
-    hop(0, 1)
     third(1)
+    hop(1)
     fourth(2)
-    hop(1, 1)
     third(0)
     fourth(1)
-    hop(0, 2)
+    hop(2)
     last(2)
     fourth(0)
-    hop(1, 2)
     last(1)
-    hop(0, 3)
+    hop(3)
     last(0)
-    hop(1, 3)
-    for i in range(2):
-        close_line(i)
+    close_line()
     for b in range(3):
         close(b)
 
 
-def scatter(grads, mixed, ig, cid=2):
+def scatter(grads, ig, cid=2):
     rows_of = [g.shape[2] for g in grads]
     nb = len(rows_of)
     S, V = pltpu.SemaphoreType.DMA, pltpu.VMEM
     hb = pl.BlockSpec(memory_space=pl.ANY)
     scratch = [V((4, 4, r, D), bf16) for r in rows_of] + [V((4, 4, r, D), bf16) for r in rows_of]
     scratch += [V((4, r, D), bf16) for r in rows_of] + [V((2, 4, r, D), bf16) for r in rows_of] * 2
-    scratch += [S((nb, 4))] * 3 + [S((nb, 2))] * 4 + [S((nb, 4)), S((nb, 2, 4)), S((2, 2, 4)), S((2, 4)), S((2,))]
+    scratch += [S((nb, 4))] * 3 + [S((nb, 2))] * 4 + [S((nb, 4)), S((nb, 2, 4)), S((2, 4)), S((4,)), S((1,))]
     return pl.pallas_call(
         functools.partial(scatter_kernel, rows_of),
-        out_shape=[jax.ShapeDtypeStruct((4, LEN, D), bf16)] * 2 + [jax.ShapeDtypeStruct((sum(rows_of), D), f32)],
-        in_specs=[hb] * (nb + 2),
-        out_specs=[hb, hb, pl.BlockSpec(memory_space=V)],
+        out_shape=[jax.ShapeDtypeStruct((4, LEN, D), bf16)] + [jax.ShapeDtypeStruct((sum(rows_of), D), f32)],
+        in_specs=[hb] * (nb + 1),
+        out_specs=[hb, pl.BlockSpec(memory_space=V)],
         scratch_shapes=scratch,
         compiler_params=pltpu.CompilerParams(collective_id=cid, has_side_effects=True, vmem_limit_bytes=60 * 1024 * 1024),
-    )(*grads, mixed, ig)
+    )(*grads, ig)
 
 
 def step_kernel(total, *refs):
@@ -711,13 +804,23 @@
 def gather_plain(masters):
     qkv, out, up, down, shared, split = (t.astype(bf16) for t in masters)
     band, thin, width = shared.shape[1], split.shape[1], down.shape[1] * lax.axis_size("tensor")
-    groups, copies = lax.axis_size("tensor"), lax.axis_size("dp")
-    vecs = jnp.zeros((16, width), bf16).at[:6, :band].set(shared).at[:6, 128 : 128 + thin].set(split)
-    own = jnp.concatenate(
-        [pack_attention(qkv, out.T), vecs, up.reshape(band, -1), down.reshape(-1, band).T]
+    groups = lax.axis_size("tensor")
+    own = jnp.stack(
+        [pack_attention(qkv, out.T), up.reshape(band, -1), down.reshape(-1, band).T]
     )
-    whole = lax.all_gather(own, AXES).reshape(groups, copies, -1, width)
-    return jnp.split(whole, [band + 16, 2 * band + 16], axis=2)
+    mats = lax.all_gather(own, AXES, axis=1, tiled=True).reshape(3, groups, 8, BAND, width)
+    shared = lax.all_gather(shared, "dp", axis=1, tiled=True)
+    split = lax.all_gather(split, AXES, axis=1, tiled=True).reshape(-1, groups, width // groups)
+    bq, bv = split[0], split[1]
+    zero = jnp.zeros((groups, 128), bf16)
+    attn_bias = [bq[:, :128], zero, bv[:, :128], bq[:, 128:], bv[:, 128:], zero, zero]
+    lines = [
+        jnp.broadcast_to(shared, (groups, 6, width)),
+        jnp.concatenate(attn_bias, axis=1)[:, None],
+        jnp.swapaxes(split[2:], 0, 1).reshape(groups, 1, width),
+    ]
+    lines = jnp.pad(jnp.concatenate(lines, axis=1)[:, None], ((0, 0), (0, 7), (0, 8), (0, 0)))
+    return jnp.concatenate([mats[0], lines], axis=2), mats[1], mats[2]
 
 
 def step_plain(grads, mixed, grad_inputs, state):
@@ -765,45 +868,13 @@
 
 def local(tokens, cotangent, counts, *state):
     masters = state[0::3]
-    shared_master, split_master = masters[4:]
-    groups = lax.axis_size("tensor")
-    copies = lax.axis_size("dp")
-    seq_count, length, width = tokens.shape
-    share = seq_count // groups
-    mine = lax.axis_index("tensor") * share
-    band = shared_master.shape[1]
-    thin = split_master.shape[1]
-    linked = (groups, copies) == (4, 8)
-
-    if linked:
-        mats = gather(masters, (band + 16, band, band))
+    if (lax.axis_size("tensor"), lax.axis_size("dp")) == (4, 8):
+        mixed, grad_inputs, *grads = layer(True, tokens, cotangent, counts, masters)
+        grad_inputs, total = scatter(grads, grad_inputs)
+        outputs = step(total, state)
     else:
         mats = gather_plain(masters)
-    vec_all = mats[0][:, :, band:].astype(f32)
-    attn_all, up_all, down_all = (t[:, :, :band].reshape(groups, width, width) for t in mats)
-    shared_vecs = jnp.swapaxes(vec_all[0, :, :6, :band], 0, 1).reshape(6, width)
-    split_vecs = vec_all[:, :, :6, 128 : 128 + thin].reshape(groups, copies, 6, thin)
-    split_vecs = jnp.swapaxes(split_vecs, 1, 2).reshape(groups, 6, copies * thin)
-    bq, bv = split_vecs[:, 0], split_vecs[:, 1]
-    zero = jnp.zeros((groups, 128), f32)
-    attn_bias = jnp.concatenate(
-        [bq[:, :128], zero, bv[:, :128], bq[:, 128:], bv[:, 128:], zero, zero], axis=1
-    )
-    up_bias = split_vecs[:, 2:].reshape(groups, width)
-    bias = jnp.stack([attn_bias, up_bias]).reshape(2, groups, 1, width)
-
-    x = lax.dynamic_slice_in_dim(tokens, mine, share, 0).reshape(length, width)
-    cot = lax.dynamic_slice_in_dim(cotangent, mine, share, 0).reshape(length, width)
-    count = lax.dynamic_slice_in_dim(counts, mine, share, 0)
-    valid = lax.broadcasted_iota(jnp.int32, (length, 1), 0) < count
-    mixed, grad_inputs, *grads = compute(
-        x, cot, valid.astype(f32), jnp.where(valid, 0.0, MASK_FILL), shared_vecs, bias,
-        attn_all, up_all, down_all,
-    )
-    if linked:
-        mixed, grad_inputs, total = scatter(grads, mixed, grad_inputs)
-        outputs = step(total, state)
-    else:
+        mixed, grad_inputs, *grads = layer(False, tokens, cotangent, counts, mats)
         mixed, grad_inputs, outputs = step_plain(grads, mixed, grad_inputs, state)
     return (mixed, grad_inputs.astype(f32), *outputs)
 

time: 349 us -> 272 us (0.78)
  Pallas kernels: 316 us -> 253 us
  local copies, waits for them, and re-layouts: 22.5 us -> 12.5 us
  other arithmetic: 9.74 us -> 5.63 us
    pallas_call x1, Pallas kernels: 139 us -> 89.6 us  [scatter(): pl.pallas_call(functools.partial(scatter_kernel, rows_of), out_shape=[jax...]
    pallas_call x2 -> x1, Pallas kernels: 169 us -> 155 us  [layer(): pl.pallas_call(functools.partial(layer_kernel, linked), out_shape=[shape(...]
    slice x7 -> x0, local copies, waits for them, and re-layouts: 4.83 us -> none  [the longest x1 4.81 us: local(): t[:, :, :band].reshape(groups, width, width)]
    reshape x4 -> x0, local copies, waits for them, and re-layouts: 4.26 us -> none  [the longest x1 2.85 us: local(): lax.dynamic_slice_in_dim(cotangent, mine, share, 0).reshape(length, width)]
    unnamed x16 -> x14, local copies, waits for them, and re-layouts: 12.6 us -> 12.5 us
where the time goes in v4:
time: 272 us
  Pallas kernels  253 us (93%)
  local copies, waits for them, and re-layouts  12.5 us (5%)
  other arithmetic  5.63 us (2%)
    pallas_call x1, Pallas kernels, layer(): pl.pallas_call(functools.partial(layer_kernel, linked), out_shape=[shape(...  155 us
    pallas_call x1, Pallas kernels, scatter(): pl.pallas_call(functools.partial(scatter_kernel, rows_of), out_shape=[jax...  89.6 us
    unnamed x14, local copies, waits for them, and re-layouts  12.5 us
    pallas_call x1, Pallas kernels, step(): pl.pallas_call(step_kernel, out_shape=shapes, in_specs=[vm] * 19, out_spe...  8.36 us
    convert_element_type x1, other arithmetic, local(): return (mixed, grad_inputs.astype(f32), *outputs)  5.63 us

profile of v4, /device:TPU:0, one launch (start us, length us, event | category | flops | bytes accessed | tf_op | source)
XLA Modules:
  0.0 271.9 jit_solution(5817102136803632551)
XLA Ops:
  0.7 1.9 copy.47.refs_3_.refs_0_
  2.6 155.0 %shard_map.404 = (bf16[4,576,768]{2,1,0:T(8,128)(2,1)}, bf16[576,768]{1,0:T(8,128)(2,1)}, bf16[4,8,112,768]{3,2,1,0:T(8,128)(2,1)}, bf16[4,8,96,768]{3,2,1,0:T(8,128)(2,1)}, bf16[4,8,96,768]{3,2,1,0:T(8,128)(2,1)}) custom-call(bf16[4,576,768]{2,1,0:T(8,128)(2,1)} %refs_0_.2, bf16[4,576,768]{2,1,0:T(8,128)(2,1)} %refs_1_.2, s32[4]{0:T(128)} %refs_2_.2, ...), custom_call_target="tpu_custom_call" | custom-call | flops 57000001536 | bytes 32000000 | tf_op jit(solution)/shard_map/pallas_call | solution.py:562
  157.6 89.6 %shard_map.405 = (bf16[4,576,768]{2,1,0:T(8,128)(2,1)}, f32[304,768]{1,0:T(8,128)}) custom-call(bf16[4,8,112,768]{3,2,1,0:T(8,128)(2,1)} %get-tuple-element.58.refs_0_, bf16[4,8,96,768]{3,2,1,0:T(8,128)(2,1)} %get-tuple-element.59.refs_1_, bf16[4,8,96,768]{3,2,1,0:T(8,128)(2,1)} %get-tuple-element.60.refs_2_, bf16[576,768]{1,0:T(8,128)(2,1)} %get-tuple-element.61.refs_3_), custom_call_target="tpu_custom_call" | custom-call | tf_op jit(solution)/shard_map/pallas_call | solution.py:708
  247.3 0.0 copy-start.1
  247.3 0.0 copy-start.2
  247.3 5.6 %convert_element_type.3 = f32[4,576,768]{2,1,0:T(8,128)} convert(bf16[4,576,768]{2,1,0:T(8,128)(2,1)} %get-tuple-element.62) | non-fusion elementwise | flops 1769472 | bytes 10616832 | tf_op jit(solution)/shard_map/convert_element_type | solution.py:879
  252.9 0.0 copy-done.1
  252.9 0.9 copy.49.refs_1_
  253.9 0.0 copy-done.2
  253.9 0.9 copy.50.refs_2_
  254.8 0.0 copy-start
  254.8 8.4 %shard_map.406 = (f32[96,3,192]{2,1,0:T(4,128)}, bf16[96,3,192]{2,1,0:T(4,128)(2,1)}, f32[96,3,192]{2,1,0:T(4,128)}, f32[96,3,192]{2,1,0:T(4,128)}, f32[192,96]{...) custom-call(f32[304,768]{1,0:T(8,128)} %get-tuple-element.63.total, ...), custom_call_target="tpu_custom_call" | custom-call | tf_op jit(solution)/shard_map/pallas_call | solution.py:775
  263.2 1.8 copy.51
  264.9 1.6 copy.52
  266.5 1.8 copy.53
  268.3 1.8 copy.54
  270.1 0.0 copy-done
  270.1 1.8 copy.56
Async XLA Ops:
  247.3 5.7 %copy-start.1 = (f32[96,3,192]{2,0,1:T(8,128)S(1)}, f32[96,3,192]{2,0,1:T(8,128)}, u32[]{:S(2)}) copy-start(f32[96,3,192]{2,0,1:T(8,128)} %param.25) | copy-start | bytes 663556
  247.3 6.6 %copy-start.2 = (f32[96,3,192]{2,0,1:T(8,128)S(1)}, f32[96,3,192]{2,0,1:T(8,128)}, u32[]{:S(2)}) copy-start(f32[96,3,192]{2,0,1:T(8,128)} %param.26) | copy-start | bytes 663556
  254.8 15.3 %copy-start = (bf16[4,576,768]{2,1,0:T(8,128)(2,1)S(1)}, bf16[4,576,768]{2,1,0:T(8,128)(2,1)}, u32[]{:S(2)}) copy-start(bf16[4,576,768]{2,1,0:T(8,128)(2,1)} %get-tuple-element.140) | copy-start | bytes 10616836

commit v5 on v4

--- a/solution.py
+++ b/solution.py
@@ -119,7 +119,7 @@
     width = D // 4
     for f in range(4):
         own[band + 16 : 2 * band + 16, f * width : (f + 1) * width] = up[:, f].astype(bf16)
-        own[2 * band + 16 :, f * width : (f + 1) * width] = down[f].T.astype(bf16)
+        own[2 * band + 16 : 3 * band + 16, f * width : (f + 1) * width] = down[f].T.astype(bf16)
     pad[...] = jnp.zeros_like(pad)
     pad[0:6, 0:band] = shared[...]
     pad[8:14, 0:thin] = split[...]
@@ -265,6 +265,88 @@
     return opens, hop, close
 
 
+def reduce_steps(own, got_b, landing, rows_of, z, me, sems):
+    cs, cr, hs, hr, ss, sr, zs, zr, ds, dr = sems
+    nz = 4
+    xp, yp = flip(me, 2), flip(me, 4)
+    pair = (xp, yp)
+    cp = flip(me, 1)
+    half = [((0, 48), (48, r - 48)) for r in rows_of]
+    everything = slice(None)
+
+    def add(dst, *srcs):
+        dst[...] = sum((t[...].astype(f32) for t in srcs), dst[...].astype(f32)).astype(bf16)
+    def over_z(body):
+        lax.fori_loop(0, nz, lambda g, c: (body(g), c)[1], 0)
+    def twin(b, g, src, j):
+        return send(src, came(b, j, g), cs.at[b, j, g], cr.at[b, j, g], (cp, z))
+    def came(b, j, g):
+        return got_b[b - 1].at[j, g] if b else landing(0, 5 + j, g, pl.ds(0, 96))
+    def twin_vec(g, j, src):
+        return send(src, landing(0, 5 + j, g, pl.ds(96, 16)), ds.at[j, g], dr.at[j, g], (cp, z))
+    def merge(b):
+        def body(g):
+            for j in (3, 1, 2, 0):
+                arrived(came(b, j, g), cr.at[b, j, g])
+                if b:
+                    add(own[b].at[j, g], came(b, j, g))
+                else:
+                    arrived(landing(0, 5 + j, g, pl.ds(96, 16)), dr.at[j, g])
+                    add(own[0].at[j, g], landing(0, 5 + j, g, pl.ds(0, 112)))
+        over_z(body)
+        for k in range(2):
+            corner(b, k).start()
+    def corner(b, k):
+        part = pl.ds(*half[b][k])
+        return send(own[b].at[3, :, part], landing(b, 0, everything, part), hs.at[b, k], hr.at[b, k], (pair[k], z))
+    def square(b, k):
+        return send(own[b].at[1 + k], landing(b, 1 + k), ss.at[b, k], sr.at[b, k], (pair[k], z))
+    def third(b):
+        for k in range(2):
+            part = pl.ds(*half[b][k])
+            arrived(landing(b, 0, everything, part), hr.at[b, k])
+            over_z(lambda g: add(own[b].at[2 - k, g, part], landing(b, 0, g, part)))
+            square(b, 1 - k).start()
+    def fourth(b):
+        for k in range(2):
+            arrived(landing(b, 1 + k), sr.at[b, k])
+        over_z(lambda g: add(own[b].at[0, g], landing(b, 1, g), landing(b, 2, g)))
+        along(b, 0)
+    def line(b, t, way):
+        side = (1 - way) // 2
+        return send(own[b].at[0, t], landing(b, 3 + side, t), zs.at[b, t], zr.at[b, side, t], (me, z + way))
+    def along(b, i):
+        for way, begin in ((1, i), (-1, nz - 1 - i)):
+            side = (1 - way) // 2
+            targets = range(nz - 1, begin, -1) if way > 0 else range(begin)
+            @pl.when(z == begin)
+            def _():
+                for t in targets:
+                    if i:
+                        arrived(landing(b, 3 + side, t), zr.at[b, side, t])
+                        add(own[b].at[0, t], landing(b, 3 + side, t))
+                    line(b, t, way).start()
+    def last(b, total, at):
+        total[pl.ds(at, rows_of[b])] = own[b][0, z].astype(f32)
+        for side, ok in ((0, z > 0), (1, z < nz - 1)):
+            @pl.when(ok)
+            def _():
+                arrived(landing(b, 3 + side, z), zr.at[b, side, z])
+                total[pl.ds(at, rows_of[b])] += landing(b, 3 + side, z)[...].astype(f32)
+    def closed(b):
+        for k in range(2):
+            corner(b, k).wait_send()
+            square(b, k).wait_send()
+        for t in range(nz):
+            @pl.when(z < t)
+            def _():
+                line(b, t, 1).wait_send()
+            @pl.when(z > t)
+            def _():
+                line(b, t, -1).wait_send()
+    return twin, twin_vec, merge, third, fourth, along, last, closed
+
+
 QT = ((0, 256), (256, 256), (512, 64))
 
 
@@ -272,21 +354,55 @@
     tokens, cotangent, counts = refs[:3]
     weights_in = refs[3 : 9 if linked else 6]
     refs = refs[9 if linked else 6 :]
-    mixed_all, ig_out, gA, gB, gC = refs[:5]
-    (WA, WB, WC, x, gout_low, first_in, second_in, gm_low, left_t, right_t, qkv, probs, att,
-     middle, acc, acc2, hidden, slope, stage, bsum, vrow, vecs, bias, mixed, sems) = refs[5:30]
+    n_out = 3 if linked else 5
+    outs, refs = refs[:n_out], refs[n_out:]
+    (WA, WB, WC, x, gout_low, first_in, second_in, left_t, right_t, qkv, probs, att,
+     middle, acc, hs, stage, bsum, vrow, vecs, bias, mixed, sems) = refs[:22]
+    refs = refs[22:]
+    gm_low, ig = second_in, first_in
+    hidden, slope = hs.at[pl.ds(0, 4)], hs.at[pl.ds(4, 4)]
     z, me = lax.axis_index("tensor"), lax.axis_index("dp")
     band = BAND
     if linked:
-        own, pad = refs[30:32]
+        mixed_all, ig_all, total_out = outs
+        own, pad = stage, refs[0]
+        rows_of = (band + 16, band, band)
         opens, hop, lined, square, corner, ready, sent = gather_steps(
-            own, (WA, WB, WC), (band + 16, band, band), z, me, refs[32:41]
+            own, (WA, WB, WC), rows_of, z, me, refs[1:10]
         )
-        mopen, mhop, mclose = line_steps(mixed, mixed_all, z, me, refs[41:44])
+        mopen, mhop, mclose = line_steps(mixed, mixed_all, z, me, refs[10:13])
+        iopen, ihop, iclose = line_steps(ig, ig_all, z, me, refs[13:16])
+        parts, got_b, freed = refs[16:19], refs[19:21], refs[21]
+        def landing(b, i, g=slice(None), part=None):
+            if b:
+                part = pl.ds(0, band) if part is None else part
+                return (WB, WC)[b - 1].at[g, i, part]
+            base, spot = (0, 4) if i == 0 else (4, i - 1) if i < 5 else (0, i - 5)
+            lo, n = (0, band + 16) if part is None else (part.start, part.size)
+            g = pl.ds(base, 4) if isinstance(g, slice) else base + g
+            return hs.at[g, pl.ds((band + 16) * spot + lo, n)]
+        twin, twin_vec, merge, third, fourth, along, last, closed = reduce_steps(
+            parts, got_b, landing, rows_of, z, me, refs[22:32]
+        )
+        def staged(slot, j):
+            return stage.at[pl.ds((4 * slot + j) * band, band)]
+        def release():
+            for d in (flip(me, 1), flip(me, 2), flip(me, 4)):
+                pl.semaphore_signal(freed, inc=1, device_id=(d, z), device_id_type=MESH)
+            @pl.when(z > 0)
+            def _():
+                pl.semaphore_signal(freed, inc=1, device_id=(me, z - 1), device_id_type=MESH)
+            @pl.when(z < 3)
+            def _():
+                pl.semaphore_signal(freed, inc=1, device_id=(me, z + 1), device_id_type=MESH)
+        def acquire():
+            pl.semaphore_wait(freed, 3 + jnp.where(z > 0, 1, 0) + jnp.where(z < 3, 1, 0))
     else:
         def nothing(*args):
             return None
         opens = hop = lined = square = corner = sent = mhop = nothing
+        release = acquire = merge = third = fourth = along = nothing
+        mixed_all, ig_out, gA, gB, gC = outs
         def ready(b):
             pltpu.make_async_copy(weights_in[b], (WA, WB, WC)[b], sems.at[8 + b]).wait()
         def mopen():
@@ -311,6 +427,15 @@
     def valid(r):
         return jnp.where(lax.broadcasted_iota(jnp.int32, (RL, 1), 0) + r < count, 1.0, 0.0)
 
+    def transpose(dst, src):
+        turned = src[...].T
+        for d in range(8):
+            spot = d
+            if linked:
+                apart = [lax.rem(lax.div(me, 1 << i) + (d >> i), 2) for i in range(3)]
+                spot = 4 * apart[0] + apart[1] + 2 * apart[2]
+            dst[pl.ds(pl.multiple_of(spot * band, 32), band)] = turned[d * band : (d + 1) * band]
+
     opens(0)
     for load in loads:
         load.wait()
@@ -321,16 +446,20 @@
     hop(0, 1)
     hop(0, 2)
     opens(1)
-    right_t[...] = gout_low[...].T
+    transpose(right_t, gout_low)
     hop(0, 3)
     lined(0)
+    hop(1, 1)
+    opens(2)
     square(0)
-    hop(1, 1)
     hop(1, 2)
-    opens(2)
+    hop(2, 1)
     hop(1, 3)
     lined(1)
+    hop(2, 2)
     corner(0)
+    hop(2, 3)
+    lined(2)
     ready(0)
     lines = [sum(WA[g, i, band : band + 16].astype(f32) for i in range(8)) for g in range(4)]
     vecs[...] = lines[0]
@@ -383,7 +512,7 @@
         for r in row_tiles(RT):
             rs = pl.ds(r, RT)
             acc[rs] += mm(att[g, rs], wa(g, 512, D), NT)
-        at(g, [[(hop, 2, 1), (hop, 2, 2)], [(hop, 2, 3), (lined, 2), (square, 1)], [(corner, 1)], []])
+        at(g, [[(square, 1)], [], [(corner, 1)], [(square, 2)]])
         return carry
     lax.fori_loop(0, 4, forward, 0)
 
@@ -392,9 +521,8 @@
         m = x[rs].astype(f32) + acc[rs] + vecs[2:3]
         middle[rs] = m
         second_in[rs] = (normal_of(m)[0] * vecs[3:4] + vecs[4:5]).astype(bf16)
-    left_t[...] = second_in[...].T
+    transpose(left_t, second_in)
     acc[...] = jnp.zeros_like(acc)
-    acc2[...] = jnp.zeros_like(acc2)
     ready(1)
 
     def mlp_up(g, carry):
@@ -404,7 +532,6 @@
             phi = 0.5 * (1.0 + lax.erf(u * SQRT_HALF))
             hidden[g, rs] = (u * phi).astype(bf16)
             slope[g, rs] = (phi + u * jnp.exp(-0.5 * u * u) * INV_ROOT_TAU).astype(bf16)
-        at(g, [[], [(square, 2)], [], []])
         return carry
     lax.fori_loop(0, 4, mlp_up, 0)
     corner(2)
@@ -420,6 +547,7 @@
         rs = pl.ds(r, RL)
         mixed[rs] = ((middle[rs] + acc[rs] + vecs[5:6]) * valid(r)).astype(bf16)
     mopen()
+    acc[...] = jnp.zeros_like(acc)
 
     def off(dst, g, slot):
         return pltpu.make_async_copy(stage.at[slot], dst.at[g, :, pl.ds(0, band)], sems.at[slot])
@@ -430,26 +558,52 @@
         for c in range(0, D, 2 * band):
             stage[slot, pl.ds(c // band, 2)] = part(c).astype(bf16).reshape(2, band, D)
         off(dst, g, slot).start()
+    def share_out(b, g, slot, part):
+        def sending(gg):
+            return [twin(b, gg, staged(slot, j), j) for j in range(4)]
+        kept = part(0, 4 * band).astype(bf16)
+        for j in range(4):
+            parts[b][j, g, pl.ds(0, band)] = kept[j * band : (j + 1) * band]
+        @pl.when(g > 0)
+        def _():
+            for copy in sending(g - 1):
+                copy.wait_send()
+        stage[pl.ds(4 * slot * band, 4 * band)] = part(4 * band, 4 * band).astype(bf16)
+        for copy in sending(g):
+            copy.start()
+        @pl.when(g == 3)
+        def _():
+            for copy in sending(g):
+                copy.wait_send()
+    def give(b, g, slot, part):
+        if linked:
+            share_out(b, g, slot, part)
+        else:
+            put((gA, gB, gC)[b], g, slot, lambda c: part(c, 2 * band))
 
     def mlp_back(g, carry):
         for r in row_tiles(RT):
             rs = pl.ds(r, RT)
             gp = (mm(gout_low[rs], wc(g)) * slope[g, rs].astype(f32)).astype(bf16)
             slope[g, rs] = gp
-            acc2[rs] += mm(gp, wb(g), NT)
+            acc[rs] += mm(gp, wb(g), NT)
         bsum[1, g] = colsum(slope[g].astype(f32))
-        put(gC, g, 0, lambda c: mm(right_t[pl.ds(c, 2 * band)], hidden[g]))
-        put(gB, g, 1, lambda c: mm(left_t[pl.ds(c, 2 * band)], slope[g]))
+        give(2, g, 0, lambda c, n: mm(right_t[pl.ds(c, n)], hidden[g]))
+        give(1, g, 1, lambda c, n: mm(left_t[pl.ds(c, n)], slope[g]))
         return carry
+    for b in range(3):
+        sent(b)
     lax.fori_loop(0, 4, mlp_back, 0)
-    off(gC, 3, 0).wait()
-    off(gB, 3, 1).wait()
+    release()
+    if not linked:
+        off(gC, 3, 0).wait()
+        off(gB, 3, 1).wait()
 
     sums = [jnp.zeros((1, D), f32) for _ in range(6)]
     for r in row_tiles(RL):
         rs = pl.ds(r, RL)
         n, inv = normal_of(middle[rs])
-        gn = acc2[rs]
+        gn = acc[rs]
         go = gout_low[rs].astype(f32)
         t = go + normal_back(gn, n, inv, vecs[3:4])
         middle[rs] = t
@@ -458,8 +612,11 @@
         sums[3] += colsum(gn * n)
         sums[4] += colsum(gn)
         sums[5] += colsum(go)
-    left_t[...] = first_in[...].T
-    right_t[...] = gm_low[...].T
+    merged = [(acquire,), (merge, 2), (merge, 1), (mhop, 1)]
+    for act, *args in merged:
+        act(*args)
+    transpose(left_t, first_in)
+    transpose(right_t, gm_low)
     acc[...] = jnp.zeros_like(acc)
 
     def backward(g, carry):
@@ -504,12 +661,7 @@
         for r in row_tiles(RT):
             rs = pl.ds(r, RT)
             acc[rs] += mm(qkv[g, rs], wa(g), NT)
-        def part(c):
-            first = mm(left_t[pl.ds(c, 2 * band)], qkv[g])
-            second = mm(right_t[pl.ds(c, 2 * band)], att[g])
-            return jnp.concatenate([first[:, :512], first[:, 512:] + second], axis=1)
-        put(gA, g, 0, part)
-        at(g, [[(mhop, 1)], [], [(mhop, 2)], []])
+        at(g, [[(third, 2)], [(mhop, 2), (third, 1)], [], []])
         return carry
     lax.fori_loop(0, 4, backward, 0)
 
@@ -520,24 +672,64 @@
         first_in[rs] = (middle[rs] + normal_back(gn, n, inv, vecs[0:1])).astype(bf16)
         sums[0] += colsum(gn * n)
         sums[1] += colsum(gn)
-    ig_copy = pltpu.make_async_copy(first_in, ig_out, sems.at[1])
-    ig_copy.start()
     lines = sums + [bsum[i, j] for i in range(2) for j in range(4)] + [jnp.zeros((2, D), f32)]
     lines = jnp.concatenate(lines, axis=0).astype(bf16)
-    for i in range(8):
-        vrow[i] = lines
-    def vecs_out(g):
-        return pltpu.make_async_copy(vrow, gA.at[g, :, pl.ds(band, 16)], sems.at[2 + g])
-    for g in range(4):
-        vecs_out(g).start()
-    mhop(3)
-    off(gA, 3, 0).wait()
-    ig_copy.wait()
-    for g in range(4):
-        vecs_out(g).wait()
+    fourth(2)
+    if linked:
+        iopen()
+
+    def attention_grads(g, carry):
+        def part(c, n):
+            first = mm(left_t[pl.ds(c, n)], qkv[g])
+            second = mm(right_t[pl.ds(c, n)], att[g])
+            return jnp.concatenate([first[:, :512], first[:, 512:] + second], axis=1)
+        give(0, g, 0, part)
+        at(g, [[(mhop, 3)], [], [(along, 2, 1)], []])
+        return carry
+    lax.fori_loop(0, 4, attention_grads, 0)
+    if linked:
+        vrow[0] = lines
+        def vec_step(g, act):
+            for j in range(4):
+                act(twin_vec(g, j, vrow.at[0]))
+        for g in range(4):
+            vec_step(g, lambda copy: copy.start())
+            for j in range(4):
+                parts[0][j, g, pl.ds(band, 16)] = lines
+        fourth(1)
+        merge(0)
+        third(0)
+        ihop(1)
+        along(2, 2)
+        along(1, 1)
+        fourth(0)
+        ihop(2)
+        along(1, 2)
+        last(2, acc, 2 * band + 16)
+        along(0, 1)
+        last(1, acc, band + 16)
+        along(0, 2)
+        last(0, acc, 0)
+        done = pltpu.make_async_copy(acc.at[pl.ds(0, 3 * band + 16)], total_out, sems.at[1])
+        done.start()
+        ihop(3)
+        for g in range(4):
+            vec_step(g, lambda copy: copy.wait_send())
+        done.wait()
+        iclose()
+        for b in range(3):
+            closed(b)
+    else:
+        for i in range(8):
+            vrow[i] = lines
+        copies = [pltpu.make_async_copy(ig, ig_out, sems.at[1])]
+        copies += [pltpu.make_async_copy(vrow, gA.at[g, :, pl.ds(band, 16)], sems.at[2 + g]) for g in range(4)]
+        for copy in copies:
+            copy.start()
+        for copy in copies:
+            copy.wait()
+        off(gA, 3, 0).wait()
     mclose()
-    for b in range(3):
-        sent(b)
 
 
 def layer(linked, tokens, cotangent, counts, weights, cid=1):
@@ -546,173 +738,34 @@
     hb, vm = pl.BlockSpec(memory_space=pl.ANY), pl.BlockSpec(memory_space=V)
     band, nb = BAND, 3
     rows_of = (band + 16, band, band)
-    mixed_shape = (4, LEN, D) if linked else (LEN, D)
     scratch = [V((4, 8, r, D), bf16) for r in rows_of]
-    scratch += [V((LEN, D), bf16)] * 5 + [V((D, LEN), bf16)] * 2
+    scratch += [V((LEN, D), bf16)] * 4 + [V((D, LEN), bf16)] * 2
     scratch += [V((4, LEN, D), bf16), V((4, 3, LEN, LEN), bf16), V((4, LEN, 256), bf16)]
-    scratch += [V((LEN, D), f32)] * 3 + [V((4, LEN, D), bf16)] * 2
-    scratch += [V((2, 8, band, D), bf16), V((2, 4, 1, D), f32), V((8, 16, D), bf16), V((16, D), f32)]
+    scratch += [V((LEN, D), f32)] * 2 + [V((8, LEN, D), bf16), V((8 * band, D) if linked else (2, 8, band, D), bf16)]
+    scratch += [V((2, 4, 1, D), f32), V((1 if linked else 8, 16, D), bf16), V((16, D), f32)]
     scratch += [V((2, 4, 1, D), f32), V((LEN, D), bf16), S((12,))]
+    outs = [shape((LEN, D), bf16)] * 2 + [shape((4, 8, r, D), bf16) for r in rows_of]
     if linked:
-        scratch += [V((sum(rows_of), D), bf16), V((16, 128), f32)]
+        outs = [shape((4, LEN, D), bf16)] * 2 + [shape((sum(rows_of), D), f32)]
+        scratch += [V((16, 128), f32)]
         scratch += [S((nb,)), S((nb, 2, 4)), S((nb, 4))]
         scratch += [S((nb, 2, 4))] * 2 + [S((nb, 2))] * 2 + [S((nb, 4))] * 2
-        scratch += [S((2, 4)), S((4,)), S((1,))]
+        scratch += [S((2, 4)), S((4,)), S((1,))] * 2
+        scratch += [V((4, 4, r, D), bf16) for r in rows_of] + [V((4, 4, band, D), bf16)] * 2
+        scratch += [pltpu.SemaphoreType.REGULAR] + [S((nb, 4, 4))] * 2 + [S((nb, 2))] * 4
+        scratch += [S((nb, 4)), S((nb, 2, 4))] + [S((4, 4))] * 2
     params = dict(collective_id=cid, has_side_effects=True) if linked else {}
     return pl.pallas_call(
         functools.partial(layer_kernel, linked),
-        out_shape=[shape(mixed_shape, bf16), shape((LEN, D), bf16)]
-        + [shape((4, 8, r, D), bf16) for r in rows_of],
+        out_shape=outs,
         in_specs=[hb, hb, pl.BlockSpec(memory_space=pltpu.SMEM)] + ([vm] * 6 if linked else [hb] * 3),
-        out_specs=[hb] * 5,
+        out_specs=[hb] * len(outs),
         scratch_shapes=scratch,
         compiler_params=pltpu.CompilerParams(vmem_limit_bytes=63 * 1024 * 1024, **params),
         cost_estimate=pl.CostEstimate(
             flops=57_000_000_000, bytes_accessed=32_000_000, transcendentals=6_000_000
         ),
     )(tokens, cotangent, counts, *weights)
-
-
-def scatter_kernel(rows_of, *refs):
-    nb = len(rows_of)
-    grads, (ig, ig_all, total) = refs[:nb], refs[nb : nb + 3]
-    refs = refs[nb + 3 :]
-    own, got1, got2, got3, gotz = (refs[i * nb : (i + 1) * nb] for i in range(5))
-    ls, cs, cr, hs, hr, ss, sr, zs, zr = refs[5 * nb : 5 * nb + 9]
-    z, me = lax.axis_index("tensor"), lax.axis_index("dp")
-    nz = 4
-    cp, xp, yp = flip(me, 1), flip(me, 2), flip(me, 4)
-    groups = (me, xp, yp, flip(xp, 4))
-    pair = (xp, yp)
-    greet(z, nz, me, (cp, xp, yp), lambda: None)
-    starts = [sum(rows_of[:b]) for b in range(nb)]
-    half = [((0, 48), (48, r - 48)) for r in rows_of]
-
-    open_line, hop, close_line = line_steps(ig, ig_all, z, me, refs[5 * nb + 9 :])
-
-    def twin(b, j):
-        return send(grads[b].at[:, flip(groups[j], 1)], got1[b].at[j], cs.at[b, j], cr.at[b, j], (cp, z))
-    def load(b, j):
-        return pltpu.make_async_copy(grads[b].at[:, groups[j]], own[b].at[j], ls.at[b, j])
-    def corner(b, k):
-        lo, n = half[b][k]
-        return send(own[b].at[3, :, pl.ds(lo, n)], got2[b].at[:, pl.ds(lo, n)], hs.at[b, k], hr.at[b, k], (pair[k], z))
-    def square(b, k):
-        return send(own[b].at[1 + k], got3[b].at[k], ss.at[b, k], sr.at[b, k], (pair[k], z))
-    def line(b, t, step):
-        return send(own[b].at[0, t], gotz[b].at[(1 - step) // 2, t], zs.at[b, t], zr.at[b, (1 - step) // 2, t], (me, z + step))
-
-    def add(dst, *srcs):
-        dst[...] = sum((s[...].astype(f32) for s in srcs), dst[...].astype(f32)).astype(bf16)
-    def over_z(body):
-        lax.fori_loop(0, 4, lambda s, c: (body(s), c)[1], 0)
-
-    def first(b):
-        for j in (3, 1, 2, 0):
-            twin(b, j).start()
-            load(b, j).start()
-    def merge(b, j):
-        load(b, j).wait()
-        arrived(got1[b].at[j], cr.at[b, j])
-        over_z(lambda s: add(own[b].at[j, s], got1[b].at[j, s]))
-    def second(b):
-        merge(b, 3)
-        for k in range(2):
-            corner(b, k).start()
-    def third(b):
-        for k in range(2):
-            lo, n = half[b][k]
-            part = pl.ds(lo, n)
-            arrived(got2[b].at[:, part], hr.at[b, k])
-            over_z(lambda s: add(own[b].at[2 - k, s, part], got2[b].at[s, part]))
-        for k in range(2):
-            square(b, k).start()
-    def fourth(b):
-        for k in range(2):
-            arrived(got3[b].at[k], sr.at[b, k])
-        over_z(lambda s: add(own[b].at[0, s], got3[b].at[0, s], got3[b].at[1, s]))
-        for t in (3, 2, 1):
-            @pl.when(z + t < nz)
-            def _():
-                @pl.when(z > 0)
-                def _():
-                    arrived(gotz[b].at[0, z + t], zr.at[b, 0, z + t])
-                    add(own[b].at[0, z + t], gotz[b].at[0, z + t])
-                line(b, z + t, 1).start()
-            @pl.when(z >= t)
-            def _():
-                @pl.when(z < nz - 1)
-                def _():
-                    arrived(gotz[b].at[1, z - t], zr.at[b, 1, z - t])
-                    add(own[b].at[0, z - t], gotz[b].at[1, z - t])
-                line(b, z - t, -1).start()
-    def last(b):
-        span = pl.ds(starts[b], rows_of[b])
-        total[span] = own[b][0, z].astype(f32)
-        for i, ok in ((0, z > 0), (1, z < nz - 1)):
-            @pl.when(ok)
-            def _():
-                arrived(gotz[b].at[i, z], zr.at[b, i, z])
-                total[span] += gotz[b][i, z].astype(f32)
-    def close(b):
-        for j in range(4):
-            twin(b, j).wait_send()
-        for k in range(2):
-            corner(b, k).wait_send()
-            square(b, k).wait_send()
-        for t in (3, 2, 1):
-            @pl.when(z + t < nz)
-            def _():
-                line(b, z + t, 1).wait_send()
-            @pl.when(z >= t)
-            def _():
-                line(b, z - t, -1).wait_send()
-    def rest(b):
-        for j in (1, 2, 0):
-            merge(b, j)
-
-    for b in (2, 1, 0):
-        first(b)
-    open_line()
-    second(2)
-    rest(2)
-    second(1)
-    rest(1)
-    third(2)
-    second(0)
-    rest(0)
-    third(1)
-    hop(1)
-    fourth(2)
-    third(0)
-    fourth(1)
-    hop(2)
-    last(2)
-    fourth(0)
-    last(1)
-    hop(3)
-    last(0)
-    close_line()
-    for b in range(3):
-        close(b)
-
-
-def scatter(grads, ig, cid=2):
-    rows_of = [g.shape[2] for g in grads]
-    nb = len(rows_of)
-    S, V = pltpu.SemaphoreType.DMA, pltpu.VMEM
-    hb = pl.BlockSpec(memory_space=pl.ANY)
-    scratch = [V((4, 4, r, D), bf16) for r in rows_of] + [V((4, 4, r, D), bf16) for r in rows_of]
-    scratch += [V((4, r, D), bf16) for r in rows_of] + [V((2, 4, r, D), bf16) for r in rows_of] * 2
-    scratch += [S((nb, 4))] * 3 + [S((nb, 2))] * 4 + [S((nb, 4)), S((nb, 2, 4)), S((2, 4)), S((4,)), S((1,))]
-    return pl.pallas_call(
-        functools.partial(scatter_kernel, rows_of),
-        out_shape=[jax.ShapeDtypeStruct((4, LEN, D), bf16)] + [jax.ShapeDtypeStruct((sum(rows_of), D), f32)],
-        in_specs=[hb] * (nb + 1),
-        out_specs=[hb, pl.BlockSpec(memory_space=V)],
-        scratch_shapes=scratch,
-        compiler_params=pltpu.CompilerParams(collective_id=cid, has_side_effects=True, vmem_limit_bytes=60 * 1024 * 1024),
-    )(*grads, ig)
 
 
 def step_kernel(total, *refs):
@@ -869,8 +922,7 @@
 def local(tokens, cotangent, counts, *state):
     masters = state[0::3]
     if (lax.axis_size("tensor"), lax.axis_size("dp")) == (4, 8):
-        mixed, grad_inputs, *grads = layer(True, tokens, cotangent, counts, masters)
-        grad_inputs, total = scatter(grads, grad_inputs)
+        mixed, grad_inputs, total = layer(True, tokens, cotangent, counts, masters)
         outputs = step(total, state)
     else:
         mats = gather_plain(masters)

time: 272 us -> 256 us (0.941)
  Pallas kernels: 253 us -> 237 us
    pallas_call x2 -> x1, Pallas kernels: 245 us -> 229 us  [layer(): pl.pallas_call(functools.partial(layer_kernel, linked), out_shape=outs, i...]
where the time goes in v5:
time: 256 us
  Pallas kernels  237 us (93%)
  local copies, waits for them, and re-layouts  12.5 us (5%)
  other arithmetic  5.63 us (2%)
    pallas_call x1, Pallas kernels, layer(): pl.pallas_call(functools.partial(layer_kernel, linked), out_shape=outs, i...  229 us
    unnamed x14, local copies, waits for them, and re-layouts  12.5 us
    pallas_call x1, Pallas kernels, step(): pl.pallas_call(step_kernel, out_shape=shapes, in_specs=[vm] * 19, out_spe...  8.36 us
    convert_element_type x1, other arithmetic, local(): return (mixed, grad_inputs.astype(f32), *outputs)  5.63 us

profile of v5, /device:TPU:0, one launch (start us, length us, event | category | flops | bytes accessed | tf_op | source)
XLA Modules:
  0.0 256.0 jit_solution(2489791887120930904)
XLA Ops:
  0.7 1.9 copy.47.refs_3_.refs_0_
  2.6 228.8 %shard_map.404 = (bf16[4,576,768]{2,1,0:T(8,128)(2,1)}, bf16[4,576,768]{2,1,0:T(8,128)(2,1)}, f32[304,768]{1,0:T(8,128)}) custom-call(bf16[4,576,768]{2,1,0:T(8,128)(2,1)} %refs_0_.2, bf16[4,576,768]{2,1,0:T(8,128)(2,1)} %refs_1_.2, s32[4]{0:T(128)} %refs_2_.2, f32[96,3,192]{2,1,0:T(4,128)} %copy.47.refs_3_.refs_0_, f32[192,96]{1,0:T(8,128)} %refs_3_.2, ...), custom_call_target="tpu_custom_call" | custom-call | flops 57000001536 | bytes 32000000 | tf_op jit(solution)/shard_map/pallas_call | solution.py:758
  231.3 0.0 copy-start.1
  231.4 0.0 copy-start.2
  231.4 5.6 %convert_element_type.3 = f32[4,576,768]{2,1,0:T(8,128)} convert(bf16[4,576,768]{2,1,0:T(8,128)(2,1)} %get-tuple-element.54) | non-fusion elementwise | flops 1769472 | bytes 10616832 | tf_op jit(solution)/shard_map/convert_element_type | solution.py:931
  237.0 0.0 copy-done.1
  237.0 0.9 copy.49.refs_1_
  237.9 0.0 copy-done.2
  237.9 0.9 copy.50.refs_2_
  238.9 0.0 copy-start
  238.9 8.4 %shard_map.405 = (f32[96,3,192]{2,1,0:T(4,128)}, bf16[96,3,192]{2,1,0:T(4,128)(2,1)}, f32[96,3,192]{2,1,0:T(4,128)}, f32[96,3,192]{2,1,0:T(4,128)}, f32[192,96]{...) custom-call(f32[304,768]{1,0:T(8,128)} %get-tuple-element.55.total, ...), custom_call_target="tpu_custom_call" | custom-call | tf_op jit(solution)/shard_map/pallas_call | solution.py:828
  247.3 1.8 copy.51
  249.0 1.6 copy.52
  250.6 1.8 copy.53
  252.4 1.8 copy.54
  254.2 0.0 copy-done
  254.2 1.8 copy.56
Async XLA Ops:
  231.3 5.7 %copy-start.1 = (f32[96,3,192]{2,0,1:T(8,128)S(1)}, f32[96,3,192]{2,0,1:T(8,128)}, u32[]{:S(2)}) copy-start(f32[96,3,192]{2,0,1:T(8,128)} %param.25) | copy-start | bytes 663556
  231.4 6.6 %copy-start.2 = (f32[96,3,192]{2,0,1:T(8,128)S(1)}, f32[96,3,192]{2,0,1:T(8,128)}, u32[]{:S(2)}) copy-start(f32[96,3,192]{2,0,1:T(8,128)} %param.26) | copy-start | bytes 663556
  238.9 15.3 %copy-start = (bf16[4,576,768]{2,1,0:T(8,128)(2,1)S(1)}, bf16[4,576,768]{2,1,0:T(8,128)(2,1)}, u32[]{:S(2)}) copy-start(bf16[4,576,768]{2,1,0:T(8,128)(2,1)} %get-tuple-element.132) | copy-start | bytes 10616836

commit v6 on v5

--- a/solution.py
+++ b/solution.py
@@ -103,10 +103,10 @@
 def colsum(v):
     return jnp.sum(v, axis=0, keepdims=True)
 
-def pack(own, pad, qkv, out, up, down, shared, split):
+def pack(own, pad, qkv, out, shared, split):
     band, thin = shared.shape[1], split.shape[1]
     me = lax.axis_index("dp")
-    low = [qkv[:, i].astype(bf16) for i in range(3)]
+    low = [qkv[i].astype(bf16) for i in range(3)]
     ot = out[...].T.astype(bf16)
     pieces = [
         low[0][:, :128], low[1][:, :128], low[2][:, :128],
@@ -117,9 +117,6 @@
     for i, piece in enumerate(pieces):
         own[0:band, 128 * i : 128 * i + 128] = piece
     width = D // 4
-    for f in range(4):
-        own[band + 16 : 2 * band + 16, f * width : (f + 1) * width] = up[:, f].astype(bf16)
-        own[2 * band + 16 : 3 * band + 16, f * width : (f + 1) * width] = down[f].T.astype(bf16)
     pad[...] = jnp.zeros_like(pad)
     pad[0:6, 0:band] = shared[...]
     pad[8:14, 0:thin] = split[...]
@@ -136,6 +133,14 @@
     ups = sum(placed(f * width + at)[10 + f : 11 + f] for f in range(4))
     rows = [placed(me * band + src)[0:6], attn, ups, jnp.zeros((8, D), f32)]
     own[band : band + 16] = jnp.concatenate(rows, axis=0).astype(bf16)
+
+
+def pack_rest(own, up, down):
+    band = up.shape[0]
+    width = D // 4
+    for f in range(4):
+        own[band + 16 : 2 * band + 16, f * width : (f + 1) * width] = up[:, f].astype(bf16)
+        own[2 * band + 16 : 3 * band + 16, f * width : (f + 1) * width] = down[f].T.astype(bf16)
 
 
 def gather_steps(own, outs, masters_rows, z, me, sems):
@@ -228,40 +233,40 @@
     return opens, hop, lined, square, corner, ready, sent
 
 
-def line_steps(block, whole, z, me, sems):
+def line_steps(block, whole, z, me, sems, rows=pl.ds(0, LEN)):
     nz = 4
     ms, mr, ml = sems
 
     def along(s, src, way):
-        return send(src, whole.at[s], ms.at[(way + 1) // 2, jnp.abs(s - z)], mr.at[s], (me, z + way))
+        return send(src, whole.at[s, rows], ms.at[(way + 1) // 2, jnp.abs(s - z)], mr.at[s], (me, z + way))
     def keep():
-        return pltpu.make_async_copy(block, whole.at[z], ml.at[0])
+        return pltpu.make_async_copy(block.at[rows], whole.at[z, rows], ml.at[0])
     def opens():
         @pl.when(z < nz - 1)
         def _():
-            along(z, block, 1).start()
+            along(z, block.at[rows], 1).start()
         @pl.when(z > 0)
         def _():
-            along(z, block, -1).start()
+            along(z, block.at[rows], -1).start()
         keep().start()
     def hop(t):
         for way, ok in ((-1, z >= t), (1, z + t < nz)):
             @pl.when(ok)
             def _():
                 s = z + way * t
-                arrived(whole.at[s], mr.at[s])
+                arrived(whole.at[s, rows], mr.at[s])
                 @pl.when((z < nz - 1) if way < 0 else (z > 0))
                 def _():
-                    along(s, whole.at[s], -way).start()
+                    along(s, whole.at[s, rows], -way).start()
     def close():
         keep().wait()
         for t in range(4):
             @pl.when((z < nz - 1) & (z >= t))
             def _():
-                along(z - t, whole.at[z - t], 1).wait_send()
+                along(z - t, whole.at[z - t, rows], 1).wait_send()
             @pl.when((z > 0) & (z + t < nz))
             def _():
-                along(z + t, whole.at[z + t], -1).wait_send()
+                along(z + t, whole.at[z + t, rows], -1).wait_send()
     return opens, hop, close
 
 
@@ -370,9 +375,25 @@
         opens, hop, lined, square, corner, ready, sent = gather_steps(
             own, (WA, WB, WC), rows_of, z, me, refs[1:10]
         )
-        mopen, mhop, mclose = line_steps(mixed, mixed_all, z, me, refs[10:13])
-        iopen, ihop, iclose = line_steps(ig, ig_all, z, me, refs[13:16])
-        parts, got_b, freed = refs[16:19], refs[19:21], refs[21]
+        tail_sems = refs[len(refs) - 18 :]
+        pieces = [
+            line_steps(block, whole, z, me, tail_sems[3 * (3 * i + c) : 3 * (3 * i + c) + 3], pl.ds(192 * c, 192))
+            for i, (block, whole) in enumerate(((mixed, mixed_all), (ig, ig_all)))
+            for c in range(3)
+        ]
+        def mopen():
+            for c in range(3):
+                pieces[c][0]()
+        def mhop(t, c):
+            pieces[c][1](t)
+        def mclose():
+            for c in range(3):
+                pieces[c][2]()
+        def iopen(c):
+            pieces[3 + c][0]()
+        def ihop(t, c):
+            pieces[3 + c][1](t)
+        parts, got_b, freed = refs[10:13], refs[13:15], refs[15]
         def landing(b, i, g=slice(None), part=None):
             if b:
                 part = pl.ds(0, band) if part is None else part
@@ -382,7 +403,7 @@
             g = pl.ds(base, 4) if isinstance(g, slice) else base + g
             return hs.at[g, pl.ds((band + 16) * spot + lo, n)]
         twin, twin_vec, merge, third, fourth, along, last, closed = reduce_steps(
-            parts, got_b, landing, rows_of, z, me, refs[22:32]
+            parts, got_b, landing, rows_of, z, me, refs[16:26]
         )
         def staged(slot, j):
             return stage.at[pl.ds((4 * slot + j) * band, band)]
@@ -417,7 +438,7 @@
     for load in loads:
         load.start()
     if linked:
-        greet(z, 4, me, (flip(me, 1), flip(me, 2), flip(me, 4)), lambda: pack(own, pad, *weights_in))
+        greet(z, 4, me, (flip(me, 1), flip(me, 2), flip(me, 4)), lambda: pack(own, pad, *weights_in[:2], *weights_in[4:]))
     else:
         for b in range(3):
             pltpu.make_async_copy(weights_in[b], (WA, WB, WC)[b], sems.at[8 + b]).start()
@@ -437,6 +458,8 @@
             dst[pl.ds(pl.multiple_of(spot * band, 32), band)] = turned[d * band : (d + 1) * band]
 
     opens(0)
+    if linked:
+        pack_rest(own, *weights_in[2:4])
     for load in loads:
         load.wait()
     for r in row_tiles(RL):
@@ -590,6 +613,7 @@
         bsum[1, g] = colsum(slope[g].astype(f32))
         give(2, g, 0, lambda c, n: mm(right_t[pl.ds(c, n)], hidden[g]))
         give(1, g, 1, lambda c, n: mm(left_t[pl.ds(c, n)], slope[g]))
+        at(g, [[], [], [(mhop, 1, 0)], [(mhop, 1, 1)]])
         return carry
     for b in range(3):
         sent(b)
@@ -612,7 +636,7 @@
         sums[3] += colsum(gn * n)
         sums[4] += colsum(gn)
         sums[5] += colsum(go)
-    merged = [(acquire,), (merge, 2), (merge, 1), (mhop, 1)]
+    merged = [(mhop, 1, 2), (acquire,), (merge, 2), (merge, 1), (mhop, 2, 0)]
     for act, *args in merged:
         act(*args)
     transpose(left_t, first_in)
@@ -661,8 +685,14 @@
         for r in row_tiles(RT):
             rs = pl.ds(r, RT)
             acc[rs] += mm(qkv[g, rs], wa(g), NT)
-        at(g, [[(third, 2)], [(mhop, 2), (third, 1)], [], []])
+        at(g, BACK)
         return carry
+    BACK = [
+        [(third, 2), (mhop, 2, 1)],
+        [(mhop, 2, 2), (third, 1)],
+        [],
+        [],
+    ]
     lax.fori_loop(0, 4, backward, 0)
 
     for r in row_tiles(RL):
@@ -676,7 +706,8 @@
     lines = jnp.concatenate(lines, axis=0).astype(bf16)
     fourth(2)
     if linked:
-        iopen()
+        for c in range(3):
+            iopen(c)
 
     def attention_grads(g, carry):
         def part(c, n):
@@ -684,7 +715,7 @@
             second = mm(right_t[pl.ds(c, n)], att[g])
             return jnp.concatenate([first[:, :512], first[:, 512:] + second], axis=1)
         give(0, g, 0, part)
-        at(g, [[(mhop, 3)], [], [(along, 2, 1)], []])
+        at(g, [[], [], [(along, 2, 1)], []])
         return carry
     lax.fori_loop(0, 4, attention_grads, 0)
     if linked:
@@ -698,25 +729,31 @@
                 parts[0][j, g, pl.ds(band, 16)] = lines
         fourth(1)
         merge(0)
+        ihop(1, 0)
         third(0)
-        ihop(1)
+        ihop(1, 1)
+        along(1, 1)
+        ihop(1, 2)
         along(2, 2)
-        along(1, 1)
+        ihop(2, 0)
         fourth(0)
-        ihop(2)
+        ihop(2, 1)
         along(1, 2)
+        along(0, 1)
+        ihop(2, 2)
         last(2, acc, 2 * band + 16)
-        along(0, 1)
+        along(0, 2)
         last(1, acc, band + 16)
-        along(0, 2)
         last(0, acc, 0)
         done = pltpu.make_async_copy(acc.at[pl.ds(0, 3 * band + 16)], total_out, sems.at[1])
         done.start()
-        ihop(3)
+        for c in range(3):
+            ihop(3, c)
         for g in range(4):
             vec_step(g, lambda copy: copy.wait_send())
         done.wait()
-        iclose()
+        for c in range(3):
+            pieces[3 + c][2]()
         for b in range(3):
             closed(b)
     else:
@@ -729,6 +766,8 @@
         for copy in copies:
             copy.wait()
         off(gA, 3, 0).wait()
+    for c in range(3):
+        mhop(3, c)
     mclose()
 
 
@@ -750,10 +789,10 @@
         scratch += [V((16, 128), f32)]
         scratch += [S((nb,)), S((nb, 2, 4)), S((nb, 4))]
         scratch += [S((nb, 2, 4))] * 2 + [S((nb, 2))] * 2 + [S((nb, 4))] * 2
-        scratch += [S((2, 4)), S((4,)), S((1,))] * 2
         scratch += [V((4, 4, r, D), bf16) for r in rows_of] + [V((4, 4, band, D), bf16)] * 2
         scratch += [pltpu.SemaphoreType.REGULAR] + [S((nb, 4, 4))] * 2 + [S((nb, 2))] * 4
         scratch += [S((nb, 4)), S((nb, 2, 4))] + [S((4, 4))] * 2
+        scratch += [S((2, 4)), S((4,)), S((1,))] * 6
     params = dict(collective_id=cid, has_side_effects=True) if linked else {}
     return pl.pallas_call(
         functools.partial(layer_kernel, linked),
@@ -768,8 +807,17 @@
     )(tokens, cotangent, counts, *weights)
 
 
-def step_kernel(total, *refs):
-    ins, outs = refs[:18], refs[18:]
+def step_kernel(total, low, *refs):
+    ins, outs, full, (held, wide, got, put) = refs[:18], refs[18:42], refs[42], refs[43:]
+    fetch = [pltpu.make_async_copy(low.at[s], held.at[s], got.at[s]) for s in range(4)]
+    store = [pltpu.make_async_copy(wide.at[s], full.at[s], put.at[s]) for s in range(4)]
+    for copy in fetch:
+        copy.start()
+    for s in range(4):
+        fetch[s].wait()
+        for r in row_tiles(RL):
+            wide[s, pl.ds(r, RL)] = held[s, pl.ds(r, RL)].astype(f32)
+        store[s].start()
     z, me = lax.axis_index("tensor"), lax.axis_index("dp")
     band, thin = ins[12].shape[1], ins[15].shape[1]
     vec = total[band : band + 16]
@@ -804,9 +852,9 @@
     attn = total[:band]
     def pair(a, b):
         return jnp.concatenate([attn[:, a : a + 128], attn[:, b : b + 64]], axis=1)
-    apply(0, (slice(None), 0), pair(0, 384))
-    apply(0, (slice(None), 1), pair(128, 512))
-    apply(0, (slice(None), 2), pair(256, 448))
+    apply(0, (0,), pair(0, 384))
+    apply(0, (1,), pair(128, 512))
+    apply(0, (2,), pair(256, 448))
     apply(1, (slice(None),), pair(640, 576).T)
     up = total[band + 16 : 2 * band + 16]
     down = total[2 * band + 16 :]
@@ -817,21 +865,26 @@
         apply(3, (f,), down[f * width : (f + 1) * width])
     apply(4, (slice(None),), shared)
     apply(5, (slice(None),), split)
-
-
-def step(total, state):
-    vm = pl.BlockSpec(memory_space=pltpu.VMEM)
+    for copy in store:
+        copy.wait()
+
+
+def step(total, low, state):
+    V, S = pltpu.VMEM, pltpu.SemaphoreType.DMA
+    vm, hb = pl.BlockSpec(memory_space=V), pl.BlockSpec(memory_space=pl.ANY)
     shapes = []
     for kind in range(6):
         shape = state[3 * kind].shape
         shapes += [jax.ShapeDtypeStruct(shape, t) for t in (f32, bf16, f32, f32)]
+    shapes.append(jax.ShapeDtypeStruct(low.shape, f32))
     return pl.pallas_call(
         step_kernel,
         out_shape=shapes,
-        in_specs=[vm] * 19,
-        out_specs=[vm] * 24,
+        in_specs=[vm, hb] + [vm] * 18,
+        out_specs=[vm] * 24 + [hb],
+        scratch_shapes=[V(low.shape, bf16), V(low.shape, f32), S((4,)), S((4,))],
         compiler_params=pltpu.CompilerParams(vmem_limit_bytes=56 * 1024 * 1024),
-    )(total, *state)
+    )(total, low, *state)
 
 
 def pack_attention(qkv, out):
@@ -922,13 +975,16 @@
 def local(tokens, cotangent, counts, *state):
     masters = state[0::3]
     if (lax.axis_size("tensor"), lax.axis_size("dp")) == (4, 8):
-        mixed, grad_inputs, total = layer(True, tokens, cotangent, counts, masters)
-        outputs = step(total, state)
+        turned = tuple(jnp.swapaxes(t, 0, 1) for t in state[:3])
+        mixed, low, total = layer(True, tokens, cotangent, counts, turned[:1] + masters[1:])
+        *outputs, grad_inputs = step(total, low, turned + state[3:])
+        outputs[:4] = [jnp.swapaxes(t, 0, 1) for t in outputs[:4]]
     else:
         mats = gather_plain(masters)
         mixed, grad_inputs, *grads = layer(False, tokens, cotangent, counts, mats)
         mixed, grad_inputs, outputs = step_plain(grads, mixed, grad_inputs, state)
-    return (mixed, grad_inputs.astype(f32), *outputs)
+        grad_inputs = grad_inputs.astype(f32)
+    return (mixed, grad_inputs, *outputs)
 
 
 def solution(mesh):

time: 256 us -> 231 us (0.902)
  local copies, waits for them, and re-layouts: 12.5 us -> 1.8 us
  Pallas kernels: 237 us -> 229 us
  other arithmetic: 5.63 us -> 0 us
    pallas_call x1, Pallas kernels: 229 us -> 217 us  [layer(): pl.pallas_call(functools.partial(layer_kernel, linked), out_shape=outs, i...]
    unnamed x14 -> x3, local copies, waits for them, and re-layouts: 12.5 us -> 1.8 us
    convert_element_type x1 -> x0, other arithmetic: 5.63 us -> none  [local(): return (mixed, grad_inputs.astype(f32), *outputs)]
    pallas_call x1, Pallas kernels: 8.36 us -> 11.5 us  [step(): pl.pallas_call(step_kernel, out_shape=shapes, in_specs=[vm, hb] + [vm] *...]
where the time goes in v6:
time: 231 us
  Pallas kernels  229 us (99%)
    pallas_call x1, Pallas kernels, layer(): pl.pallas_call(functools.partial(layer_kernel, linked), out_shape=outs, i...  217 us
    pallas_call x1, Pallas kernels, step(): pl.pallas_call(step_kernel, out_shape=shapes, in_specs=[vm, hb] + [vm] *...  11.5 us

profile of v6, /device:TPU:0, one launch (start us, length us, event | category | flops | bytes accessed | tf_op | source)
XLA Modules:
  0.0 231.0 jit_solution(9339299983028235649)
XLA Ops:
  0.7 217.1 %shard_map.404 = (bf16[4,576,768]{2,1,0:T(8,128)(2,1)}, bf16[4,576,768]{2,1,0:T(8,128)(2,1)}, f32[304,768]{1,0:T(8,128)}) custom-call(bf16[4,576,768]{2,1,0:T(8,128)(2,1)} %refs_0_.1, bf16[4,576,768]{2,1,0:T(8,128)(2,1)} %refs_1_.1, s32[4]{0:T(128)} %refs_2_.1, f32[3,96,192]{2,1,0:T(8,128)} %bitcast.7, f32[192,96]{1,0:T(8,128)} %refs_3_.1, ...), custom_call_target="tpu_custom_call" | custom-call | flops 57000001536 | bytes 32000000 | tf_op jit(solution)/shard_map/pallas_call | solution.py:797
  217.7 0.0 copy-start
  217.7 11.5 %shard_map.405 = (f32[3,96,192]{2,1,0:T(8,128)}, bf16[3,96,192]{2,1,0:T(8,128)(2,1)}, f32[3,96,192]{2,1,0:T(8,128)}, f32[3,96,192]{2,1,0:T(8,128)}, f32[192,96]{...) custom-call(f32[304,768]{1,0:T(8,128)} %get-tuple-element.55.total, ...), custom_call_target="tpu_custom_call" | custom-call | tf_op jit(solution)/shard_map/pallas_call | solution.py:880
  229.2 0.0 copy-done
  229.2 1.8 copy.48
Async XLA Ops:
  217.7 11.5 %copy-start = (bf16[4,576,768]{2,1,0:T(8,128)(2,1)S(1)}, bf16[4,576,768]{2,1,0:T(8,128)(2,1)}, u32[]{:S(2)}) copy-start(bf16[4,576,768]{2,1,0:T(8,128)(2,1)} %get-tuple-element.108) | copy-start | bytes 10616836

commit v7 on v6

--- a/solution.py
+++ b/solution.py
@@ -362,8 +362,8 @@
     n_out = 3 if linked else 5
     outs, refs = refs[:n_out], refs[n_out:]
     (WA, WB, WC, x, gout_low, first_in, second_in, left_t, right_t, qkv, probs, att,
-     middle, acc, hs, stage, bsum, vrow, vecs, bias, mixed, sems) = refs[:22]
-    refs = refs[22:]
+     middle, acc, hs, stage, bsum, vrow, vecs, bias, mixed, invs, sems) = refs[:23]
+    refs = refs[23:]
     gm_low, ig = second_in, first_in
     hidden, slope = hs.at[pl.ds(0, 4)], hs.at[pl.ds(4, 4)]
     z, me = lax.axis_index("tensor"), lax.axis_index("dp")
@@ -516,20 +516,24 @@
             qkv[g, rs] = (mm(first_in[rs], wa(g)) + bias[0, g]).astype(bf16)
         def tile(i):
             return qkv[g, :, 128 * i : 128 * i + 128]
-        outs = []
+        outs, scales = [], []
         for h in range(3):
             q, k, v = (tile(0), tile(1), tile(2)) if h < 2 else (tile(3), tile(4), tile(3))
             q = jnp.where(low if h != 1 else ~low, q, 0) * bf16(0.125)
             vt = v.T
             vt = vt[64:] if h else vt[:64]
-            cols = []
+            cols, tops = [], []
             for r, n in QT:
                 s = mm(k, q[r : r + n], NT) + keybias
                 e = jnp.exp(s - jnp.max(s, axis=0, keepdims=True))
-                p = (e * (1.0 / jnp.sum(e, axis=0, keepdims=True))).astype(bf16)
-                probs[g, h, :, pl.ds(r, n)] = p
-                cols.append(mm(vt, p))
+                inv = 1.0 / jnp.sum(e, axis=0, keepdims=True)
+                low_e = e.astype(bf16)
+                probs[g, h, :, pl.ds(r, n)] = low_e
+                cols.append(mm(vt, low_e) * inv)
+                tops.append(inv)
             outs.append(jnp.concatenate(cols, axis=1))
+            scales.append(jnp.concatenate(tops, axis=1))
+        invs[g] = jnp.concatenate(scales + [jnp.zeros((5, LEN), f32)], axis=0)
         att[g, :, 128:256] = jnp.concatenate(outs[:2], axis=0).T.astype(bf16)
         att[g, :, 0:128] = jnp.concatenate([jnp.zeros_like(outs[2]), outs[2]], axis=0).T.astype(bf16)
         for r in row_tiles(RT):
@@ -648,9 +652,11 @@
         def tile(i):
             return qkv[g, :, 128 * i : 128 * i + 128]
         dq, dk, dv = [], [], []
+        scale = invs[g].T
         for h in range(3):
             q, k, v = (tile(0), tile(1), tile(2)) if h < 2 else (tile(3), tile(4), tile(3))
             gt = ga[:, 128:256] if h < 2 else ga[:, 0:128]
+            gt = (gt.astype(f32) * scale[:, h : h + 1]).astype(bf16)
             gmask = jnp.where(low if h == 0 else ~low, gt, 0)
             kt = k.T
             kt = kt[64:] if h == 1 else kt[:64]
@@ -660,7 +666,7 @@
                 dp = mm(v, gmask[r : r + n], NT)
                 pf = p.astype(f32)
                 inner = jnp.sum(pf * dp, axis=0, keepdims=True)
-                ds = (pf * (dp - inner)).astype(bf16)
+                ds = (pf * (dp - inner * invs[g, h : h + 1, pl.ds(r, n)])).astype(bf16)
                 dqs.append(mm(kt, ds))
                 dks = dks + mm(ds, q[r : r + n])
                 dvs = dvs + mm(p, gt[r : r + n])
@@ -782,7 +788,7 @@
     scratch += [V((4, LEN, D), bf16), V((4, 3, LEN, LEN), bf16), V((4, LEN, 256), bf16)]
     scratch += [V((LEN, D), f32)] * 2 + [V((8, LEN, D), bf16), V((8 * band, D) if linked else (2, 8, band, D), bf16)]
     scratch += [V((2, 4, 1, D), f32), V((1 if linked else 8, 16, D), bf16), V((16, D), f32)]
-    scratch += [V((2, 4, 1, D), f32), V((LEN, D), bf16), S((12,))]
+    scratch += [V((2, 4, 1, D), f32), V((LEN, D), bf16), V((4, 8, LEN), f32), S((12,))]
     outs = [shape((LEN, D), bf16)] * 2 + [shape((4, 8, r, D), bf16) for r in rows_of]
     if linked:
         outs = [shape((4, LEN, D), bf16)] * 2 + [shape((sum(rows_of), D), f32)]
@@ -807,17 +813,21 @@
     )(tokens, cotangent, counts, *weights)
 
 
-def step_kernel(total, low, *refs):
-    ins, outs, full, (held, wide, got, put) = refs[:18], refs[18:42], refs[42], refs[43:]
+def step_kernel(total, low, first, *refs):
+    ins, outs, full, same, (held, wide, passed, got, put) = refs[:18], refs[18:42], refs[42], refs[43], refs[44:]
+    entry = pltpu.make_async_copy(first, passed, got.at[4])
+    leave = pltpu.make_async_copy(passed, same, put.at[4])
     fetch = [pltpu.make_async_copy(low.at[s], held.at[s], got.at[s]) for s in range(4)]
     store = [pltpu.make_async_copy(wide.at[s], full.at[s], put.at[s]) for s in range(4)]
-    for copy in fetch:
+    for copy in fetch + [entry]:
         copy.start()
     for s in range(4):
         fetch[s].wait()
         for r in row_tiles(RL):
             wide[s, pl.ds(r, RL)] = held[s, pl.ds(r, RL)].astype(f32)
         store[s].start()
+    entry.wait()
+    leave.start()
     z, me = lax.axis_index("tensor"), lax.axis_index("dp")
     band, thin = ins[12].shape[1], ins[15].shape[1]
     vec = total[band : band + 16]
@@ -865,26 +875,26 @@
         apply(3, (f,), down[f * width : (f + 1) * width])
     apply(4, (slice(None),), shared)
     apply(5, (slice(None),), split)
-    for copy in store:
+    for copy in store + [leave]:
         copy.wait()
 
 
-def step(total, low, state):
+def step(total, low, first, state):
     V, S = pltpu.VMEM, pltpu.SemaphoreType.DMA
     vm, hb = pl.BlockSpec(memory_space=V), pl.BlockSpec(memory_space=pl.ANY)
     shapes = []
     for kind in range(6):
         shape = state[3 * kind].shape
         shapes += [jax.ShapeDtypeStruct(shape, t) for t in (f32, bf16, f32, f32)]
-    shapes.append(jax.ShapeDtypeStruct(low.shape, f32))
+    shapes += [jax.ShapeDtypeStruct(low.shape, t) for t in (f32, bf16)]
     return pl.pallas_call(
         step_kernel,
         out_shape=shapes,
-        in_specs=[vm, hb] + [vm] * 18,
-        out_specs=[vm] * 24 + [hb],
-        scratch_shapes=[V(low.shape, bf16), V(low.shape, f32), S((4,)), S((4,))],
+        in_specs=[vm, hb, hb] + [vm] * 18,
+        out_specs=[vm] * 24 + [hb] * 2,
+        scratch_shapes=[V(low.shape, bf16), V(low.shape, f32), V(low.shape, bf16), S((5,)), S((5,))],
         compiler_params=pltpu.CompilerParams(vmem_limit_bytes=56 * 1024 * 1024),
-    )(total, low, *state)
+    )(total, low, first, *state)
 
 
 def pack_attention(qkv, out):
@@ -977,7 +987,7 @@
     if (lax.axis_size("tensor"), lax.axis_size("dp")) == (4, 8):
         turned = tuple(jnp.swapaxes(t, 0, 1) for t in state[:3])
         mixed, low, total = layer(True, tokens, cotangent, counts, turned[:1] + masters[1:])
-        *outputs, grad_inputs = step(total, low, turned + state[3:])
+        *outputs, grad_inputs, mixed = step(total, low, mixed, turned + state[3:])
         outputs[:4] = [jnp.swapaxes(t, 0, 1) for t in outputs[:4]]
     else:
         mats = gather_plain(masters)

time: 231 us -> 226 us (0.978)
  Pallas kernels: 229 us -> 223 us
    pallas_call x1, Pallas kernels: 217 us -> 210 us  [layer(): pl.pallas_call(functools.partial(layer_kernel, linked), out_shape=outs, i...]
where the time goes in v7:
time: 226 us; the launch traced here: 224 us
  Pallas kernels  223 us (99%)
    pallas_call x1, Pallas kernels, layer(): pl.pallas_call(functools.partial(layer_kernel, linked), out_shape=outs, i...  210 us
    pallas_call x1, Pallas kernels, step(): pl.pallas_call(step_kernel, out_shape=shapes, in_specs=[vm, hb, hb] + [vm...  13.1 us

profile of v7, /device:TPU:0, one launch (start us, length us, event | category | flops | bytes accessed | tf_op | source)
XLA Modules:
  0.0 223.7 jit_solution(2003196594418642797)
XLA Ops:
  0.7 209.7 %shard_map.404 = (bf16[4,576,768]{2,1,0:T(8,128)(2,1)}, bf16[4,576,768]{2,1,0:T(8,128)(2,1)}, f32[304,768]{1,0:T(8,128)}) custom-call(bf16[4,576,768]{2,1,0:T(8,128)(2,1)} %refs_0_.1, bf16[4,576,768]{2,1,0:T(8,128)(2,1)} %refs_1_.1, s32[4]{0:T(128)} %refs_2_.1, f32[3,96,192]{2,1,0:T(8,128)} %bitcast.7, f32[192,96]{1,0:T(8,128)} %refs_3_.1, ...), custom_call_target="tpu_custom_call" | custom-call | flops 57000001536 | bytes 32000000 | tf_op jit(solution)/shard_map/pallas_call | solution.py:803
  210.4 13.1 %shard_map.405 = (f32[3,96,192]{2,1,0:T(8,128)}, bf16[3,96,192]{2,1,0:T(8,128)(2,1)}, f32[3,96,192]{2,1,0:T(8,128)}, f32[3,96,192]{2,1,0:T(8,128)}, f32[192,96]{...) custom-call(f32[304,768]{1,0:T(8,128)} %get-tuple-element.55.total, ...), custom_call_target="tpu_custom_call" | custom-call | tf_op jit(solution)/shard_map/pallas_call | solution.py:890

commit v8 on v7

--- a/solution.py
+++ b/solution.py
@@ -733,22 +733,22 @@
             vec_step(g, lambda copy: copy.start())
             for j in range(4):
                 parts[0][j, g, pl.ds(band, 16)] = lines
+        merge(0)
         fourth(1)
-        merge(0)
-        ihop(1, 0)
+        ihop(1,0)
         third(0)
-        ihop(1, 1)
-        along(1, 1)
-        ihop(1, 2)
-        along(2, 2)
-        ihop(2, 0)
+        ihop(1,1)
+        along(1,1)
+        ihop(1,2)
+        along(2,2)
+        ihop(2,0)
         fourth(0)
-        ihop(2, 1)
-        along(1, 2)
-        along(0, 1)
-        ihop(2, 2)
+        along(0,1)
+        ihop(2,1)
+        along(1,2)
+        along(0,2)
+        ihop(2,2)
         last(2, acc, 2 * band + 16)
-        along(0, 2)
         last(1, acc, band + 16)
         last(0, acc, 0)
         done = pltpu.make_async_copy(acc.at[pl.ds(0, 3 * band + 16)], total_out, sems.at[1])
@@ -831,25 +831,27 @@
     z, me = lax.axis_index("tensor"), lax.axis_index("dp")
     band, thin = ins[12].shape[1], ins[15].shape[1]
     vec = total[band : band + 16]
-    row = lax.broadcasted_iota(jnp.int32, (D, 128), 0)
-    col = lax.broadcasted_iota(jnp.int32, (D, 128), 1)
-
-    def pick(source):
-        chosen = jnp.where(row == source, 1.0, 0.0)
-        return lax.dot_general(
-            vec, chosen, NN, precision=lax.Precision.HIGHEST, preferred_element_type=f32
-        )
-
-    place = me * thin + col
-    shared = pick(me * band + col)[:6, :band]
+    high = vec.astype(bf16)
+    rest = vec - high.astype(f32)
+    mid = rest.astype(bf16)
+    parts = jnp.concatenate([high, mid, (rest - mid.astype(f32)).astype(bf16)], axis=0)
+    row = lax.broadcasted_iota(jnp.int32, (D, 256), 0)
+    col = lax.broadcasted_iota(jnp.int32, (D, 256), 1)
+    kind = lax.div(col - band, thin)
+    place = me * thin + lax.rem(col - band, thin)
     head = jnp.where(place < 128, place, place + 256)
     late = jnp.where(place < 128, place + 256, place + 320)
-    spots = [head, late] + [f * (D // 4) + place for f in range(4)]
-    at = lax.broadcasted_iota(jnp.int32, (16, 128), 0)
+    spot = jnp.where(kind == 0, head, jnp.where(kind == 1, late, (kind - 2) * (D // 4) + place))
+    spot = jnp.where(col < band, me * band + col, spot)
+    found = mm(parts, jnp.where(row == spot, 1.0, 0.0).astype(bf16))
+    found = found[0:16] + found[16:32] + found[32:48]
+    shared = found[:6, :band]
+    at = lax.broadcasted_iota(jnp.int32, (16, 256), 0)
     lines = []
-    for i, spot in enumerate(spots):
-        mine = jnp.where(at == z + (6 if i < 2 else 10), pick(spot), 0.0)
-        lines.append(jnp.sum(mine, axis=0, keepdims=True)[:, :thin])
+    for i in range(6):
+        mine = jnp.where(at == z + (6 if i < 2 else 10), found, 0.0)
+        mine = jnp.sum(mine, axis=0, keepdims=True)
+        lines.append(mine[:, band + i * thin : band + (i + 1) * thin])
     split = jnp.concatenate(lines, axis=0)
 
     def apply(kind, where, gradient):

time: 226 us -> 224 us (level)
  no operation moved by 1% of the time
where the time goes in v8:
time: 224 us; the launch traced here: 223 us
  Pallas kernels  223 us (100%)
    pallas_call x1, Pallas kernels, layer(): pl.pallas_call(functools.partial(layer_kernel, linked), out_shape=outs, i...  210 us
    pallas_call x1, Pallas kernels, step(): pl.pallas_call(step_kernel, out_shape=shapes, in_specs=[vm, hb, hb] + [vm...  12.1 us

profile of v8, /device:TPU:0, one launch (start us, length us, event | category | flops | bytes accessed | tf_op | source)
XLA Modules:
  0.0 223.5 jit_solution(17059405055048448823)
XLA Ops:
  0.7 210.5 %shard_map.404 = (bf16[4,576,768]{2,1,0:T(8,128)(2,1)}, bf16[4,576,768]{2,1,0:T(8,128)(2,1)}, f32[304,768]{1,0:T(8,128)}) custom-call(bf16[4,576,768]{2,1,0:T(8,128)(2,1)} %refs_0_.1, bf16[4,576,768]{2,1,0:T(8,128)(2,1)} %refs_1_.1, s32[4]{0:T(128)} %refs_2_.1, f32[3,96,192]{2,1,0:T(8,128)} %bitcast.7, f32[192,96]{1,0:T(8,128)} %refs_3_.1, ...), custom_call_target="tpu_custom_call" | custom-call | flops 57000001536 | bytes 32000000 | tf_op jit(solution)/shard_map/pallas_call | solution.py:803
  211.1 12.1 %shard_map.405 = (f32[3,96,192]{2,1,0:T(8,128)}, bf16[3,96,192]{2,1,0:T(8,128)(2,1)}, f32[3,96,192]{2,1,0:T(8,128)}, f32[3,96,192]{2,1,0:T(8,128)}, f32[192,96]{...) custom-call(f32[304,768]{1,0:T(8,128)} %get-tuple-element.55.total, ...), custom_call_target="tpu_custom_call" | custom-call | tf_op jit(solution)/shard_map/pallas_call | solution.py:892
